TPU v7x, 256 devices: a whole 4x4x8 slice. The times are simulated.
256 devices in a mesh: pw: 32 (over z_lo, y, core), band: 8 (over x, z_hi).
Axes of the slice: x: 4, y: 4, z: 8 (z_hi: 2, z_lo: 4; z = z_hi * 4 + z_lo), core: 2. Of those that a mesh axis runs over, the one named last changes fastest.
Arguments:
- waves: bfloat16 [2, 40960, 7168], P(None, 'pw', 'band'), may hold values from -6 to 6
- projectors: bfloat16 [2, 128, 40960], P(None, 'band', 'pw'), may hold values from -0.01953125 to 0.01953125
- coupling: float32 [12, 13, 13], replicated, may hold values from -32.19938 to 32.19938
- offsets: int32 [12], replicated, may hold values from 0 to 119, as said below
- counts: int32 [12], replicated, may hold values from 9 to 13, as said below
Outputs:
- applied: bfloat16 [2, 40960, 7168], P(None, 'pw', 'band')
Inputs may be any that keep to these rules, and one draw needn't show every extreme that they name: `counts`: each atom has 9 or 13 projectors, exactly 5 atoms have 13, so the atoms fill all 128 projectors. offsets are the running sums of counts before each atom, so atoms take consecutive projectors in order.
All inputs are finite; a program needn't handle non-finite values.
Results may differ from a plain program's by a relative error of at most 0.0049.
Values may be sent and summed in bfloat16 or wider, within the bound.
No kernel may reach another device: no remote copies, remote signals or barrier semaphores. Data moves between devices by JAX's collectives and lax.ppermute only.
A program may use at most 64 MiB of HBM per device.

v0:
```python
import jax
import jax.numpy as jnp
from jax import lax
from jax.sharding import PartitionSpec as P

NP = 128
M = 13


def coupling_block(coupling, offsets, counts):
    proj = jnp.arange(NP, dtype=jnp.int32)
    local = jnp.arange(M, dtype=jnp.int32)
    target = offsets[:, None] + local[None, :]
    select = (proj[None, :, None] == target[:, None, :]) & (
        local[None, None, :] < counts[:, None, None]
    )
    select = select.astype(jnp.float32)
    sym = (coupling + jnp.swapaxes(coupling, 1, 2)) * 0.5
    return jnp.einsum("api,aij,aqj->pq", select, sym, select, precision=lax.Precision.HIGHEST)


def project(rows, waves):
    real = jnp.dot(rows[0], waves[0], preferred_element_type=jnp.float32) + jnp.dot(
        rows[1], waves[1], preferred_element_type=jnp.float32
    )
    imag = jnp.dot(rows[0], waves[1], preferred_element_type=jnp.float32) - jnp.dot(
        rows[1], waves[0], preferred_element_type=jnp.float32
    )
    return jnp.stack([real, imag])


def spread_back(rows, coupled):
    dims = (((0,), (0,)), ((), ()))
    real = lax.dot_general(
        rows[0], coupled[0], dims, preferred_element_type=jnp.float32
    ) - lax.dot_general(rows[1], coupled[1], dims, preferred_element_type=jnp.float32)
    imag = lax.dot_general(
        rows[0], coupled[1], dims, preferred_element_type=jnp.float32
    ) + lax.dot_general(rows[1], coupled[0], dims, preferred_element_type=jnp.float32)
    return jnp.stack([real, imag])


def shards(waves, projectors, coupling, offsets, counts):
    block = coupling_block(coupling, offsets, counts)
    gathered = lax.all_gather(projectors, "band", axis=1, tiled=True)
    partial_coeffs = project(gathered, waves)
    coeffs = lax.psum(partial_coeffs, "pw")
    coupled = jnp.einsum("pq,kqb->kpb", block, coeffs, precision=lax.Precision.HIGHEST).astype(
        jnp.bfloat16
    )
    result = spread_back(gathered, coupled)
    return result.astype(jnp.bfloat16)


def solution(mesh):
    placed = (P(None, "pw", "band"), P(None, "band", "pw"), P(), P(), P())
    return jax.shard_map(
        shards, mesh=mesh, in_specs=placed, out_specs=P(None, "pw", "band"), check_vma=False
    )
```

profile of v0, /device:TPU:1, one launch (start us, length us, event | category | flops | bytes accessed | tf_op | source)
XLA Modules:
  0.0 364.0 jit_solution(13705950301523723169)
XLA Ops:
  6.5 0.0 all-reduce.2.cloned.1.call-start
  6.5 0.0 copy-start.3
  6.5 54.6 %all_gather.3 = bf16[2,128,1280]{2,1,0:T(8,128)(2,1)S(1)} all-gather(bf16[2,16,1280]{2,1,0:T(8,128)(2,1)} %param.6), channel_id=1, replica_groups=mesh['pw'=32,'band'=8] {'band'}, dimensions={1}, use_global_device_ids=true | all-gather | bytes 737280 | tf_op jit(solution)/shard_map/all_gather | solution.py:45
  61.2 2.2 fusion.2
  63.3 2.2 fusion.4
  65.5 0.0 copy-done.3
  65.5 0.0 copy-start
  65.5 0.0 copy-start.1
  65.5 0.0 copy-start.2
  65.6 0.5 fusion.24
  66.1 0.5 fusion.18
  66.6 1.0 pad_maximum_fusion.1
  67.6 0.0 all-reduce.2.cloned.1.call-update
  67.6 0.0 copy-done
  67.6 0.2 copy.6
  67.8 0.0 copy-done.1
  67.8 0.1 iota_compare_fusion.1
  67.9 0.0 copy-done.2
  67.9 0.1 iota_add_fusion
  67.9 0.8 fusion.30
  68.7 0.8 fusion.28
  69.5 272.1 %all-reduce.2.cloned.1.call-done = f32[2,128,896]{2,1,0:T(8,128)} async-done(((f32[2,128,896]{2,1,0:T(8,128)}), f32[2,128,896]{2,1,0:T(8,128)}) %all-reduce.2.cloned.1.call-update) | async-done | bytes 917520 | tf_op jit(solution)/shard_map/psum | solution.py:47
  341.6 2.8 fusion.14
  344.4 0.7 fusion.36
  345.1 0.7 fusion.37
  345.9 0.8 fusion.1
  346.6 0.8 fusion
  347.4 2.5 pad_maximum_fusion
  349.8 7.3 %copy.8 = bf16[2,1280,896]{2,1,0:T(8,128)(2,1)} copy(bf16[2,1280,896]{1,2,0:T(8,128)(2,1)} %pad_maximum_fusion) | data formatting | bytes 9175040 | tf_op jit(solution)/shard_map/stack | solution.py:40
Async XLA Ops:
  6.5 335.0 %all-reduce.2.cloned.1.call-start = ((), (), s32[]{:S(2)}) async-start(), calls=%async_computation | async-start | bytes 1835008 | tf_op jit(solution)/shard_map/psum | solution.py:47
  6.5 59.0 %copy-start.3 = (bf16[2,1280,896]{2,1,0:T(8,128)(2,1)S(1)}, bf16[2,1280,896]{2,1,0:T(8,128)(2,1)}, u32[]{:S(2)}) copy-start(bf16[2,1280,896]{2,1,0:T(8,128)(2,1)} %param.5) | copy-start | bytes 13762564
  65.5 2.1 copy-start
  65.5 2.2 copy-start.1
  65.5 2.3 copy-start.2
Sparse Core Ops, SparseCore 0:
  67.7 273.8 all-reduce.1
where the time goes:
time: 365 us; the launch traced here: 364 us
  waiting for transfers between devices  272 us (75%)
  blocking collectives  54.6 us (15%)
  between operations  13.5 us (4%)
  matrix products  12.7 us (3%)
  local copies, waits for them, and re-layouts  7.46 us (2%)
    psum x1, waiting for transfers between devices, shards(): coeffs = lax.psum(partial_coeffs, 'pw')  272 us
    all_gather x1, blocking collectives, shards(): gathered = lax.all_gather(projectors, 'band', axis=1, tiled=True)  54.6 us
  transfers between devices with their start and end apart: 1, of which 1 were waited for; matrix products, arithmetic and copies ran while one was open for 1% of the time, Pallas kernels for 0%

commit v1 on v0

v1 whole, which is shorter than its diff:
```python
import jax
import jax.numpy as jnp
from jax import lax
from jax.experimental import pallas as pl
from jax.experimental.pallas import tpu as pltpu
from jax.sharding import PartitionSpec as P

NP = 128
M = 13
ROWS = 16
NPW_DEV = 1280
NB_DEV = 896
CHUNK = 32
BLOCK_PW = 256
BF16 = jnp.bfloat16
F32 = jnp.float32


def coupling_block(coupling, offsets, counts, proj):
    local = jnp.arange(M, dtype=jnp.int32)
    target = offsets[:, None] + local[None, :]
    select = (proj[None, :, None] == target[:, None, :]) & (
        local[None, None, :] < counts[:, None, None]
    )
    select = select.astype(jnp.float32)
    sym = (coupling + jnp.swapaxes(coupling, 1, 2)) * 0.5
    return jnp.einsum("api,aij,aqj->pq", select, sym, select, precision=lax.Precision.HIGHEST)


def over_pw(x, bits):
    return lax.ppermute(x, "pw", [(i, i ^ bits) for i in range(32)])


def over_band(x, bits):
    return lax.ppermute(x, "band", [(i, i ^ bits) for i in range(8)])


def two_terms(x):
    high = x.astype(BF16)
    return high, (x - high.astype(F32)).astype(BF16)


def project_kernel(place_ref, block_ref, *refs):
    pieces, (waves_ref, keep_ref, send_ref, rows_ref) = refs[:8], refs[8:]
    core, y = place_ref[0], place_ref[1]
    for r, piece in enumerate(pieces):
        for k in range(2):
            rows_ref[pl.ds(k * NP + r * ROWS, ROWS), :] = piece[k]
    rows = rows_ref[...]
    first = jnp.dot(rows, waves_ref[0], preferred_element_type=F32)
    second = jnp.dot(rows, waves_ref[1], preferred_element_type=F32)
    real = first[:NP] + second[NP:]
    imag = second[:NP] - first[NP:]
    block_high, block_low = two_terms(block_ref[...])
    left = jnp.concatenate([block_high, block_high, block_low], axis=1)

    def couple(part):
        high, low = two_terms(part)
        right = jnp.concatenate([high, low, high], axis=0)
        return jnp.dot(left, right, preferred_element_type=F32)

    real, imag = couple(real), couple(imag)
    keep = jnp.where(core == 0, real, imag)
    send = jnp.where(core == 0, imag, real)
    for t in range(4):
        at = jnp.bitwise_xor(y, t)
        keep_ref[at] = keep[t * CHUNK : (t + 1) * CHUNK]
        send_ref[at] = send[t * CHUNK : (t + 1) * CHUNK]


def project(place, block, pieces, waves):
    vmem = pl.BlockSpec(memory_space=pltpu.VMEM)
    half = jax.ShapeDtypeStruct((4, CHUNK, NB_DEV), F32)
    return pl.pallas_call(
        project_kernel,
        out_shape=(half, half),
        in_specs=[pl.BlockSpec(memory_space=pltpu.SMEM)] + [vmem] * 10,
        out_specs=(vmem, vmem),
        scratch_shapes=[pltpu.VMEM((2 * NP, NPW_DEV), BF16)],
        compiler_params=pltpu.CompilerParams(vmem_limit_bytes=24 * 1024 * 1024),
        cost_estimate=pl.CostEstimate(
            flops=4 * 2 * NP * NPW_DEV * NB_DEV, bytes_accessed=6 * 1024 * 1024, transcendentals=0
        ),
    )(place, block, *pieces, waves)


def turn_kernel(*refs):
    pieces, out_ref, rows_ref = refs[:8], refs[8], refs[9]
    for r, piece in enumerate(pieces):
        for k in range(2):
            rows_ref[pl.ds(k * NP + r * ROWS, ROWS), :] = piece[k]
    out_ref[...] = rows_ref[...].T


def turn(pieces):
    vmem = pl.BlockSpec(memory_space=pltpu.VMEM)
    return pl.pallas_call(
        turn_kernel,
        out_shape=jax.ShapeDtypeStruct((NPW_DEV, 2 * NP), BF16),
        in_specs=[vmem] * 8,
        out_specs=vmem,
        scratch_shapes=[pltpu.VMEM((2 * NP, NPW_DEV), BF16)],
        compiler_params=pltpu.CompilerParams(vmem_limit_bytes=16 * 1024 * 1024),
        cost_estimate=pl.CostEstimate(
            flops=2 * NP * NPW_DEV, bytes_accessed=4 * 1024 * 1024, transcendentals=0
        ),
    )(*pieces)


def spread_kernel(place_ref, own_ref, other_ref, turned_ref, out_ref, right_ref):
    @pl.when(pl.program_id(0) == 0)
    def _():
        core, y = place_ref[0], place_ref[1]
        for t in range(4):
            at = jnp.bitwise_xor(y, t)
            own, other = own_ref[at], other_ref[at]
            real = jnp.where(core == 0, own, other)
            imag = jnp.where(core == 0, other, own)
            low, high = pl.ds(t * CHUNK, CHUNK), pl.ds(NP + t * CHUNK, CHUNK)
            right_ref[0, low, :] = real
            right_ref[0, high, :] = -imag
            right_ref[1, low, :] = imag
            right_ref[1, high, :] = real

    left = turned_ref[...]
    for k in range(2):
        out_ref[k] = jnp.dot(left, right_ref[k], preferred_element_type=F32).astype(BF16)


def spread_back(place, own, other, turned):
    whole = pl.BlockSpec((4, CHUNK, NB_DEV), lambda i: (0, 0, 0))
    return pl.pallas_call(
        spread_kernel,
        grid=(NPW_DEV // BLOCK_PW,),
        out_shape=jax.ShapeDtypeStruct((2, NPW_DEV, NB_DEV), BF16),
        in_specs=[
            pl.BlockSpec(memory_space=pltpu.SMEM),
            whole,
            whole,
            pl.BlockSpec((BLOCK_PW, 2 * NP), lambda i: (i, 0)),
        ],
        out_specs=pl.BlockSpec((2, BLOCK_PW, NB_DEV), lambda i: (0, i, 0)),
        scratch_shapes=[pltpu.VMEM((2, 2 * NP, NB_DEV), BF16)],
        compiler_params=pltpu.CompilerParams(vmem_limit_bytes=16 * 1024 * 1024),
        cost_estimate=pl.CostEstimate(
            flops=4 * 2 * NP * NPW_DEV * NB_DEV, bytes_accessed=6 * 1024 * 1024, transcendentals=0
        ),
    )(place, own, other, turned)


def shards(waves, projectors, coupling, offsets, counts):
    pw, band = lax.axis_index("pw"), lax.axis_index("band")
    core, y = pw & 1, (pw >> 1) & 3
    place = jnp.stack([core, y])

    far = over_band(projectors, 1)
    near = [over_band(projectors, bits) for bits in (2, 6, 4)]
    rest = [over_band(far, bits) for bits in (2, 6, 4)]
    pieces = [projectors, far, near[0], rest[0], near[2], rest[2], near[1], rest[1]]
    proj = jnp.arange(NP, dtype=jnp.int32) ^ (band * ROWS)
    block = coupling_block(coupling, offsets, counts, proj)

    keep, send = project(place, block, pieces, waves)
    turned = turn(pieces)
    total = keep + over_pw(send, 1)

    sums = total[0]
    for arrived in [over_pw(total[s].astype(BF16), 2 * s) for s in (1, 3, 2)]:
        sums = sums + arrived.astype(F32)
    sent = sums.astype(BF16)
    for arrived in [over_pw(sent, 8 * s) for s in (1, 2, 3)]:
        sums = sums + arrived.astype(F32)
    mine = sums.astype(BF16)
    chunk = {s: over_pw(mine, 2 * s) for s in (1, 3, 2)}
    own = jnp.stack([mine, chunk[1], chunk[2], chunk[3]])
    other = over_pw(own, 1)
    return spread_back(place, own, other, turned)


def solution(mesh):
    placed = (P(None, "pw", "band"), P(None, "band", "pw"), P(), P(), P())
    return jax.shard_map(
        shards, mesh=mesh, in_specs=placed, out_specs=P(None, "pw", "band"), check_vma=False
    )
```

time: 365 us -> 64 us (0.18)
  waiting for transfers between devices: 272 us -> 17.6 us
  blocking collectives: 54.6 us -> 0 us
  starting transfers between devices: 0.01 us -> 31.1 us
  between operations: 13.5 us -> 0.08 us
  matrix products: 12.7 us -> 1.6 us
  Pallas kernels: 0 us -> 7.4 us
    psum x1 -> x0, waiting for transfers between devices: 272 us -> none  [shards(): coeffs = lax.psum(partial_coeffs, 'pw')]
    all_gather x1 -> x0, blocking collectives: 54.6 us -> none  [shards(): gathered = lax.all_gather(projectors, 'band', axis=1, tiled=True)]
    ppermute x0 -> x18, starting transfers between devices: none -> 31.1 us  [the longest x11 16.8 us: over_pw(): return lax.ppermute(x, 'pw', [(i, i ^ bits) for i in range(32)])]
    ppermute x0 -> x18, waiting for transfers between devices: none -> 17.6 us  [the longest x11 13.5 us: over_pw(): return lax.ppermute(x, 'pw', [(i, i ^ bits) for i in range(32)])]
    dot_general x9 -> x0, matrix products: 11.1 us -> none  [the longest x1 2.78 us: shards(): jnp.einsum('pq,kqb->kpb', block, coeffs, precision=lax.Precision.HIGHEST)]
    pallas_call x0 -> x3, Pallas kernels: none -> 7.4 us  [the longest x1 4.74 us: spread_back(): pl.pallas_call(spread_kernel, grid=(NPW_DEV // BLOCK_PW,), out_shape=jax....]
    another operation x1 -> x0, local copies, waits for them, and re-layouts: 7.27 us -> none  [spread_back(): return jnp.stack([real, imag])]
    unnamed x9 -> x5, local copies, waits for them, and re-layouts: 0.18 us -> 4.23 us
  transfers between devices with their start and end apart: 1 -> 18, of which waited for: 1 -> 10; matrix products, arithmetic and copies ran while one was open for 1% -> 7% of each run, Pallas kernels for 0% -> 0%
where the time goes in v1:
time: 64 us; the launch traced here: 63.7 us
  starting transfers between devices  31.1 us (49%)
  waiting for transfers between devices  17.6 us (28%)
  Pallas kernels  7.4 us (12%)
  local copies, waits for them, and re-layouts  4.25 us (7%)
  other arithmetic  1.71 us (3%)
  matrix products  1.6 us (2%)
    ppermute x11, starting transfers between devices, over_pw(): return lax.ppermute(x, 'pw', [(i, i ^ bits) for i in range(32)])  16.8 us
    ppermute x7, starting transfers between devices, over_band(): return lax.ppermute(x, 'band', [(i, i ^ bits) for i in range(8)])  14.3 us
    ppermute x11, waiting for transfers between devices, over_pw(): return lax.ppermute(x, 'pw', [(i, i ^ bits) for i in range(32)])  13.5 us
    pallas_call x1, Pallas kernels, spread_back(): pl.pallas_call(spread_kernel, grid=(NPW_DEV // BLOCK_PW,), out_shape=jax....  4.74 us
    unnamed x5, local copies, waits for them, and re-layouts  4.23 us
    ppermute x7, waiting for transfers between devices, over_band(): return lax.ppermute(x, 'band', [(i, i ^ bits) for i in range(8)])  4.05 us
    pallas_call x1, Pallas kernels, project(): pl.pallas_call(project_kernel, out_shape=(half, half), in_specs=[pl.Block...  2.44 us
    dot_general x2, matrix products, coupling_block(): jnp.einsum('api,aij,aqj->pq', select, sym, select, precision=lax.Precisio...  1.6 us
  transfers between devices with their start and end apart: 18, of which 10 were waited for; matrix products, arithmetic and copies ran while one was open for 7% of the time, Pallas kernels for 0%

profile of v1, /device:TPU:1, one launch (start us, length us, event | category | flops | bytes accessed | tf_op | source)
XLA Modules:
  0.0 63.7 jit_solution(15072072458870795493)
XLA Ops:
  0.0 3.3 %collective-permute-start.5 = (bf16[2,16,1280]{2,1,0:T(8,128)(2,1)}, bf16[2,16,1280]{2,1,0:T(8,128)(2,1)S(1)}, u32[]{:S(2)}, u32[]{:S(2)}) collective-permute-start(bf16[2,16,1280]{2,1,0:T(8,128)(2,1)} %refs_0_.3), channel_id=1, source_target_pairs={{0,6},{1,7},{2,4},{3,5},{4,2},{5,3},{6,0},{7,1},{8,14},{9,15},{10,... | collective-permute-start | bytes 245768 | tf_op jit(solution)/shard_map/ppermute | solution.py:35
  3.3 0.5 collective-permute-start.3
  3.9 7.1 %collective-permute-start = (bf16[2,16,1280]{2,1,0:T(8,128)(2,1)}, bf16[2,16,1280]{2,1,0:T(8,128)(2,1)S(1)}, u32[]{:S(2)}, u32[]{:S(2)}) collective-permute-start(bf16[2,16,1280]{2,1,0:T(8,128)(2,1)} %refs_0_.3), channel_id=1, source_target_pairs={{0,1},{1,0},{2,3},{3,2},{4,5},{5,4},{6,7},{7,6},{8,9},{9,8},{10,11... | collective-permute-start | bytes 245768 | tf_op jit(solution)/shard_map/ppermute | solution.py:35
  11.0 0.7 %iota_compare_fusion = pred[12,13]{1,0:T(8,128)(4,1)S(1)} fusion(s32[12]{0:T(128)} %param.9), kind=kLoop, calls=%fused_computation.21 | loop fusion | flops 156 | bytes 204 | tf_op jit(solution)/shard_map/lt | solution.py:23
  11.7 0.7 %iota_add_fusion = s32[12,13]{1,0:T(8,128)S(1)} fusion(s32[12]{0:T(128)} %param.8), kind=kLoop, calls=%fused_computation.22 | loop fusion | flops 156 | bytes 672 | tf_op jit(solution)/shard_map/add | solution.py:21
  12.5 1.0 %copy.6 = f32[12,13,13]{1,2,0:T(8,128)S(1)} copy(f32[12,13,13]{2,1,0:T(8,128)} %param.7) | data formatting | bytes 16224 | tf_op args[2]
  13.5 1.2 %fusion.4 = f32[12,13,128]{2,1,0:T(8,128)S(1)} fusion(f32[12,13,13]{2,1,0:T(8,128)} %param.7, f32[12,13,13]{1,2,0:T(8,128)S(1)} %copy.6, s32[12,13]{1,0:T(8,128)S(1)} %iota_add_fusion, s32[128]{0:T(128)S(1)} %iota_xor_fusion, pred[12,13]{1,0:T(8,128)(4,1)S(1)} %iota_compare_fusion), kind=kOutput, calls=%fused_computation.9 | convolution fusion | flops 3159000 | bytes 97388 | tf_op jit(solution)/shard_map/api,aij,aqj->pq/dot_general | solution.py:27
  14.7 0.4 convolution_bitcast_fusion.block_ref
  15.1 2.6 %collective-permute-start.6 = (bf16[2,16,1280]{2,1,0:T(8,128)(2,1)S(1)}, bf16[2,16,1280]{2,1,0:T(8,128)(2,1)S(1)}, u32[]{:S(2)}, u32[]{:S(2)}) collective-permute-start(bf16[2,16,1280]{2,1,0:T(8,128)(2,1)S(1)} %collective-permute-done.refs_1_), channel_id=1, source_target_pairs={{0,6},{1,7},{2,4},{3,5},{4,2},{5,3},{6,0},{7,1},{8,14},{9,15},{10,... | collective-permute-start | bytes 245768 | tf_op jit(solution)/shard_map/ppermute | solution.py:35
  17.7 0.5 collective-permute-start.4
  18.5 1.4 %collective-permute-done.6.refs_7_ = bf16[2,16,1280]{2,1,0:T(8,128)(2,1)S(1)} collective-permute-done((bf16[2,16,1280]{2,1,0:T(8,128)(2,1)S(1)}, bf16[2,16,1280]{2,1,0:T(8,128)(2,1)S(1)}, u32[]{:S(2)}, u32[]{:S(2)}) %collective-permute-start.6) | collective-permute-done | bytes 81952 | tf_op jit(solution)/shard_map/ppermute | solution.py:35
  19.9 2.6 %collective-permute-done.4.refs_5_ = bf16[2,16,1280]{2,1,0:T(8,128)(2,1)S(1)} collective-permute-done((bf16[2,16,1280]{2,1,0:T(8,128)(2,1)S(1)}, bf16[2,16,1280]{2,1,0:T(8,128)(2,1)S(1)}, u32[]{:S(2)}, u32[]{:S(2)}) %collective-permute-start.4) | collective-permute-done | bytes 81952 | tf_op jit(solution)/shard_map/ppermute | solution.py:35
  22.6 2.3 %copy-done = bf16[2,1280,896]{2,1,0:T(8,128)(2,1)S(1)} copy-done((bf16[2,1280,896]{2,1,0:T(8,128)(2,1)S(1)}, bf16[2,1280,896]{2,1,0:T(8,128)(2,1)}, u32[]{:S(2)}) %copy-start) | copy-done | bytes 4587544
  24.9 0.9 %copy-done.1 = bf16[2,16,1280]{2,1,0:T(8,128)(2,1)S(1)} copy-done((bf16[2,16,1280]{2,1,0:T(8,128)(2,1)S(1)}, bf16[2,16,1280]{2,1,0:T(8,128)(2,1)}, u32[]{:S(2)}) %copy-start.1) | copy-done | bytes 81944
  25.8 2.4 %shard_map.55 = (f32[4,32,896]{2,1,0:T(8,128)S(1)}, f32[4,32,896]{2,1,0:T(8,128)S(1)}) custom-call(s32[2]{0:T(128)S(1)} %pad_add_fusion.place_ref, f32[128,128]{1,0:T(8,128)S(1)} %convolution_bitcast_fusion.block_ref, bf16[2,16,1280]{2,1,0:T(8,128)(2,1)S(1)} %copy-done.1, bf16[2,16,1280]{2,1,0:T(8,128)(2,1)S(1)} %collective-permute-done.refs_1_, ...), custom_call_target="tpu_custom_call" | custom-call | flops 1174405120 | bytes 6291456 | tf_op jit(solution)/shard_map/pallas_call | solution.py:74
  28.2 3.2 %collective-permute-start.7 = (f32[4,32,896]{2,1,0:T(8,128)S(1)}, f32[4,32,896]{2,1,0:T(8,128)S(1)}, u32[]{:S(2)}, u32[]{:S(2)}) collective-permute-start(f32[4,32,896]{2,1,0:T(8,128)S(1)} %get-tuple-element.8), channel_id=1, source_target_pairs={{0,8},{8,0},{16,24},{24,16},{32,40},{40,32},{48,56},{56,48},{64,72... | collective-permute-start | bytes 1376264 | tf_op jit(solution)/shard_map/ppermute | solution.py:31
  31.4 1.4 %collective-permute-done.7 = f32[4,32,896]{2,1,0:T(8,128)S(1)} collective-permute-done((f32[4,32,896]{2,1,0:T(8,128)S(1)}, f32[4,32,896]{2,1,0:T(8,128)S(1)}, u32[]{:S(2)}, u32[]{:S(2)}) %collective-permute-start.7) | collective-permute-done | bytes 458784 | tf_op jit(solution)/shard_map/ppermute | solution.py:31
  33.0 1.4 %collective-permute-start.8 = (bf16[32,896]{1,0:T(8,128)(2,1)S(1)}, bf16[32,896]{1,0:T(8,128)(2,1)S(1)}, u32[]{:S(2)}, u32[]{:S(2)}) collective-permute-start(bf16[32,896]{1,0:T(8,128)(2,1)S(1)} %get-tuple-element.11), channel_id=1, source_target_pairs={{0,16},{8,24},{16,0},{24,8},{32,48},{40,56},{48,32},{56,40},{64,80... | collective-permute-start | bytes 172040 | tf_op jit(solution)/shard_map/ppermute | solution.py:31
  34.3 2.6 %collective-permute-start.10 = (bf16[32,896]{1,0:T(8,128)(2,1)S(1)}, bf16[32,896]{1,0:T(8,128)(2,1)S(1)}, u32[]{:S(2)}, u32[]{:S(2)}) collective-permute-start(bf16[32,896]{1,0:T(8,128)(2,1)S(1)} %get-tuple-element.12), channel_id=1, source_target_pairs={{0,32},{8,40},{16,48},{24,56},{32,0},{40,8},{48,16},{56,24},{64,96... | collective-permute-start | bytes 172040 | tf_op jit(solution)/shard_map/ppermute | solution.py:31
  37.0 2.6 %collective-permute-done.10 = bf16[32,896]{1,0:T(8,128)(2,1)S(1)} collective-permute-done((bf16[32,896]{1,0:T(8,128)(2,1)S(1)}, bf16[32,896]{1,0:T(8,128)(2,1)S(1)}, u32[]{:S(2)}, u32[]{:S(2)}) %collective-permute-start.10) | collective-permute-done | bytes 57376 | tf_op jit(solution)/shard_map/ppermute | solution.py:31
  39.6 1.6 %collective-permute-done.9 = bf16[32,896]{1,0:T(8,128)(2,1)S(1)} collective-permute-done((bf16[32,896]{1,0:T(8,128)(2,1)S(1)}, bf16[32,896]{1,0:T(8,128)(2,1)S(1)}, u32[]{:S(2)}, u32[]{:S(2)}) %collective-permute-start.9) | collective-permute-done | bytes 57376 | tf_op jit(solution)/shard_map/ppermute | solution.py:31
  41.2 1.7 %collective-permute-start.13 = (bf16[32,896]{1,0:T(8,128)(2,1)S(1)}, bf16[32,896]{1,0:T(8,128)(2,1)S(1)}, u32[]{:S(2)}, u32[]{:S(2)}) collective-permute-start(bf16[32,896]{1,0:T(8,128)(2,1)S(1)} %fusion.13), channel_id=1, source_target_pairs={{0,192},{8,200},{16,208},{24,216},{32,224},{40,232},{48,240},{56,2... | collective-permute-start | bytes 172040 | tf_op jit(solution)/shard_map/ppermute | solution.py:31
  43.2 1.6 %collective-permute-start.11 = (bf16[32,896]{1,0:T(8,128)(2,1)S(1)}, bf16[32,896]{1,0:T(8,128)(2,1)S(1)}, u32[]{:S(2)}, u32[]{:S(2)}) collective-permute-start(bf16[32,896]{1,0:T(8,128)(2,1)S(1)} %fusion.13), channel_id=1, source_target_pairs={{0,64},{8,72},{16,80},{24,88},{32,96},{40,104},{48,112},{56,120},{... | collective-permute-start | bytes 172040 | tf_op jit(solution)/shard_map/ppermute | solution.py:31
  44.9 1.3 %collective-permute-done.13 = bf16[32,896]{1,0:T(8,128)(2,1)S(1)} collective-permute-done((bf16[32,896]{1,0:T(8,128)(2,1)S(1)}, bf16[32,896]{1,0:T(8,128)(2,1)S(1)}, u32[]{:S(2)}, u32[]{:S(2)}) %collective-permute-start.13) | collective-permute-done | bytes 57376 | tf_op jit(solution)/shard_map/ppermute | solution.py:31
  46.2 1.8 %collective-permute-done.12 = bf16[32,896]{1,0:T(8,128)(2,1)S(1)} collective-permute-done((bf16[32,896]{1,0:T(8,128)(2,1)S(1)}, bf16[32,896]{1,0:T(8,128)(2,1)S(1)}, u32[]{:S(2)}, u32[]{:S(2)}) %collective-permute-start.12) | collective-permute-done | bytes 57376 | tf_op jit(solution)/shard_map/ppermute | solution.py:31
  48.0 2.8 %collective-permute-start.16 = (bf16[32,896]{1,0:T(8,128)(2,1)S(1)}, bf16[32,896]{1,0:T(8,128)(2,1)S(1)}, u32[]{:S(2)}, u32[]{:S(2)}) collective-permute-start(bf16[32,896]{1,0:T(8,128)(2,1)S(1)} %add_convert_fusion), channel_id=1, source_target_pairs={{0,48},{8,56},{16,32},{24,40},{32,16},{40,24},{48,0},{56,8},{64,11... | collective-permute-start | bytes 172040 | tf_op jit(solution)/shard_map/ppermute | solution.py:31
  50.9 0.6 %collective-permute-start.14 = (bf16[32,896]{1,0:T(8,128)(2,1)S(1)}, bf16[32,896]{1,0:T(8,128)(2,1)S(1)}, u32[]{:S(2)}, u32[]{:S(2)}) collective-permute-start(bf16[32,896]{1,0:T(8,128)(2,1)S(1)} %add_convert_fusion), channel_id=1, source_target_pairs={{0,16},{8,24},{16,0},{24,8},{32,48},{40,56},{48,32},{56,40},{64,80... | collective-permute-start | bytes 172040 | tf_op jit(solution)/shard_map/ppermute | solution.py:31
  51.5 0.9 %collective-permute-done.16 = bf16[32,896]{1,0:T(8,128)(2,1)S(1)} collective-permute-done((bf16[32,896]{1,0:T(8,128)(2,1)S(1)}, bf16[32,896]{1,0:T(8,128)(2,1)S(1)}, u32[]{:S(2)}, u32[]{:S(2)}) %collective-permute-start.16) | collective-permute-done | bytes 57376 | tf_op jit(solution)/shard_map/ppermute | solution.py:31
  52.4 3.0 %collective-permute-done.15 = bf16[32,896]{1,0:T(8,128)(2,1)S(1)} collective-permute-done((bf16[32,896]{1,0:T(8,128)(2,1)S(1)}, bf16[32,896]{1,0:T(8,128)(2,1)S(1)}, u32[]{:S(2)}, u32[]{:S(2)}) %collective-permute-start.15) | collective-permute-done | bytes 57376 | tf_op jit(solution)/shard_map/ppermute | solution.py:31
  55.5 2.4 %collective-permute-start.17 = (bf16[4,32,896]{2,1,0:T(8,128)(2,1)S(1)}, bf16[4,32,896]{2,1,0:T(8,128)(2,1)S(1)}, u32[]{:S(2)}, u32[]{:S(2)}) collective-permute-start(bf16[4,32,896]{2,1,0:T(8,128)(2,1)S(1)} %pad_maximum_fusion.own_ref), channel_id=1, source_target_pairs={{0,8},{8,0},{16,24},{24,16},{32,40},{40,32},{48,56},{56,48},{64,72... | collective-permute-start | bytes 688136 | tf_op jit(solution)/shard_map/ppermute | solution.py:31
  58.1 0.9 %collective-permute-done.17.other_ref = bf16[4,32,896]{2,1,0:T(8,128)(2,1)S(1)} collective-permute-done((bf16[4,32,896]{2,1,0:T(8,128)(2,1)S(1)}, bf16[4,32,896]{2,1,0:T(8,128)(2,1)S(1)}, u32[]{:S(2)}, u32[]{:S(2)}) %collective-permute-start.17) | collective-permute-done | bytes 229408 | tf_op jit(solution)/shard_map/ppermute | solution.py:31
  59.0 4.7 %shard_map.57 = bf16[2,1280,896]{2,1,0:T(8,128)(2,1)} custom-call(s32[2]{0:T(128)S(1)} %pad_add_fusion.place_ref, bf16[4,32,896]{2,1,0:T(8,128)(2,1)S(1)} %pad_maximum_fusion.own_ref, bf16[4,32,896]{2,1,0:T(8,128)(2,1)S(1)} %collective-permute-done.17.other_ref, bf16[1280,256]{1,0:T(8,128)(2,1)S(1)} %shard_map.56.turned_ref), custom_call_target="tpu_custom_call" | custom-call | flops 1174405120 | bytes 6291456 | tf_op jit(solution)/shard_map/pallas_call | solution.py:132
  (23 shorter events, 1.1 us)
Async XLA Ops:
  0.0 18.2 %collective-permute-start.5 = (bf16[2,16,1280]{2,1,0:T(8,128)(2,1)}, bf16[2,16,1280]{2,1,0:T(8,128)(2,1)S(1)}, u32[]{:S(2)}, u32[]{:S(2)}) collective-permute-start(bf16[2,16,1280]{2,1,0:T(8,128)(2,1)} %refs_0_.3), channel_id=1, source_target_pairs={{0,6},{1,7},{2,4},{3,5},{4,2},{5,3},{6,0},{7,1},{8,14},{9,15},{10,... | collective-permute-start | bytes 245768 | tf_op jit(solution)/shard_map/ppermute | solution.py:35
  3.3 15.2 %collective-permute-start.3 = (bf16[2,16,1280]{2,1,0:T(8,128)(2,1)}, bf16[2,16,1280]{2,1,0:T(8,128)(2,1)S(1)}, u32[]{:S(2)}, u32[]{:S(2)}) collective-permute-start(bf16[2,16,1280]{2,1,0:T(8,128)(2,1)} %refs_0_.3), channel_id=1, source_target_pairs={{0,4},{1,5},{2,6},{3,7},{4,0},{5,1},{6,2},{7,3},{8,12},{9,13},{10,... | collective-permute-start | bytes 245768 | tf_op jit(solution)/shard_map/ppermute | solution.py:35
  3.8 14.7 %collective-permute-start.1 = (bf16[2,16,1280]{2,1,0:T(8,128)(2,1)}, bf16[2,16,1280]{2,1,0:T(8,128)(2,1)S(1)}, u32[]{:S(2)}, u32[]{:S(2)}) collective-permute-start(bf16[2,16,1280]{2,1,0:T(8,128)(2,1)} %refs_0_.3), channel_id=1, source_target_pairs={{0,2},{1,3},{2,0},{3,1},{4,6},{5,7},{6,4},{7,5},{8,10},{9,11},{10,... | collective-permute-start | bytes 245768 | tf_op jit(solution)/shard_map/ppermute | solution.py:35
  3.9 11.2 %collective-permute-start = (bf16[2,16,1280]{2,1,0:T(8,128)(2,1)}, bf16[2,16,1280]{2,1,0:T(8,128)(2,1)S(1)}, u32[]{:S(2)}, u32[]{:S(2)}) collective-permute-start(bf16[2,16,1280]{2,1,0:T(8,128)(2,1)} %refs_0_.3), channel_id=1, source_target_pairs={{0,1},{1,0},{2,3},{3,2},{4,5},{5,4},{6,7},{7,6},{8,9},{9,8},{10,11... | collective-permute-start | bytes 245768 | tf_op jit(solution)/shard_map/ppermute | solution.py:35
  15.1 4.8 %collective-permute-start.6 = (bf16[2,16,1280]{2,1,0:T(8,128)(2,1)S(1)}, bf16[2,16,1280]{2,1,0:T(8,128)(2,1)S(1)}, u32[]{:S(2)}, u32[]{:S(2)}) collective-permute-start(bf16[2,16,1280]{2,1,0:T(8,128)(2,1)S(1)} %collective-permute-done.refs_1_), channel_id=1, source_target_pairs={{0,6},{1,7},{2,4},{3,5},{4,2},{5,3},{6,0},{7,1},{8,14},{9,15},{10,... | collective-permute-start | bytes 245768 | tf_op jit(solution)/shard_map/ppermute | solution.py:35
  17.7 4.9 %collective-permute-start.4 = (bf16[2,16,1280]{2,1,0:T(8,128)(2,1)S(1)}, bf16[2,16,1280]{2,1,0:T(8,128)(2,1)S(1)}, u32[]{:S(2)}, u32[]{:S(2)}) collective-permute-start(bf16[2,16,1280]{2,1,0:T(8,128)(2,1)S(1)} %collective-permute-done.refs_1_), channel_id=1, source_target_pairs={{0,4},{1,5},{2,6},{3,7},{4,0},{5,1},{6,2},{7,3},{8,12},{9,13},{10,... | collective-permute-start | bytes 245768 | tf_op jit(solution)/shard_map/ppermute | solution.py:35
  18.2 4.4 %collective-permute-start.2 = (bf16[2,16,1280]{2,1,0:T(8,128)(2,1)S(1)}, bf16[2,16,1280]{2,1,0:T(8,128)(2,1)S(1)}, u32[]{:S(2)}, u32[]{:S(2)}) collective-permute-start(bf16[2,16,1280]{2,1,0:T(8,128)(2,1)S(1)} %collective-permute-done.refs_1_), channel_id=1, source_target_pairs={{0,2},{1,3},{2,0},{3,1},{4,6},{5,7},{6,4},{7,5},{8,10},{9,11},{10,... | collective-permute-start | bytes 245768 | tf_op jit(solution)/shard_map/ppermute | solution.py:35
  22.6 2.3 %copy-start = (bf16[2,1280,896]{2,1,0:T(8,128)(2,1)S(1)}, bf16[2,1280,896]{2,1,0:T(8,128)(2,1)}, u32[]{:S(2)}) copy-start(bf16[2,1280,896]{2,1,0:T(8,128)(2,1)} %refs_8_.1) | copy-start | bytes 13762564
  24.9 0.9 %copy-start.1 = (bf16[2,16,1280]{2,1,0:T(8,128)(2,1)S(1)}, bf16[2,16,1280]{2,1,0:T(8,128)(2,1)}, u32[]{:S(2)}) copy-start(bf16[2,16,1280]{2,1,0:T(8,128)(2,1)} %refs_0_.3) | copy-start | bytes 245764
  28.2 4.6 %collective-permute-start.7 = (f32[4,32,896]{2,1,0:T(8,128)S(1)}, f32[4,32,896]{2,1,0:T(8,128)S(1)}, u32[]{:S(2)}, u32[]{:S(2)}) collective-permute-start(f32[4,32,896]{2,1,0:T(8,128)S(1)} %get-tuple-element.8), channel_id=1, source_target_pairs={{0,8},{8,0},{16,24},{24,16},{32,40},{40,32},{48,56},{56,48},{64,72... | collective-permute-start | bytes 1376264 | tf_op jit(solution)/shard_map/ppermute | solution.py:31
  33.0 4.0 %collective-permute-start.8 = (bf16[32,896]{1,0:T(8,128)(2,1)S(1)}, bf16[32,896]{1,0:T(8,128)(2,1)S(1)}, u32[]{:S(2)}, u32[]{:S(2)}) collective-permute-start(bf16[32,896]{1,0:T(8,128)(2,1)S(1)} %get-tuple-element.11), channel_id=1, source_target_pairs={{0,16},{8,24},{16,0},{24,8},{32,48},{40,56},{48,32},{56,40},{64,80... | collective-permute-start | bytes 172040 | tf_op jit(solution)/shard_map/ppermute | solution.py:31
  34.3 5.2 %collective-permute-start.10 = (bf16[32,896]{1,0:T(8,128)(2,1)S(1)}, bf16[32,896]{1,0:T(8,128)(2,1)S(1)}, u32[]{:S(2)}, u32[]{:S(2)}) collective-permute-start(bf16[32,896]{1,0:T(8,128)(2,1)S(1)} %get-tuple-element.12), channel_id=1, source_target_pairs={{0,32},{8,40},{16,48},{24,56},{32,0},{40,8},{48,16},{56,24},{64,96... | collective-permute-start | bytes 172040 | tf_op jit(solution)/shard_map/ppermute | solution.py:31
  37.0 4.2 %collective-permute-start.9 = (bf16[32,896]{1,0:T(8,128)(2,1)S(1)}, bf16[32,896]{1,0:T(8,128)(2,1)S(1)}, u32[]{:S(2)}, u32[]{:S(2)}) collective-permute-start(bf16[32,896]{1,0:T(8,128)(2,1)S(1)} %get-tuple-element.13), channel_id=1, source_target_pairs={{0,48},{8,56},{16,32},{24,40},{32,16},{40,24},{48,0},{56,8},{64,11... | collective-permute-start | bytes 172040 | tf_op jit(solution)/shard_map/ppermute | solution.py:31
  41.2 4.9 %collective-permute-start.13 = (bf16[32,896]{1,0:T(8,128)(2,1)S(1)}, bf16[32,896]{1,0:T(8,128)(2,1)S(1)}, u32[]{:S(2)}, u32[]{:S(2)}) collective-permute-start(bf16[32,896]{1,0:T(8,128)(2,1)S(1)} %fusion.13), channel_id=1, source_target_pairs={{0,192},{8,200},{16,208},{24,216},{32,224},{40,232},{48,240},{56,2... | collective-permute-start | bytes 172040 | tf_op jit(solution)/shard_map/ppermute | solution.py:31
  43.0 5.0 %collective-permute-start.12 = (bf16[32,896]{1,0:T(8,128)(2,1)S(1)}, bf16[32,896]{1,0:T(8,128)(2,1)S(1)}, u32[]{:S(2)}, u32[]{:S(2)}) collective-permute-start(bf16[32,896]{1,0:T(8,128)(2,1)S(1)} %fusion.13), channel_id=1, source_target_pairs={{0,128},{8,136},{16,144},{24,152},{32,160},{40,168},{48,176},{56,1... | collective-permute-start | bytes 172040 | tf_op jit(solution)/shard_map/ppermute | solution.py:31
  43.2 4.7 %collective-permute-start.11 = (bf16[32,896]{1,0:T(8,128)(2,1)S(1)}, bf16[32,896]{1,0:T(8,128)(2,1)S(1)}, u32[]{:S(2)}, u32[]{:S(2)}) collective-permute-start(bf16[32,896]{1,0:T(8,128)(2,1)S(1)} %fusion.13), channel_id=1, source_target_pairs={{0,64},{8,72},{16,80},{24,88},{32,96},{40,104},{48,112},{56,120},{... | collective-permute-start | bytes 172040 | tf_op jit(solution)/shard_map/ppermute | solution.py:31
  48.0 4.4 %collective-permute-start.16 = (bf16[32,896]{1,0:T(8,128)(2,1)S(1)}, bf16[32,896]{1,0:T(8,128)(2,1)S(1)}, u32[]{:S(2)}, u32[]{:S(2)}) collective-permute-start(bf16[32,896]{1,0:T(8,128)(2,1)S(1)} %add_convert_fusion), channel_id=1, source_target_pairs={{0,48},{8,56},{16,32},{24,40},{32,16},{40,24},{48,0},{56,8},{64,11... | collective-permute-start | bytes 172040 | tf_op jit(solution)/shard_map/ppermute | solution.py:31
  50.8 4.6 %collective-permute-start.15 = (bf16[32,896]{1,0:T(8,128)(2,1)S(1)}, bf16[32,896]{1,0:T(8,128)(2,1)S(1)}, u32[]{:S(2)}, u32[]{:S(2)}) collective-permute-start(bf16[32,896]{1,0:T(8,128)(2,1)S(1)} %add_convert_fusion), channel_id=1, source_target_pairs={{0,32},{8,40},{16,48},{24,56},{32,0},{40,8},{48,16},{56,24},{64,96... | collective-permute-start | bytes 172040 | tf_op jit(solution)/shard_map/ppermute | solution.py:31
  50.9 4.5 %collective-permute-start.14 = (bf16[32,896]{1,0:T(8,128)(2,1)S(1)}, bf16[32,896]{1,0:T(8,128)(2,1)S(1)}, u32[]{:S(2)}, u32[]{:S(2)}) collective-permute-start(bf16[32,896]{1,0:T(8,128)(2,1)S(1)} %add_convert_fusion), channel_id=1, source_target_pairs={{0,16},{8,24},{16,0},{24,8},{32,48},{40,56},{48,32},{56,40},{64,80... | collective-permute-start | bytes 172040 | tf_op jit(solution)/shard_map/ppermute | solution.py:31
  55.5 3.5 %collective-permute-start.17 = (bf16[4,32,896]{2,1,0:T(8,128)(2,1)S(1)}, bf16[4,32,896]{2,1,0:T(8,128)(2,1)S(1)}, u32[]{:S(2)}, u32[]{:S(2)}) collective-permute-start(bf16[4,32,896]{2,1,0:T(8,128)(2,1)S(1)} %pad_maximum_fusion.own_ref), channel_id=1, source_target_pairs={{0,8},{8,0},{16,24},{24,16},{32,40},{40,32},{48,56},{56,48},{64,72... | collective-permute-start | bytes 688136 | tf_op jit(solution)/shard_map/ppermute | solution.py:31

commit v2 on v1

v2 whole, which is shorter than its diff:
```python
import jax
import jax.numpy as jnp
from jax import lax
from jax.experimental import pallas as pl
from jax.experimental.pallas import tpu as pltpu
from jax.sharding import PartitionSpec as P

NP = 128
NATOM = 12
M = 13
ROWS = 16
HALF = 64
NPW_DEV = 1280
NB_DEV = 896
CHUNK = 32
BLOCK_PW = 640
BF16 = jnp.bfloat16
F32 = jnp.float32
MIB = 1024 * 1024


def over_pw(x, bits):
    return lax.ppermute(x, "pw", [(i, i ^ bits) for i in range(32)])


def over_band(x, bits):
    return lax.ppermute(x, "band", [(i, i ^ bits) for i in range(8)])


def vmem():
    return pl.BlockSpec(memory_space=pltpu.VMEM)


def smem():
    return pl.BlockSpec(memory_space=pltpu.SMEM)


def params(mib):
    return pltpu.CompilerParams(vmem_limit_bytes=mib * MIB)


def cost(flops, nbytes):
    return pl.CostEstimate(flops=flops, bytes_accessed=nbytes, transcendentals=0)


def two_terms(x):
    high = x.astype(BF16)
    return high, (x - high.astype(F32)).astype(BF16)


def ahead_kernel(
    pick_ref,
    offsets_hbm,
    counts_hbm,
    coupling_hbm,
    waves_hbm,
    left_ref,
    waves_ref,
    placed_ref,
    offsets_ref,
    counts_ref,
    coupling_ref,
    sem,
):
    pairs = (
        (offsets_hbm, offsets_ref),
        (counts_hbm, counts_ref),
        (coupling_hbm, coupling_ref),
        (waves_hbm, waves_ref),
    )
    copies = [pltpu.make_async_copy(a, b, sem.at[i]) for i, (a, b) in enumerate(pairs)]
    for copy in copies:
        copy.start()
    placed_ref[...] = jnp.zeros(placed_ref.shape, F32)
    for copy in copies[:3]:
        copy.wait()
    row = lax.broadcasted_iota(jnp.int32, (M, NP), 0)
    column = lax.broadcasted_iota(jnp.int32, (M, NP), 1)
    for atom in range(NATOM):
        at, count = offsets_ref[atom], counts_ref[atom]
        wide = jnp.concatenate([coupling_ref[atom], jnp.zeros((M, NP - M), F32)], axis=1)
        wide = jnp.where((row < count) & (column < count), wide, 0.0)
        placed_ref[pl.ds(at, M), :] = pltpu.roll(wide, at, 1)
    placed = placed_ref[:NP, :]
    block = (placed + placed.T) * 0.5
    pick, pick_turned = pick_ref[0], pick_ref[1]

    def reorder(part):
        part = jnp.dot(part, pick, preferred_element_type=F32).astype(BF16)
        return jnp.dot(pick_turned, part, preferred_element_type=F32).astype(BF16)

    high, low = (reorder(part) for part in two_terms(block))
    left_ref[...] = jnp.concatenate([high, high, low], axis=1)
    copies[3].wait()


def pick_kernel(band_ref, pick_ref):
    place = lax.broadcasted_iota(jnp.int32, (NP, NP), 1)
    piece = place >> 4
    piece = ((piece & 3) << 1) | (piece >> 2)
    number = (jnp.bitwise_xor(piece, band_ref[0]) << 4) | (place & 15)
    pick = (lax.broadcasted_iota(jnp.int32, (NP, NP), 0) == number).astype(F32)
    pick_ref[0] = pick.astype(BF16)
    pick_ref[1] = pick.T.astype(BF16)


def gathered_order(band):
    return pl.pallas_call(
        pick_kernel,
        out_shape=jax.ShapeDtypeStruct((2, NP, NP), BF16),
        in_specs=[smem()],
        out_specs=vmem(),
        compiler_params=params(8),
        cost_estimate=cost(4 * 10**9, 1),
    )(band)


def ahead(pick, offsets, counts, coupling, waves):
    hbm = pl.BlockSpec(memory_space=pltpu.HBM)
    return pl.pallas_call(
        ahead_kernel,
        out_shape=(
            jax.ShapeDtypeStruct((NP, 3 * NP), BF16),
            jax.ShapeDtypeStruct(waves.shape, BF16),
        ),
        in_specs=[vmem()] + [hbm] * 4,
        out_specs=(vmem(), vmem()),
        scratch_shapes=[
            pltpu.VMEM((NP + ROWS, NP), F32),
            pltpu.SMEM((NATOM,), jnp.int32),
            pltpu.SMEM((NATOM,), jnp.int32),
            pltpu.VMEM((NATOM, M, M), F32),
            pltpu.SemaphoreType.DMA((4,)),
        ],
        compiler_params=params(46),
        cost_estimate=cost(2 * 10**9, 8 * MIB),
    )(pick, offsets, counts, coupling, waves)


def fill_rows(pieces, rows_ref):
    for i, piece in enumerate(pieces):
        at = (i // 4) * HALF + (3 - i % 4) * ROWS
        for k in range(2):
            rows_ref[pl.ds(k * NP + at, ROWS), :] = piece[k]


def project_kernel(place_ref, left_ref, waves_ref, *refs):
    pieces, (keep_ref, send_ref, rows_ref) = refs[:8], refs[8:]
    core, y = place_ref[0], place_ref[1]
    fill_rows(pieces, rows_ref)
    rows = rows_ref[...]
    first = jnp.dot(rows, waves_ref[0], preferred_element_type=F32)
    second = jnp.dot(rows, waves_ref[1], preferred_element_type=F32)
    left = left_ref[...]

    def couple(part):
        high, low = two_terms(part)
        right = jnp.concatenate([high, low, high], axis=0)
        return jnp.dot(left, right, preferred_element_type=F32)

    real = couple(first[:NP] + second[NP:])
    imag = couple(second[:NP] - first[NP:])
    keep = jnp.where(core == 0, real, imag)
    send = jnp.where(core == 0, imag, real)
    for t in range(4):
        at = jnp.bitwise_xor(y, t)
        keep_ref[at] = keep[t * CHUNK : (t + 1) * CHUNK]
        send_ref[at] = send[t * CHUNK : (t + 1) * CHUNK]


def project(place, left, waves, pieces):
    half = jax.ShapeDtypeStruct((4, CHUNK, NB_DEV), F32)
    return pl.pallas_call(
        project_kernel,
        out_shape=(half, half),
        in_specs=[smem()] + [vmem()] * 10,
        out_specs=(vmem(), vmem()),
        scratch_shapes=[pltpu.VMEM((2 * NP, NPW_DEV), BF16)],
        compiler_params=params(16),
        cost_estimate=cost(8 * NP * NPW_DEV * NB_DEV, 6 * MIB),
    )(place, left, waves, *pieces)


def turn_kernel(*refs):
    pieces, (out_ref, rows_ref) = refs[:8], refs[8:]
    fill_rows(pieces, rows_ref)
    turned = rows_ref[...].T
    first, second = turned[:, :NP], turned[:, NP:]
    out_ref[0, :, :NP] = first
    out_ref[0, :, NP:] = -second
    out_ref[1, :, :NP] = second
    out_ref[1, :, NP:] = first


def turn(pieces):
    return pl.pallas_call(
        turn_kernel,
        out_shape=jax.ShapeDtypeStruct((2, NPW_DEV, 2 * NP), BF16),
        in_specs=[vmem()] * 8,
        out_specs=vmem(),
        scratch_shapes=[pltpu.VMEM((2 * NP, NPW_DEV), BF16)],
        compiler_params=params(16),
        cost_estimate=cost(2 * NP * NPW_DEV, 2 * MIB),
    )(*pieces)


def spread_kernel(place_ref, own_ref, other_ref, turned_ref, out_ref, right_ref, result_ref, sem):
    core, y = place_ref[0], place_ref[1]
    for s in range(4):
        at = jnp.bitwise_xor(y, s) * CHUNK
        own_at = pl.multiple_of(core * NP + at, CHUNK)
        other_at = pl.multiple_of((1 - core) * NP + at, CHUNK)
        right_ref[pl.ds(own_at, CHUNK), :] = own_ref[s]
        right_ref[pl.ds(other_at, CHUNK), :] = other_ref[s]
    right = right_ref[...]
    copies = []
    for k in range(2):
        for at in range(0, NPW_DEV, BLOCK_PW):
            rows = pl.ds(at, BLOCK_PW)
            result_ref[k, rows, :] = jnp.dot(
                turned_ref[k, rows, :], right, preferred_element_type=F32
            ).astype(BF16)
            copy = pltpu.make_async_copy(
                result_ref.at[k, rows], out_ref.at[k, rows], sem.at[len(copies)]
            )
            copy.start()
            copies.append(copy)
    for copy in copies:
        copy.wait()


def spread_back(place, own, other, turned):
    return pl.pallas_call(
        spread_kernel,
        out_shape=jax.ShapeDtypeStruct((2, NPW_DEV, NB_DEV), BF16),
        in_specs=[smem()] + [vmem()] * 3,
        out_specs=pl.BlockSpec(memory_space=pltpu.HBM),
        scratch_shapes=[
            pltpu.VMEM((2 * NP, NB_DEV), BF16),
            pltpu.VMEM((2, NPW_DEV, NB_DEV), BF16),
            pltpu.SemaphoreType.DMA((2 * NPW_DEV // BLOCK_PW,)),
        ],
        compiler_params=params(16),
        cost_estimate=cost(8 * NP * NPW_DEV * NB_DEV, 6 * MIB),
    )(place, own, other, turned)


def shards(waves, projectors, coupling, offsets, counts):
    pw, band = lax.axis_index("pw"), lax.axis_index("band")
    place = jnp.stack([pw & 1, (pw >> 1) & 3])

    distant = over_band(projectors, 1)
    near = [over_band(projectors, bits) for bits in (6, 4, 2)] + [projectors]
    far = [over_band(distant, bits) for bits in (6, 4, 2)] + [distant]
    pick = gathered_order(band.reshape(1))
    pick, _ = lax.optimization_barrier((pick, distant))
    left, waves = ahead(pick, offsets, counts, coupling, waves)
    keep, send = project(place, left, waves, near + far)
    turned = turn(near + far)
    total = keep + over_pw(send, 1)

    sums = total[0]
    for arrived in [over_pw(total[s].astype(BF16), 2 * s) for s in (3, 2, 1)]:
        sums = sums + arrived.astype(F32)
    sent = sums.astype(BF16)
    for arrived in [over_pw(sent, 8 * s) for s in (3, 2, 1)]:
        sums = sums + arrived.astype(F32)
    mine = sums.astype(BF16)
    chunk = {s: over_pw(mine, 2 * s) for s in (3, 2, 1)}
    own = jnp.stack([mine, chunk[1], chunk[2], chunk[3]])
    other = over_pw(own, 1)
    return spread_back(place, own, other, turned)


def solution(mesh):
    placed = (P(None, "pw", "band"), P(None, "band", "pw"), P(), P(), P())
    return jax.shard_map(
        shards, mesh=mesh, in_specs=placed, out_specs=P(None, "pw", "band"), check_vma=False
    )
```

time: 64 us -> 55.7 us (0.87)
  local copies, waits for them, and re-layouts: 4.25 us -> 0.03 us
  waiting for transfers between devices: 17.6 us -> 13.4 us
  starting transfers between devices: 31.1 us -> 33.4 us
  matrix products: 1.6 us -> 0 us
  other arithmetic: 1.71 us -> 0.28 us
  Pallas kernels: 7.4 us -> 8.39 us
    unnamed x5 -> x8, local copies, waits for them, and re-layouts: 4.23 us -> 0.02 us
    ppermute x11, starting transfers between devices: 16.8 us -> 19.1 us  [over_pw(): return lax.ppermute(x, 'pw', [(i, i ^ bits) for i in range(32)])]
    ppermute x7, waiting for transfers between devices: 4.05 us -> 1.92 us  [over_band(): return lax.ppermute(x, 'band', [(i, i ^ bits) for i in range(8)])]
    ppermute x11, waiting for transfers between devices: 13.5 us -> 11.5 us  [over_pw(): return lax.ppermute(x, 'pw', [(i, i ^ bits) for i in range(32)])]
    dot_general x2 -> x0, matrix products: 1.6 us -> none  [coupling_block(): jnp.einsum('api,aij,aqj->pq', select, sym, select, precision=lax.Precisio...]
    pallas_call x3 -> x5, Pallas kernels: 7.4 us -> 8.39 us  [the longest x1 3.26 us: spread_back(): pl.pallas_call(spread_kernel, out_shape=jax.ShapeDtypeStruct((2, NPW_DEV,...]
    lt x1 -> x0, other arithmetic: 0.73 us -> none  [coupling_block(): local[None, None, :] < counts[:, None, None]]
    add x1 -> x0, other arithmetic: 0.73 us -> none  [coupling_block(): target = offsets[:, None] + local[None, :]]
  transfers between devices with their start and end apart: 18 -> 18, of which waited for: 10 -> 9; matrix products, arithmetic and copies ran while one was open for 7% -> 0% of each run, Pallas kernels for 0% -> 5%
where the time goes in v2:
time: 55.7 us; the launch traced here: 55.6 us
  starting transfers between devices  33.4 us (60%)
  waiting for transfers between devices  13.4 us (24%)
  Pallas kernels  8.39 us (15%)
    ppermute x11, starting transfers between devices, over_pw(): return lax.ppermute(x, 'pw', [(i, i ^ bits) for i in range(32)])  19.1 us
    ppermute x7, starting transfers between devices, over_band(): return lax.ppermute(x, 'band', [(i, i ^ bits) for i in range(8)])  14.3 us
    ppermute x11, waiting for transfers between devices, over_pw(): return lax.ppermute(x, 'pw', [(i, i ^ bits) for i in range(32)])  11.5 us
    pallas_call x1, Pallas kernels, spread_back(): pl.pallas_call(spread_kernel, out_shape=jax.ShapeDtypeStruct((2, NPW_DEV,...  3.26 us
    pallas_call x1, Pallas kernels, project(): pl.pallas_call(project_kernel, out_shape=(half, half), in_specs=[smem()]...  2.46 us
    pallas_call x1, Pallas kernels, ahead(): pl.pallas_call(ahead_kernel, out_shape=(jax.ShapeDtypeStruct((NP, 3 * NP)...  2.34 us
    ppermute x7, waiting for transfers between devices, over_band(): return lax.ppermute(x, 'band', [(i, i ^ bits) for i in range(8)])  1.92 us
  transfers between devices with their start and end apart: 18, of which 9 were waited for; matrix products, arithmetic and copies ran while one was open for 0% of the time, Pallas kernels for 5%

profile of v2, /device:TPU:1, one launch (start us, length us, event | category | flops | bytes accessed | tf_op | source)
XLA Modules:
  0.0 55.6 jit_solution(16618562717268927778)
XLA Ops:
  0.0 7.7 %collective-permute-start = (bf16[2,16,1280]{2,1,0:T(8,128)(2,1)}, bf16[2,16,1280]{2,1,0:T(8,128)(2,1)S(1)}, u32[]{:S(2)}, u32[]{:S(2)}) collective-permute-start(bf16[2,16,1280]{2,1,0:T(8,128)(2,1)} %refs_3_.3), channel_id=1, source_target_pairs={{0,1},{1,0},{2,3},{3,2},{4,5},{5,4},{6,7},{7,6},{8,9},{9,8},{10,11... | collective-permute-start | bytes 245768 | tf_op jit(solution)/shard_map/ppermute | solution.py:27
  7.7 2.5 %collective-permute-start.1 = (bf16[2,16,1280]{2,1,0:T(8,128)(2,1)}, bf16[2,16,1280]{2,1,0:T(8,128)(2,1)S(1)}, u32[]{:S(2)}, u32[]{:S(2)}) collective-permute-start(bf16[2,16,1280]{2,1,0:T(8,128)(2,1)} %refs_3_.3), channel_id=1, source_target_pairs={{0,6},{1,7},{2,4},{3,5},{4,2},{5,3},{6,0},{7,1},{8,14},{9,15},{10,... | collective-permute-start | bytes 245768 | tf_op jit(solution)/shard_map/ppermute | solution.py:27
  10.2 0.5 collective-permute-start.2
  10.7 0.3 collective-permute-start.3
  11.0 0.1 shard_map.55.pick_ref
  11.2 2.5 %collective-permute-start.4 = (bf16[2,16,1280]{2,1,0:T(8,128)(2,1)S(1)}, bf16[2,16,1280]{2,1,0:T(8,128)(2,1)S(1)}, u32[]{:S(2)}, u32[]{:S(2)}) collective-permute-start(bf16[2,16,1280]{2,1,0:T(8,128)(2,1)S(1)} %collective-permute-done.refs_7_), channel_id=1, source_target_pairs={{0,6},{1,7},{2,4},{3,5},{4,2},{5,3},{6,0},{7,1},{8,14},{9,15},{10,... | collective-permute-start | bytes 245768 | tf_op jit(solution)/shard_map/ppermute | solution.py:27
  13.7 0.5 collective-permute-start.5
  14.2 0.3 collective-permute-start.6
  14.5 2.3 %shard_map.56 = (bf16[128,384]{1,0:T(8,128)(2,1)S(1)}, bf16[2,1280,896]{2,1,0:T(8,128)(2,1)S(1)}) custom-call(bf16[2,128,128]{2,1,0:T(8,128)(2,1)S(1)} %shard_map.55.pick_ref, s32[12]{0:T(128)S(1)} %copy-done.2, s32[12]{0:T(128)S(1)} %copy-done.3, f32[12,13,13]{2,1,0:T(8,128)S(1)} %copy-done.1, bf16[2,1280,896]{2,1,0:T(8,128)(2,1)} %waves_hbm.1), custom_call_target="tpu_custom_call" | custom-call | flops 2000000000 | bytes 8388608 | tf_op jit(solution)/shard_map/pallas_call | solution.py:120
  16.9 1.9 %collective-permute-done.5.refs_5_ = bf16[2,16,1280]{2,1,0:T(8,128)(2,1)S(1)} collective-permute-done((bf16[2,16,1280]{2,1,0:T(8,128)(2,1)S(1)}, bf16[2,16,1280]{2,1,0:T(8,128)(2,1)S(1)}, u32[]{:S(2)}, u32[]{:S(2)}) %collective-permute-start.5) | collective-permute-done | bytes 81952 | tf_op jit(solution)/shard_map/ppermute | solution.py:27
  18.8 2.5 %shard_map.57 = (f32[4,32,896]{2,1,0:T(8,128)S(1)}, f32[4,32,896]{2,1,0:T(8,128)S(1)}) custom-call(s32[2]{0:T(128)S(1)} %pad_add_fusion.place_ref, bf16[128,384]{1,0:T(8,128)(2,1)S(1)} %get-tuple-element.11.left_ref, bf16[2,1280,896]{2,1,0:T(8,128)(2,1)S(1)} %get-tuple-element.12.waves_ref, bf16[2,16,1280]{2,1,0:T(8,128)(2,1)S(1)} %collective-permute-done.1.refs_0_, ...), custom_call_target="tpu_custom_call" | custom-call | flops 1174405120 | bytes 6291456 | tf_op jit(solution)/shard_map/pallas_call | solution.py:173
  21.3 3.0 %collective-permute-start.7 = (f32[4,32,896]{2,1,0:T(8,128)S(1)}, f32[4,32,896]{2,1,0:T(8,128)S(1)}, u32[]{:S(2)}, u32[]{:S(2)}) collective-permute-start(f32[4,32,896]{2,1,0:T(8,128)S(1)} %get-tuple-element.14), channel_id=1, source_target_pairs={{0,8},{8,0},{16,24},{24,16},{32,40},{40,32},{48,56},{56,48},{64,72... | collective-permute-start | bytes 1376264 | tf_op jit(solution)/shard_map/ppermute | solution.py:23
  24.3 1.4 %collective-permute-done.7 = f32[4,32,896]{2,1,0:T(8,128)S(1)} collective-permute-done((f32[4,32,896]{2,1,0:T(8,128)S(1)}, f32[4,32,896]{2,1,0:T(8,128)S(1)}, u32[]{:S(2)}, u32[]{:S(2)}) %collective-permute-start.7) | collective-permute-done | bytes 458784 | tf_op jit(solution)/shard_map/ppermute | solution.py:23
  25.8 1.4 %collective-permute-start.10 = (bf16[32,896]{1,0:T(8,128)(2,1)S(1)}, bf16[32,896]{1,0:T(8,128)(2,1)S(1)}, u32[]{:S(2)}, u32[]{:S(2)}) collective-permute-start(bf16[32,896]{1,0:T(8,128)(2,1)S(1)} %get-tuple-element.18), channel_id=1, source_target_pairs={{0,16},{8,24},{16,0},{24,8},{32,48},{40,56},{48,32},{56,40},{64,80... | collective-permute-start | bytes 172040 | tf_op jit(solution)/shard_map/ppermute | solution.py:23
  27.2 1.9 %collective-permute-start.8 = (bf16[32,896]{1,0:T(8,128)(2,1)S(1)}, bf16[32,896]{1,0:T(8,128)(2,1)S(1)}, u32[]{:S(2)}, u32[]{:S(2)}) collective-permute-start(bf16[32,896]{1,0:T(8,128)(2,1)S(1)} %get-tuple-element.17), channel_id=1, source_target_pairs={{0,48},{8,56},{16,32},{24,40},{32,16},{40,24},{48,0},{56,8},{64,11... | collective-permute-start | bytes 172040 | tf_op jit(solution)/shard_map/ppermute | solution.py:23
  29.1 0.7 %collective-permute-start.9 = (bf16[32,896]{1,0:T(8,128)(2,1)S(1)}, bf16[32,896]{1,0:T(8,128)(2,1)S(1)}, u32[]{:S(2)}, u32[]{:S(2)}) collective-permute-start(bf16[32,896]{1,0:T(8,128)(2,1)S(1)} %get-tuple-element.19), channel_id=1, source_target_pairs={{0,32},{8,40},{16,48},{24,56},{32,0},{40,8},{48,16},{56,24},{64,96... | collective-permute-start | bytes 172040 | tf_op jit(solution)/shard_map/ppermute | solution.py:23
  29.9 1.6 %collective-permute-done.8 = bf16[32,896]{1,0:T(8,128)(2,1)S(1)} collective-permute-done((bf16[32,896]{1,0:T(8,128)(2,1)S(1)}, bf16[32,896]{1,0:T(8,128)(2,1)S(1)}, u32[]{:S(2)}, u32[]{:S(2)}) %collective-permute-start.8) | collective-permute-done | bytes 57376 | tf_op jit(solution)/shard_map/ppermute | solution.py:23
  31.5 2.2 %collective-permute-done.9 = bf16[32,896]{1,0:T(8,128)(2,1)S(1)} collective-permute-done((bf16[32,896]{1,0:T(8,128)(2,1)S(1)}, bf16[32,896]{1,0:T(8,128)(2,1)S(1)}, u32[]{:S(2)}, u32[]{:S(2)}) %collective-permute-start.9) | collective-permute-done | bytes 57376 | tf_op jit(solution)/shard_map/ppermute | solution.py:23
  33.7 1.7 %collective-permute-start.11 = (bf16[32,896]{1,0:T(8,128)(2,1)S(1)}, bf16[32,896]{1,0:T(8,128)(2,1)S(1)}, u32[]{:S(2)}, u32[]{:S(2)}) collective-permute-start(bf16[32,896]{1,0:T(8,128)(2,1)S(1)} %fusion.3), channel_id=1, source_target_pairs={{0,192},{8,200},{16,208},{24,216},{32,224},{40,232},{48,240},{56,2... | collective-permute-start | bytes 172040 | tf_op jit(solution)/shard_map/ppermute | solution.py:23
  35.4 0.3 collective-permute-start.12
  35.7 1.6 %collective-permute-start.13 = (bf16[32,896]{1,0:T(8,128)(2,1)S(1)}, bf16[32,896]{1,0:T(8,128)(2,1)S(1)}, u32[]{:S(2)}, u32[]{:S(2)}) collective-permute-start(bf16[32,896]{1,0:T(8,128)(2,1)S(1)} %fusion.3), channel_id=1, source_target_pairs={{0,64},{8,72},{16,80},{24,88},{32,96},{40,104},{48,112},{56,120},{... | collective-permute-start | bytes 172040 | tf_op jit(solution)/shard_map/ppermute | solution.py:23
  37.3 1.3 %collective-permute-done.11 = bf16[32,896]{1,0:T(8,128)(2,1)S(1)} collective-permute-done((bf16[32,896]{1,0:T(8,128)(2,1)S(1)}, bf16[32,896]{1,0:T(8,128)(2,1)S(1)}, u32[]{:S(2)}, u32[]{:S(2)}) %collective-permute-start.11) | collective-permute-done | bytes 57376 | tf_op jit(solution)/shard_map/ppermute | solution.py:23
  38.6 1.9 %collective-permute-done.12 = bf16[32,896]{1,0:T(8,128)(2,1)S(1)} collective-permute-done((bf16[32,896]{1,0:T(8,128)(2,1)S(1)}, bf16[32,896]{1,0:T(8,128)(2,1)S(1)}, u32[]{:S(2)}, u32[]{:S(2)}) %collective-permute-start.12) | collective-permute-done | bytes 57376 | tf_op jit(solution)/shard_map/ppermute | solution.py:23
  40.6 1.2 %collective-permute-start.16 = (bf16[32,896]{1,0:T(8,128)(2,1)S(1)}, bf16[32,896]{1,0:T(8,128)(2,1)S(1)}, u32[]{:S(2)}, u32[]{:S(2)}) collective-permute-start(bf16[32,896]{1,0:T(8,128)(2,1)S(1)} %add_convert_fusion), channel_id=1, source_target_pairs={{0,48},{8,56},{16,32},{24,40},{32,16},{40,24},{48,0},{56,8},{64,11... | collective-permute-start | bytes 172040 | tf_op jit(solution)/shard_map/ppermute | solution.py:23
  41.8 0.1 collective-permute-start.14
  41.9 2.6 %collective-permute-start.15 = (bf16[32,896]{1,0:T(8,128)(2,1)S(1)}, bf16[32,896]{1,0:T(8,128)(2,1)S(1)}, u32[]{:S(2)}, u32[]{:S(2)}) collective-permute-start(bf16[32,896]{1,0:T(8,128)(2,1)S(1)} %add_convert_fusion), channel_id=1, source_target_pairs={{0,32},{8,40},{16,48},{24,56},{32,0},{40,8},{48,16},{56,24},{64,96... | collective-permute-start | bytes 172040 | tf_op jit(solution)/shard_map/ppermute | solution.py:23
  44.5 0.4 collective-permute-done.16
  44.9 1.8 %collective-permute-done.15 = bf16[32,896]{1,0:T(8,128)(2,1)S(1)} collective-permute-done((bf16[32,896]{1,0:T(8,128)(2,1)S(1)}, bf16[32,896]{1,0:T(8,128)(2,1)S(1)}, u32[]{:S(2)}, u32[]{:S(2)}) %collective-permute-start.15) | collective-permute-done | bytes 57376 | tf_op jit(solution)/shard_map/ppermute | solution.py:23
  46.7 4.5 %collective-permute-start.17 = (bf16[4,32,896]{2,1,0:T(8,128)(2,1)S(1)}, bf16[4,32,896]{2,1,0:T(8,128)(2,1)S(1)}, u32[]{:S(2)}, u32[]{:S(2)}) collective-permute-start(bf16[4,32,896]{2,1,0:T(8,128)(2,1)S(1)} %pad_maximum_fusion.own_ref), channel_id=1, source_target_pairs={{0,8},{8,0},{16,24},{24,16},{32,40},{40,32},{48,56},{56,48},{64,72... | collective-permute-start | bytes 688136 | tf_op jit(solution)/shard_map/ppermute | solution.py:23
  51.2 0.2 shard_map.58.turned_ref
  51.4 0.9 %collective-permute-done.17.other_ref = bf16[4,32,896]{2,1,0:T(8,128)(2,1)S(1)} collective-permute-done((bf16[4,32,896]{2,1,0:T(8,128)(2,1)S(1)}, bf16[4,32,896]{2,1,0:T(8,128)(2,1)S(1)}, u32[]{:S(2)}, u32[]{:S(2)}) %collective-permute-start.17) | collective-permute-done | bytes 229408 | tf_op jit(solution)/shard_map/ppermute | solution.py:23
  52.3 3.3 %shard_map.59 = bf16[2,1280,896]{2,1,0:T(8,128)(2,1)} custom-call(s32[2]{0:T(128)S(1)} %pad_add_fusion.place_ref, bf16[4,32,896]{2,1,0:T(8,128)(2,1)S(1)} %pad_maximum_fusion.own_ref, bf16[4,32,896]{2,1,0:T(8,128)(2,1)S(1)} %collective-permute-done.17.other_ref, bf16[2,1280,256]{2,1,0:T(8,128)(2,1)S(1)} %shard_map.58.turned_ref), custom_call_target="tpu_custom_call" | custom-call | flops 1174405120 | bytes 6291456 | tf_op jit(solution)/shard_map/pallas_call | solution.py:233
  (23 shorter events, 0.3 us)
Async XLA Ops:
  0.0 11.2 %collective-permute-start = (bf16[2,16,1280]{2,1,0:T(8,128)(2,1)}, bf16[2,16,1280]{2,1,0:T(8,128)(2,1)S(1)}, u32[]{:S(2)}, u32[]{:S(2)}) collective-permute-start(bf16[2,16,1280]{2,1,0:T(8,128)(2,1)} %refs_3_.3), channel_id=1, source_target_pairs={{0,1},{1,0},{2,3},{3,2},{4,5},{5,4},{6,7},{7,6},{8,9},{9,8},{10,11... | collective-permute-start | bytes 245768 | tf_op jit(solution)/shard_map/ppermute | solution.py:27
  7.7 6.5 %collective-permute-start.1 = (bf16[2,16,1280]{2,1,0:T(8,128)(2,1)}, bf16[2,16,1280]{2,1,0:T(8,128)(2,1)S(1)}, u32[]{:S(2)}, u32[]{:S(2)}) collective-permute-start(bf16[2,16,1280]{2,1,0:T(8,128)(2,1)} %refs_3_.3), channel_id=1, source_target_pairs={{0,6},{1,7},{2,4},{3,5},{4,2},{5,3},{6,0},{7,1},{8,14},{9,15},{10,... | collective-permute-start | bytes 245768 | tf_op jit(solution)/shard_map/ppermute | solution.py:27
  10.2 6.6 %collective-permute-start.2 = (bf16[2,16,1280]{2,1,0:T(8,128)(2,1)}, bf16[2,16,1280]{2,1,0:T(8,128)(2,1)S(1)}, u32[]{:S(2)}, u32[]{:S(2)}) collective-permute-start(bf16[2,16,1280]{2,1,0:T(8,128)(2,1)} %refs_3_.3), channel_id=1, source_target_pairs={{0,4},{1,5},{2,6},{3,7},{4,0},{5,1},{6,2},{7,3},{8,12},{9,13},{10,... | collective-permute-start | bytes 245768 | tf_op jit(solution)/shard_map/ppermute | solution.py:27
  10.7 6.1 %collective-permute-start.3 = (bf16[2,16,1280]{2,1,0:T(8,128)(2,1)}, bf16[2,16,1280]{2,1,0:T(8,128)(2,1)S(1)}, u32[]{:S(2)}, u32[]{:S(2)}) collective-permute-start(bf16[2,16,1280]{2,1,0:T(8,128)(2,1)} %refs_3_.3), channel_id=1, source_target_pairs={{0,2},{1,3},{2,0},{3,1},{4,6},{5,7},{6,4},{7,5},{8,10},{9,11},{10,... | collective-permute-start | bytes 245768 | tf_op jit(solution)/shard_map/ppermute | solution.py:27
  11.0 3.5 %copy-start.1 = (f32[12,13,13]{2,1,0:T(8,128)S(1)}, f32[12,13,13]{2,1,0:T(8,128)}, u32[]{:S(2)}) copy-start(f32[12,13,13]{2,1,0:T(8,128)} %coupling_hbm.1) | copy-start | bytes 24340
  11.0 3.5 %copy-start.2 = (s32[12]{0:T(128)S(1)}, s32[12]{0:T(128)}, u32[]{:S(2)}) copy-start(s32[12]{0:T(128)} %offsets_hbm.1) | copy-start | bytes 148
  11.0 3.5 %copy-start.3 = (s32[12]{0:T(128)S(1)}, s32[12]{0:T(128)}, u32[]{:S(2)}) copy-start(s32[12]{0:T(128)} %counts_hbm.1) | copy-start | bytes 148
  11.1 7.7 %copy-start = (bf16[2,16,1280]{2,1,0:T(8,128)(2,1)S(1)}, bf16[2,16,1280]{2,1,0:T(8,128)(2,1)}, u32[]{:S(2)}) copy-start(bf16[2,16,1280]{2,1,0:T(8,128)(2,1)} %refs_3_.3) | copy-start | bytes 245764
  11.2 5.7 %collective-permute-start.4 = (bf16[2,16,1280]{2,1,0:T(8,128)(2,1)S(1)}, bf16[2,16,1280]{2,1,0:T(8,128)(2,1)S(1)}, u32[]{:S(2)}, u32[]{:S(2)}) collective-permute-start(bf16[2,16,1280]{2,1,0:T(8,128)(2,1)S(1)} %collective-permute-done.refs_7_), channel_id=1, source_target_pairs={{0,6},{1,7},{2,4},{3,5},{4,2},{5,3},{6,0},{7,1},{8,14},{9,15},{10,... | collective-permute-start | bytes 245768 | tf_op jit(solution)/shard_map/ppermute | solution.py:27
  13.7 5.1 %collective-permute-start.5 = (bf16[2,16,1280]{2,1,0:T(8,128)(2,1)S(1)}, bf16[2,16,1280]{2,1,0:T(8,128)(2,1)S(1)}, u32[]{:S(2)}, u32[]{:S(2)}) collective-permute-start(bf16[2,16,1280]{2,1,0:T(8,128)(2,1)S(1)} %collective-permute-done.refs_7_), channel_id=1, source_target_pairs={{0,4},{1,5},{2,6},{3,7},{4,0},{5,1},{6,2},{7,3},{8,12},{9,13},{10,... | collective-permute-start | bytes 245768 | tf_op jit(solution)/shard_map/ppermute | solution.py:27
  14.2 4.6 %collective-permute-start.6 = (bf16[2,16,1280]{2,1,0:T(8,128)(2,1)S(1)}, bf16[2,16,1280]{2,1,0:T(8,128)(2,1)S(1)}, u32[]{:S(2)}, u32[]{:S(2)}) collective-permute-start(bf16[2,16,1280]{2,1,0:T(8,128)(2,1)S(1)} %collective-permute-done.refs_7_), channel_id=1, source_target_pairs={{0,2},{1,3},{2,0},{3,1},{4,6},{5,7},{6,4},{7,5},{8,10},{9,11},{10,... | collective-permute-start | bytes 245768 | tf_op jit(solution)/shard_map/ppermute | solution.py:27
  21.3 4.5 %collective-permute-start.7 = (f32[4,32,896]{2,1,0:T(8,128)S(1)}, f32[4,32,896]{2,1,0:T(8,128)S(1)}, u32[]{:S(2)}, u32[]{:S(2)}) collective-permute-start(f32[4,32,896]{2,1,0:T(8,128)S(1)} %get-tuple-element.14), channel_id=1, source_target_pairs={{0,8},{8,0},{16,24},{24,16},{32,40},{40,32},{48,56},{56,48},{64,72... | collective-permute-start | bytes 1376264 | tf_op jit(solution)/shard_map/ppermute | solution.py:23
  25.8 4.0 %collective-permute-start.10 = (bf16[32,896]{1,0:T(8,128)(2,1)S(1)}, bf16[32,896]{1,0:T(8,128)(2,1)S(1)}, u32[]{:S(2)}, u32[]{:S(2)}) collective-permute-start(bf16[32,896]{1,0:T(8,128)(2,1)S(1)} %get-tuple-element.18), channel_id=1, source_target_pairs={{0,16},{8,24},{16,0},{24,8},{32,48},{40,56},{48,32},{56,40},{64,80... | collective-permute-start | bytes 172040 | tf_op jit(solution)/shard_map/ppermute | solution.py:23
  27.2 4.2 %collective-permute-start.8 = (bf16[32,896]{1,0:T(8,128)(2,1)S(1)}, bf16[32,896]{1,0:T(8,128)(2,1)S(1)}, u32[]{:S(2)}, u32[]{:S(2)}) collective-permute-start(bf16[32,896]{1,0:T(8,128)(2,1)S(1)} %get-tuple-element.17), channel_id=1, source_target_pairs={{0,48},{8,56},{16,32},{24,40},{32,16},{40,24},{48,0},{56,8},{64,11... | collective-permute-start | bytes 172040 | tf_op jit(solution)/shard_map/ppermute | solution.py:23
  29.1 4.5 %collective-permute-start.9 = (bf16[32,896]{1,0:T(8,128)(2,1)S(1)}, bf16[32,896]{1,0:T(8,128)(2,1)S(1)}, u32[]{:S(2)}, u32[]{:S(2)}) collective-permute-start(bf16[32,896]{1,0:T(8,128)(2,1)S(1)} %get-tuple-element.19), channel_id=1, source_target_pairs={{0,32},{8,40},{16,48},{24,56},{32,0},{40,8},{48,16},{56,24},{64,96... | collective-permute-start | bytes 172040 | tf_op jit(solution)/shard_map/ppermute | solution.py:23
  33.7 4.9 %collective-permute-start.11 = (bf16[32,896]{1,0:T(8,128)(2,1)S(1)}, bf16[32,896]{1,0:T(8,128)(2,1)S(1)}, u32[]{:S(2)}, u32[]{:S(2)}) collective-permute-start(bf16[32,896]{1,0:T(8,128)(2,1)S(1)} %fusion.3), channel_id=1, source_target_pairs={{0,192},{8,200},{16,208},{24,216},{32,224},{40,232},{48,240},{56,2... | collective-permute-start | bytes 172040 | tf_op jit(solution)/shard_map/ppermute | solution.py:23
  35.4 5.1 %collective-permute-start.12 = (bf16[32,896]{1,0:T(8,128)(2,1)S(1)}, bf16[32,896]{1,0:T(8,128)(2,1)S(1)}, u32[]{:S(2)}, u32[]{:S(2)}) collective-permute-start(bf16[32,896]{1,0:T(8,128)(2,1)S(1)} %fusion.3), channel_id=1, source_target_pairs={{0,128},{8,136},{16,144},{24,152},{32,160},{40,168},{48,176},{56,1... | collective-permute-start | bytes 172040 | tf_op jit(solution)/shard_map/ppermute | solution.py:23
  35.7 4.8 %collective-permute-start.13 = (bf16[32,896]{1,0:T(8,128)(2,1)S(1)}, bf16[32,896]{1,0:T(8,128)(2,1)S(1)}, u32[]{:S(2)}, u32[]{:S(2)}) collective-permute-start(bf16[32,896]{1,0:T(8,128)(2,1)S(1)} %fusion.3), channel_id=1, source_target_pairs={{0,64},{8,72},{16,80},{24,88},{32,96},{40,104},{48,112},{56,120},{... | collective-permute-start | bytes 172040 | tf_op jit(solution)/shard_map/ppermute | solution.py:23
  40.6 4.3 %collective-permute-start.16 = (bf16[32,896]{1,0:T(8,128)(2,1)S(1)}, bf16[32,896]{1,0:T(8,128)(2,1)S(1)}, u32[]{:S(2)}, u32[]{:S(2)}) collective-permute-start(bf16[32,896]{1,0:T(8,128)(2,1)S(1)} %add_convert_fusion), channel_id=1, source_target_pairs={{0,48},{8,56},{16,32},{24,40},{32,16},{40,24},{48,0},{56,8},{64,11... | collective-permute-start | bytes 172040 | tf_op jit(solution)/shard_map/ppermute | solution.py:23
  41.8 3.1 %collective-permute-start.14 = (bf16[32,896]{1,0:T(8,128)(2,1)S(1)}, bf16[32,896]{1,0:T(8,128)(2,1)S(1)}, u32[]{:S(2)}, u32[]{:S(2)}) collective-permute-start(bf16[32,896]{1,0:T(8,128)(2,1)S(1)} %add_convert_fusion), channel_id=1, source_target_pairs={{0,16},{8,24},{16,0},{24,8},{32,48},{40,56},{48,32},{56,40},{64,80... | collective-permute-start | bytes 172040 | tf_op jit(solution)/shard_map/ppermute | solution.py:23
  41.9 4.8 %collective-permute-start.15 = (bf16[32,896]{1,0:T(8,128)(2,1)S(1)}, bf16[32,896]{1,0:T(8,128)(2,1)S(1)}, u32[]{:S(2)}, u32[]{:S(2)}) collective-permute-start(bf16[32,896]{1,0:T(8,128)(2,1)S(1)} %add_convert_fusion), channel_id=1, source_target_pairs={{0,32},{8,40},{16,48},{24,56},{32,0},{40,8},{48,16},{56,24},{64,96... | collective-permute-start | bytes 172040 | tf_op jit(solution)/shard_map/ppermute | solution.py:23
  46.7 5.6 %collective-permute-start.17 = (bf16[4,32,896]{2,1,0:T(8,128)(2,1)S(1)}, bf16[4,32,896]{2,1,0:T(8,128)(2,1)S(1)}, u32[]{:S(2)}, u32[]{:S(2)}) collective-permute-start(bf16[4,32,896]{2,1,0:T(8,128)(2,1)S(1)} %pad_maximum_fusion.own_ref), channel_id=1, source_target_pairs={{0,8},{8,0},{16,24},{24,16},{32,40},{40,32},{48,56},{56,48},{64,72... | collective-permute-start | bytes 688136 | tf_op jit(solution)/shard_map/ppermute | solution.py:23

commit v3 on v2

--- a/solution.py
+++ b/solution.py
@@ -90,29 +90,36 @@
         return jnp.dot(pick_turned, part, preferred_element_type=F32).astype(BF16)
 
     high, low = (reorder(part) for part in two_terms(block))
-    left_ref[...] = jnp.concatenate([high, high, low], axis=1)
+    for h in range(2):
+        columns = slice(h * HALF, (h + 1) * HALF)
+        left_ref[h] = jnp.concatenate(
+            [high[:, columns], high[:, columns], low[:, columns]], axis=1
+        )
     copies[3].wait()
 
 
-def pick_kernel(band_ref, pick_ref):
+def pick_kernel(y_ref, band_ref, pick_ref):
+    def pick(place):
+        piece = place >> 4
+        piece = ((piece & 3) << 1) | (piece >> 2)
+        number = (jnp.bitwise_xor(piece, band_ref[0]) << 4) | (place & 15)
+        projector = lax.broadcasted_iota(jnp.int32, (NP, NP), 0)
+        return (projector == number).astype(F32)
+
     place = lax.broadcasted_iota(jnp.int32, (NP, NP), 1)
-    piece = place >> 4
-    piece = ((piece & 3) << 1) | (piece >> 2)
-    number = (jnp.bitwise_xor(piece, band_ref[0]) << 4) | (place & 15)
-    pick = (lax.broadcasted_iota(jnp.int32, (NP, NP), 0) == number).astype(F32)
-    pick_ref[0] = pick.astype(BF16)
-    pick_ref[1] = pick.T.astype(BF16)
-
-
-def gathered_order(band):
+    pick_ref[0] = pick(place).astype(BF16)
+    pick_ref[1] = pick(jnp.bitwise_xor(place, y_ref[0] << 5)).T.astype(BF16)
+
+
+def gathered_order(y, band):
     return pl.pallas_call(
         pick_kernel,
         out_shape=jax.ShapeDtypeStruct((2, NP, NP), BF16),
-        in_specs=[smem()],
+        in_specs=[smem(), smem()],
         out_specs=vmem(),
         compiler_params=params(8),
         cost_estimate=cost(4 * 10**9, 1),
-    )(band)
+    )(y, band)
 
 
 def ahead(pick, offsets, counts, coupling, waves):
@@ -120,7 +127,7 @@
     return pl.pallas_call(
         ahead_kernel,
         out_shape=(
-            jax.ShapeDtypeStruct((NP, 3 * NP), BF16),
+            jax.ShapeDtypeStruct((2, NP, 3 * HALF), BF16),
             jax.ShapeDtypeStruct(waves.shape, BF16),
         ),
         in_specs=[vmem()] + [hbm] * 4,
@@ -137,53 +144,77 @@
     )(pick, offsets, counts, coupling, waves)
 
 
-def fill_rows(pieces, rows_ref):
+def coupled_parts(h, pieces, left_ref, waves_ref, rows_ref):
+    for i, piece in enumerate(pieces):
+        at = (3 - i) * ROWS
+        rows_ref[pl.ds(at, ROWS), :] = piece[0]
+        rows_ref[pl.ds(HALF + at, ROWS), :] = piece[1]
+    rows = rows_ref[...]
+    first = jnp.dot(rows, waves_ref[0], preferred_element_type=F32)
+    second = jnp.dot(rows, waves_ref[1], preferred_element_type=F32)
+    left = left_ref[h]
+
+    def couple(part):
+        high, low = two_terms(part)
+        right = jnp.concatenate([high, low, high], axis=0)
+        return jnp.dot(left, right, preferred_element_type=F32)
+
+    return couple(first[:HALF] + second[HALF:]), couple(second[:HALF] - first[HALF:])
+
+
+def near_kernel(left_ref, waves_ref, *refs):
+    pieces, (out_ref, rows_ref) = refs[:4], refs[4:]
+    out_ref[0], out_ref[1] = coupled_parts(0, pieces, left_ref, waves_ref, rows_ref)
+
+
+def project_near(left, waves, pieces):
+    return pl.pallas_call(
+        near_kernel,
+        out_shape=jax.ShapeDtypeStruct((2, NP, NB_DEV), F32),
+        in_specs=[vmem()] * 6,
+        out_specs=vmem(),
+        scratch_shapes=[pltpu.VMEM((NP, NPW_DEV), BF16)],
+        compiler_params=params(16),
+        cost_estimate=cost(4 * NP * NPW_DEV * NB_DEV, 6 * MIB),
+    )(left, waves, *pieces)
+
+
+def far_kernel(core_ref, near_ref, left_ref, waves_ref, *refs):
+    pieces, (keep_ref, send_ref, rows_ref) = refs[:4], refs[4:]
+
+    def sums(out_refs):
+        parts = coupled_parts(1, pieces, left_ref, waves_ref, rows_ref)
+        for k in range(2):
+            out_refs[k][...] = parts[k] + near_ref[k]
+
+    @pl.when(core_ref[0] == 0)
+    def _():
+        sums((keep_ref, send_ref))
+
+    @pl.when(core_ref[0] == 1)
+    def _():
+        sums((send_ref, keep_ref))
+
+
+def project_far(core, near, left, waves, pieces):
+    half = jax.ShapeDtypeStruct((NP, NB_DEV), F32)
+    return pl.pallas_call(
+        far_kernel,
+        out_shape=(half, half),
+        in_specs=[smem()] + [vmem()] * 7,
+        out_specs=(vmem(), vmem()),
+        scratch_shapes=[pltpu.VMEM((NP, NPW_DEV), BF16)],
+        compiler_params=params(16),
+        cost_estimate=cost(4 * NP * NPW_DEV * NB_DEV, 6 * MIB),
+    )(core, near, left, waves, *pieces)
+
+
+def turn_kernel(*refs):
+    pieces, (out_ref, rows_ref) = refs[:8], refs[8:]
     for i, piece in enumerate(pieces):
         at = (i // 4) * HALF + (3 - i % 4) * ROWS
         for k in range(2):
             rows_ref[pl.ds(k * NP + at, ROWS), :] = piece[k]
-
-
-def project_kernel(place_ref, left_ref, waves_ref, *refs):
-    pieces, (keep_ref, send_ref, rows_ref) = refs[:8], refs[8:]
-    core, y = place_ref[0], place_ref[1]
-    fill_rows(pieces, rows_ref)
-    rows = rows_ref[...]
-    first = jnp.dot(rows, waves_ref[0], preferred_element_type=F32)
-    second = jnp.dot(rows, waves_ref[1], preferred_element_type=F32)
-    left = left_ref[...]
-
-    def couple(part):
-        high, low = two_terms(part)
-        right = jnp.concatenate([high, low, high], axis=0)
-        return jnp.dot(left, right, preferred_element_type=F32)
-
-    real = couple(first[:NP] + second[NP:])
-    imag = couple(second[:NP] - first[NP:])
-    keep = jnp.where(core == 0, real, imag)
-    send = jnp.where(core == 0, imag, real)
-    for t in range(4):
-        at = jnp.bitwise_xor(y, t)
-        keep_ref[at] = keep[t * CHUNK : (t + 1) * CHUNK]
-        send_ref[at] = send[t * CHUNK : (t + 1) * CHUNK]
-
-
-def project(place, left, waves, pieces):
-    half = jax.ShapeDtypeStruct((4, CHUNK, NB_DEV), F32)
-    return pl.pallas_call(
-        project_kernel,
-        out_shape=(half, half),
-        in_specs=[smem()] + [vmem()] * 10,
-        out_specs=(vmem(), vmem()),
-        scratch_shapes=[pltpu.VMEM((2 * NP, NPW_DEV), BF16)],
-        compiler_params=params(16),
-        cost_estimate=cost(8 * NP * NPW_DEV * NB_DEV, 6 * MIB),
-    )(place, left, waves, *pieces)
-
-
-def turn_kernel(*refs):
-    pieces, (out_ref, rows_ref) = refs[:8], refs[8:]
-    fill_rows(pieces, rows_ref)
     turned = rows_ref[...].T
     first, second = turned[:, :NP], turned[:, NP:]
     out_ref[0, :, :NP] = first
@@ -204,8 +235,10 @@
     )(*pieces)
 
 
-def spread_kernel(place_ref, own_ref, other_ref, turned_ref, out_ref, right_ref, result_ref, sem):
-    core, y = place_ref[0], place_ref[1]
+def spread_kernel(
+    core_ref, y_ref, own_ref, other_ref, turned_ref, out_ref, right_ref, result_ref, sem
+):
+    core, y = core_ref[0], y_ref[0]
     for s in range(4):
         at = jnp.bitwise_xor(y, s) * CHUNK
         own_at = pl.multiple_of(core * NP + at, CHUNK)
@@ -229,11 +262,11 @@
         copy.wait()
 
 
-def spread_back(place, own, other, turned):
+def spread_back(core, y, own, other, turned):
     return pl.pallas_call(
         spread_kernel,
         out_shape=jax.ShapeDtypeStruct((2, NPW_DEV, NB_DEV), BF16),
-        in_specs=[smem()] + [vmem()] * 3,
+        in_specs=[smem(), smem()] + [vmem()] * 3,
         out_specs=pl.BlockSpec(memory_space=pltpu.HBM),
         scratch_shapes=[
             pltpu.VMEM((2 * NP, NB_DEV), BF16),
@@ -242,22 +275,23 @@
         ],
         compiler_params=params(16),
         cost_estimate=cost(8 * NP * NPW_DEV * NB_DEV, 6 * MIB),
-    )(place, own, other, turned)
+    )(core, y, own, other, turned)
 
 
 def shards(waves, projectors, coupling, offsets, counts):
     pw, band = lax.axis_index("pw"), lax.axis_index("band")
-    place = jnp.stack([pw & 1, (pw >> 1) & 3])
+    core, y, band = (i.reshape(1) for i in (pw & 1, (pw >> 1) & 3, band))
 
     distant = over_band(projectors, 1)
     near = [over_band(projectors, bits) for bits in (6, 4, 2)] + [projectors]
     far = [over_band(distant, bits) for bits in (6, 4, 2)] + [distant]
-    pick = gathered_order(band.reshape(1))
+    pick = gathered_order(y, band)
     pick, _ = lax.optimization_barrier((pick, distant))
     left, waves = ahead(pick, offsets, counts, coupling, waves)
-    keep, send = project(place, left, waves, near + far)
+    sums = project_near(left, waves, near)
+    keep, send = project_far(core, sums, left, waves, far)
     turned = turn(near + far)
-    total = keep + over_pw(send, 1)
+    total = (keep + over_pw(send, 1)).reshape(4, CHUNK, NB_DEV)
 
     sums = total[0]
     for arrived in [over_pw(total[s].astype(BF16), 2 * s) for s in (3, 2, 1)]:
@@ -269,7 +303,7 @@
     chunk = {s: over_pw(mine, 2 * s) for s in (3, 2, 1)}
     own = jnp.stack([mine, chunk[1], chunk[2], chunk[3]])
     other = over_pw(own, 1)
-    return spread_back(place, own, other, turned)
+    return spread_back(core, y, own, other, turned)
 
 
 def solution(mesh):

time: 55.7 us -> 54.4 us (0.977)
  Pallas kernels: 8.39 us -> 7.7 us
  waiting for transfers between devices: 13.4 us -> 12.8 us
    ppermute x7, waiting for transfers between devices: 1.92 us -> 0.74 us  [over_band(): return lax.ppermute(x, 'band', [(i, i ^ bits) for i in range(8)])]
    pallas_call x2 -> x3, Pallas kernels: 4.8 us -> 4.66 us  [the longest x1 2.34 us: ahead(): pl.pallas_call(ahead_kernel, out_shape=(jax.ShapeDtypeStruct((2, NP, 3 *...]
  transfers between devices with their start and end apart: 18 -> 18, of which waited for: 9 -> 9; matrix products, arithmetic and copies ran while one was open for 0% -> 0% of each run, Pallas kernels for 5% -> 7%
where the time goes in v3:
time: 54.4 us; the launch traced here: 54.3 us
  starting transfers between devices  33.3 us (61%)
  waiting for transfers between devices  12.8 us (24%)
  Pallas kernels  7.7 us (14%)
    ppermute x11, starting transfers between devices, over_pw(): return lax.ppermute(x, 'pw', [(i, i ^ bits) for i in range(32)])  19 us
    ppermute x7, starting transfers between devices, over_band(): return lax.ppermute(x, 'band', [(i, i ^ bits) for i in range(8)])  14.3 us
    ppermute x11, waiting for transfers between devices, over_pw(): return lax.ppermute(x, 'pw', [(i, i ^ bits) for i in range(32)])  12.1 us
    pallas_call x1, Pallas kernels, spread_back(): pl.pallas_call(spread_kernel, out_shape=jax.ShapeDtypeStruct((2, NPW_DEV,...  2.72 us
    pallas_call x1, Pallas kernels, ahead(): pl.pallas_call(ahead_kernel, out_shape=(jax.ShapeDtypeStruct((2, NP, 3 *...  2.34 us
    pallas_call x1, Pallas kernels, project_near(): pl.pallas_call(near_kernel, out_shape=jax.ShapeDtypeStruct((2, NP, NB_DEV...  1.17 us
    pallas_call x1, Pallas kernels, project_far(): pl.pallas_call(far_kernel, out_shape=(half, half), in_specs=[smem()] + [v...  1.14 us
  transfers between devices with their start and end apart: 18, of which 9 were waited for; matrix products, arithmetic and copies ran while one was open for 0% of the time, Pallas kernels for 7%

profile of v3, /device:TPU:1, one launch (start us, length us, event | category | flops | bytes accessed | tf_op | source)
XLA Modules:
  0.0 54.3 jit_solution(15649546991138198107)
XLA Ops:
  0.0 7.7 %collective-permute-start = (bf16[2,16,1280]{2,1,0:T(8,128)(2,1)}, bf16[2,16,1280]{2,1,0:T(8,128)(2,1)S(1)}, u32[]{:S(2)}, u32[]{:S(2)}) collective-permute-start(bf16[2,16,1280]{2,1,0:T(8,128)(2,1)} %refs_3_.3), channel_id=1, source_target_pairs={{0,1},{1,0},{2,3},{3,2},{4,5},{5,4},{6,7},{7,6},{8,9},{9,8},{10,11... | collective-permute-start | bytes 245768 | tf_op jit(solution)/shard_map/ppermute | solution.py:27
  7.7 2.5 %collective-permute-start.1 = (bf16[2,16,1280]{2,1,0:T(8,128)(2,1)}, bf16[2,16,1280]{2,1,0:T(8,128)(2,1)S(1)}, u32[]{:S(2)}, u32[]{:S(2)}) collective-permute-start(bf16[2,16,1280]{2,1,0:T(8,128)(2,1)} %refs_3_.3), channel_id=1, source_target_pairs={{0,6},{1,7},{2,4},{3,5},{4,2},{5,3},{6,0},{7,1},{8,14},{9,15},{10,... | collective-permute-start | bytes 245768 | tf_op jit(solution)/shard_map/ppermute | solution.py:27
  10.2 0.5 collective-permute-start.2
  10.7 0.3 collective-permute-start.3
  11.1 2.6 %collective-permute-start.4 = (bf16[2,16,1280]{2,1,0:T(8,128)(2,1)S(1)}, bf16[2,16,1280]{2,1,0:T(8,128)(2,1)S(1)}, u32[]{:S(2)}, u32[]{:S(2)}) collective-permute-start(bf16[2,16,1280]{2,1,0:T(8,128)(2,1)S(1)} %collective-permute-done.refs_3_.refs_7_), channel_id=1, source_target_pairs={{0,6},{1,7},{2,4},{3,5},{4,2},{5,3},{6,0},{7,1},{8,14},{9,15},{10,... | collective-permute-start | bytes 245768 | tf_op jit(solution)/shard_map/ppermute | solution.py:27
  13.7 0.5 collective-permute-start.5
  14.2 0.3 collective-permute-start.6
  14.5 2.3 %shard_map.56 = (bf16[2,128,192]{2,1,0:T(8,128)(2,1)S(1)}, bf16[2,1280,896]{2,1,0:T(8,128)(2,1)S(1)}) custom-call(bf16[2,128,128]{2,1,0:T(8,128)(2,1)S(1)} %shard_map.55.pick_ref, s32[12]{0:T(128)S(1)} %copy-done.2, s32[12]{0:T(128)S(1)} %copy-done.3, f32[12,13,13]{2,1,0:T(8,128)S(1)} %copy-done.1, bf16[2,1280,896]{2,1,0:T(8,128)(2,1)} %waves_hbm.1), custom_call_target="tpu_custom_call" | custom-call | flops 2000000000 | bytes 8388608 | tf_op jit(solution)/shard_map/pallas_call | solution.py:127
  16.9 1.2 %shard_map.57.near_ref = f32[2,128,896]{2,1,0:T(8,128)S(1)} custom-call(bf16[2,128,192]{2,1,0:T(8,128)(2,1)S(1)} %get-tuple-element.11.left_ref, bf16[2,1280,896]{2,1,0:T(8,128)(2,1)S(1)} %get-tuple-element.12.waves_ref, bf16[2,16,1280]{2,1,0:T(8,128)(2,1)S(1)} %collective-permute-done.1.refs_0_, bf16[2,16,1280]{2,1,0:T(8,128)(2,1)S(1)} %collective-permute-done.2.refs_1_, ...), custom_call_target="tpu_custom_call" | custom-call | flops 587202560 | bytes 6291456 | tf_op jit(solution)/shard_map/pallas_call | solution.py:171
  18.1 0.7 %collective-permute-done.5.refs_1_.refs_5_ = bf16[2,16,1280]{2,1,0:T(8,128)(2,1)S(1)} collective-permute-done((bf16[2,16,1280]{2,1,0:T(8,128)(2,1)S(1)}, bf16[2,16,1280]{2,1,0:T(8,128)(2,1)S(1)}, u32[]{:S(2)}, u32[]{:S(2)}) %collective-permute-start.5) | collective-permute-done | bytes 81952 | tf_op jit(solution)/shard_map/ppermute | solution.py:27
  18.8 1.1 %shard_map.58 = (f32[128,896]{1,0:T(8,128)S(1)}, f32[128,896]{1,0:T(8,128)S(1)}) custom-call(s32[1]{0:T(128)} %bitcast.core_ref, f32[2,128,896]{2,1,0:T(8,128)S(1)} %shard_map.57.near_ref, bf16[2,128,192]{2,1,0:T(8,128)(2,1)S(1)} %get-tuple-element.11.left_ref, bf16[2,1280,896]{2,1,0:T(8,128)(2,1)S(1)} %get-tuple-element.12.waves_ref, ...), custom_call_target="tpu_custom_call" | custom-call | flops 587202560 | bytes 6291456 | tf_op jit(solution)/shard_map/pallas_call | solution.py:201
  19.9 3.0 %collective-permute-start.7 = (f32[128,896]{1,0:T(8,128)S(1)}, f32[128,896]{1,0:T(8,128)S(1)}, u32[]{:S(2)}, u32[]{:S(2)}) collective-permute-start(f32[128,896]{1,0:T(8,128)S(1)} %get-tuple-element.14), channel_id=1, source_target_pairs={{0,8},{8,0},{16,24},{24,16},{32,40},{40,32},{48,56},{56,48},{64,72... | collective-permute-start | bytes 1376264 | tf_op jit(solution)/shard_map/ppermute | solution.py:23
  23.0 1.4 %collective-permute-done.7 = f32[128,896]{1,0:T(8,128)S(1)} collective-permute-done((f32[128,896]{1,0:T(8,128)S(1)}, f32[128,896]{1,0:T(8,128)S(1)}, u32[]{:S(2)}, u32[]{:S(2)}) %collective-permute-start.7) | collective-permute-done | bytes 458784 | tf_op jit(solution)/shard_map/ppermute | solution.py:23
  24.5 1.4 %collective-permute-start.10 = (bf16[32,896]{1,0:T(8,128)(2,1)S(1)}, bf16[32,896]{1,0:T(8,128)(2,1)S(1)}, u32[]{:S(2)}, u32[]{:S(2)}) collective-permute-start(bf16[32,896]{1,0:T(8,128)(2,1)S(1)} %get-tuple-element.18), channel_id=1, source_target_pairs={{0,16},{8,24},{16,0},{24,8},{32,48},{40,56},{48,32},{56,40},{64,80... | collective-permute-start | bytes 172040 | tf_op jit(solution)/shard_map/ppermute | solution.py:23
  25.9 1.9 %collective-permute-start.8 = (bf16[32,896]{1,0:T(8,128)(2,1)S(1)}, bf16[32,896]{1,0:T(8,128)(2,1)S(1)}, u32[]{:S(2)}, u32[]{:S(2)}) collective-permute-start(bf16[32,896]{1,0:T(8,128)(2,1)S(1)} %get-tuple-element.17), channel_id=1, source_target_pairs={{0,48},{8,56},{16,32},{24,40},{32,16},{40,24},{48,0},{56,8},{64,11... | collective-permute-start | bytes 172040 | tf_op jit(solution)/shard_map/ppermute | solution.py:23
  27.8 0.7 %collective-permute-start.9 = (bf16[32,896]{1,0:T(8,128)(2,1)S(1)}, bf16[32,896]{1,0:T(8,128)(2,1)S(1)}, u32[]{:S(2)}, u32[]{:S(2)}) collective-permute-start(bf16[32,896]{1,0:T(8,128)(2,1)S(1)} %get-tuple-element.19), channel_id=1, source_target_pairs={{0,32},{8,40},{16,48},{24,56},{32,0},{40,8},{48,16},{56,24},{64,96... | collective-permute-start | bytes 172040 | tf_op jit(solution)/shard_map/ppermute | solution.py:23
  28.5 1.6 %collective-permute-done.8 = bf16[32,896]{1,0:T(8,128)(2,1)S(1)} collective-permute-done((bf16[32,896]{1,0:T(8,128)(2,1)S(1)}, bf16[32,896]{1,0:T(8,128)(2,1)S(1)}, u32[]{:S(2)}, u32[]{:S(2)}) %collective-permute-start.8) | collective-permute-done | bytes 57376 | tf_op jit(solution)/shard_map/ppermute | solution.py:23
  30.1 2.2 %collective-permute-done.9 = bf16[32,896]{1,0:T(8,128)(2,1)S(1)} collective-permute-done((bf16[32,896]{1,0:T(8,128)(2,1)S(1)}, bf16[32,896]{1,0:T(8,128)(2,1)S(1)}, u32[]{:S(2)}, u32[]{:S(2)}) %collective-permute-start.9) | collective-permute-done | bytes 57376 | tf_op jit(solution)/shard_map/ppermute | solution.py:23
  32.4 1.7 %collective-permute-start.11 = (bf16[32,896]{1,0:T(8,128)(2,1)S(1)}, bf16[32,896]{1,0:T(8,128)(2,1)S(1)}, u32[]{:S(2)}, u32[]{:S(2)}) collective-permute-start(bf16[32,896]{1,0:T(8,128)(2,1)S(1)} %fusion.2), channel_id=1, source_target_pairs={{0,192},{8,200},{16,208},{24,216},{32,224},{40,232},{48,240},{56,2... | collective-permute-start | bytes 172040 | tf_op jit(solution)/shard_map/ppermute | solution.py:23
  34.1 0.3 collective-permute-start.12
  34.4 1.6 %collective-permute-start.13 = (bf16[32,896]{1,0:T(8,128)(2,1)S(1)}, bf16[32,896]{1,0:T(8,128)(2,1)S(1)}, u32[]{:S(2)}, u32[]{:S(2)}) collective-permute-start(bf16[32,896]{1,0:T(8,128)(2,1)S(1)} %fusion.2), channel_id=1, source_target_pairs={{0,64},{8,72},{16,80},{24,88},{32,96},{40,104},{48,112},{56,120},{... | collective-permute-start | bytes 172040 | tf_op jit(solution)/shard_map/ppermute | solution.py:23
  36.0 1.3 %collective-permute-done.11 = bf16[32,896]{1,0:T(8,128)(2,1)S(1)} collective-permute-done((bf16[32,896]{1,0:T(8,128)(2,1)S(1)}, bf16[32,896]{1,0:T(8,128)(2,1)S(1)}, u32[]{:S(2)}, u32[]{:S(2)}) %collective-permute-start.11) | collective-permute-done | bytes 57376 | tf_op jit(solution)/shard_map/ppermute | solution.py:23
  37.3 1.9 %collective-permute-done.12 = bf16[32,896]{1,0:T(8,128)(2,1)S(1)} collective-permute-done((bf16[32,896]{1,0:T(8,128)(2,1)S(1)}, bf16[32,896]{1,0:T(8,128)(2,1)S(1)}, u32[]{:S(2)}, u32[]{:S(2)}) %collective-permute-start.12) | collective-permute-done | bytes 57376 | tf_op jit(solution)/shard_map/ppermute | solution.py:23
  39.3 0.5 collective-permute-start.14
  39.8 1.9 %collective-permute-start.15 = (bf16[32,896]{1,0:T(8,128)(2,1)S(1)}, bf16[32,896]{1,0:T(8,128)(2,1)S(1)}, u32[]{:S(2)}, u32[]{:S(2)}) collective-permute-start(bf16[32,896]{1,0:T(8,128)(2,1)S(1)} %add_convert_fusion), channel_id=1, source_target_pairs={{0,32},{8,40},{16,48},{24,56},{32,0},{40,8},{48,16},{56,24},{64,96... | collective-permute-start | bytes 172040 | tf_op jit(solution)/shard_map/ppermute | solution.py:23
  41.7 1.5 %collective-permute-start.16 = (bf16[32,896]{1,0:T(8,128)(2,1)S(1)}, bf16[32,896]{1,0:T(8,128)(2,1)S(1)}, u32[]{:S(2)}, u32[]{:S(2)}) collective-permute-start(bf16[32,896]{1,0:T(8,128)(2,1)S(1)} %add_convert_fusion), channel_id=1, source_target_pairs={{0,48},{8,56},{16,32},{24,40},{32,16},{40,24},{48,0},{56,8},{64,11... | collective-permute-start | bytes 172040 | tf_op jit(solution)/shard_map/ppermute | solution.py:23
  43.2 1.1 %collective-permute-done.15 = bf16[32,896]{1,0:T(8,128)(2,1)S(1)} collective-permute-done((bf16[32,896]{1,0:T(8,128)(2,1)S(1)}, bf16[32,896]{1,0:T(8,128)(2,1)S(1)}, u32[]{:S(2)}, u32[]{:S(2)}) %collective-permute-start.15) | collective-permute-done | bytes 57376 | tf_op jit(solution)/shard_map/ppermute | solution.py:23
  44.3 1.6 %collective-permute-done.16 = bf16[32,896]{1,0:T(8,128)(2,1)S(1)} collective-permute-done((bf16[32,896]{1,0:T(8,128)(2,1)S(1)}, bf16[32,896]{1,0:T(8,128)(2,1)S(1)}, u32[]{:S(2)}, u32[]{:S(2)}) %collective-permute-start.16) | collective-permute-done | bytes 57376 | tf_op jit(solution)/shard_map/ppermute | solution.py:23
  46.0 4.4 %collective-permute-start.17 = (bf16[4,32,896]{2,1,0:T(8,128)(2,1)S(1)}, bf16[4,32,896]{2,1,0:T(8,128)(2,1)S(1)}, u32[]{:S(2)}, u32[]{:S(2)}) collective-permute-start(bf16[4,32,896]{2,1,0:T(8,128)(2,1)S(1)} %pad_maximum_fusion.own_ref), channel_id=1, source_target_pairs={{0,8},{8,0},{16,24},{24,16},{32,40},{40,32},{48,56},{56,48},{64,72... | collective-permute-start | bytes 688136 | tf_op jit(solution)/shard_map/ppermute | solution.py:23
  50.3 0.2 shard_map.59.turned_ref
  50.6 0.9 %collective-permute-done.17.other_ref = bf16[4,32,896]{2,1,0:T(8,128)(2,1)S(1)} collective-permute-done((bf16[4,32,896]{2,1,0:T(8,128)(2,1)S(1)}, bf16[4,32,896]{2,1,0:T(8,128)(2,1)S(1)}, u32[]{:S(2)}, u32[]{:S(2)}) %collective-permute-start.17) | collective-permute-done | bytes 229408 | tf_op jit(solution)/shard_map/ppermute | solution.py:23
  51.5 2.7 %shard_map.60 = bf16[2,1280,896]{2,1,0:T(8,128)(2,1)} custom-call(s32[1]{0:T(128)} %bitcast.core_ref, s32[1]{0:T(128)} %bitcast.1.y_ref, bf16[4,32,896]{2,1,0:T(8,128)(2,1)S(1)} %pad_maximum_fusion.own_ref, bf16[4,32,896]{2,1,0:T(8,128)(2,1)S(1)} %collective-permute-done.17.other_ref, bf16[2,1280,256]{2,1,0:T(8,128)(2,1)S(1)} %shard_map.59.turned_ref), custom_call_target="tpu_custom_call" | custom-call | flops 1174405120 | bytes 6291456 | tf_op jit(solution)/shard_map/pallas_call | solution.py:266
  (23 shorter events, 0.4 us)
Async XLA Ops:
  0.0 11.1 %collective-permute-start = (bf16[2,16,1280]{2,1,0:T(8,128)(2,1)}, bf16[2,16,1280]{2,1,0:T(8,128)(2,1)S(1)}, u32[]{:S(2)}, u32[]{:S(2)}) collective-permute-start(bf16[2,16,1280]{2,1,0:T(8,128)(2,1)} %refs_3_.3), channel_id=1, source_target_pairs={{0,1},{1,0},{2,3},{3,2},{4,5},{5,4},{6,7},{7,6},{8,9},{9,8},{10,11... | collective-permute-start | bytes 245768 | tf_op jit(solution)/shard_map/ppermute | solution.py:27
  7.7 6.5 %collective-permute-start.1 = (bf16[2,16,1280]{2,1,0:T(8,128)(2,1)}, bf16[2,16,1280]{2,1,0:T(8,128)(2,1)S(1)}, u32[]{:S(2)}, u32[]{:S(2)}) collective-permute-start(bf16[2,16,1280]{2,1,0:T(8,128)(2,1)} %refs_3_.3), channel_id=1, source_target_pairs={{0,6},{1,7},{2,4},{3,5},{4,2},{5,3},{6,0},{7,1},{8,14},{9,15},{10,... | collective-permute-start | bytes 245768 | tf_op jit(solution)/shard_map/ppermute | solution.py:27
  10.2 6.6 %collective-permute-start.2 = (bf16[2,16,1280]{2,1,0:T(8,128)(2,1)}, bf16[2,16,1280]{2,1,0:T(8,128)(2,1)S(1)}, u32[]{:S(2)}, u32[]{:S(2)}) collective-permute-start(bf16[2,16,1280]{2,1,0:T(8,128)(2,1)} %refs_3_.3), channel_id=1, source_target_pairs={{0,4},{1,5},{2,6},{3,7},{4,0},{5,1},{6,2},{7,3},{8,12},{9,13},{10,... | collective-permute-start | bytes 245768 | tf_op jit(solution)/shard_map/ppermute | solution.py:27
  10.7 6.1 %collective-permute-start.3 = (bf16[2,16,1280]{2,1,0:T(8,128)(2,1)}, bf16[2,16,1280]{2,1,0:T(8,128)(2,1)S(1)}, u32[]{:S(2)}, u32[]{:S(2)}) collective-permute-start(bf16[2,16,1280]{2,1,0:T(8,128)(2,1)} %refs_3_.3), channel_id=1, source_target_pairs={{0,2},{1,3},{2,0},{3,1},{4,6},{5,7},{6,4},{7,5},{8,10},{9,11},{10,... | collective-permute-start | bytes 245768 | tf_op jit(solution)/shard_map/ppermute | solution.py:27
  11.0 3.5 %copy-start.1 = (f32[12,13,13]{2,1,0:T(8,128)S(1)}, f32[12,13,13]{2,1,0:T(8,128)}, u32[]{:S(2)}) copy-start(f32[12,13,13]{2,1,0:T(8,128)} %coupling_hbm.1) | copy-start | bytes 24340
  11.0 3.5 %copy-start.2 = (s32[12]{0:T(128)S(1)}, s32[12]{0:T(128)}, u32[]{:S(2)}) copy-start(s32[12]{0:T(128)} %offsets_hbm.1) | copy-start | bytes 148
  11.0 3.5 %copy-start.3 = (s32[12]{0:T(128)S(1)}, s32[12]{0:T(128)}, u32[]{:S(2)}) copy-start(s32[12]{0:T(128)} %counts_hbm.1) | copy-start | bytes 148
  11.1 5.8 %copy-start = (bf16[2,16,1280]{2,1,0:T(8,128)(2,1)S(1)}, bf16[2,16,1280]{2,1,0:T(8,128)(2,1)}, u32[]{:S(2)}) copy-start(bf16[2,16,1280]{2,1,0:T(8,128)(2,1)} %refs_3_.3) | copy-start | bytes 245764
  11.1 6.9 %collective-permute-start.4 = (bf16[2,16,1280]{2,1,0:T(8,128)(2,1)S(1)}, bf16[2,16,1280]{2,1,0:T(8,128)(2,1)S(1)}, u32[]{:S(2)}, u32[]{:S(2)}) collective-permute-start(bf16[2,16,1280]{2,1,0:T(8,128)(2,1)S(1)} %collective-permute-done.refs_3_.refs_7_), channel_id=1, source_target_pairs={{0,6},{1,7},{2,4},{3,5},{4,2},{5,3},{6,0},{7,1},{8,14},{9,15},{10,... | collective-permute-start | bytes 245768 | tf_op jit(solution)/shard_map/ppermute | solution.py:27
  13.7 5.1 %collective-permute-start.5 = (bf16[2,16,1280]{2,1,0:T(8,128)(2,1)S(1)}, bf16[2,16,1280]{2,1,0:T(8,128)(2,1)S(1)}, u32[]{:S(2)}, u32[]{:S(2)}) collective-permute-start(bf16[2,16,1280]{2,1,0:T(8,128)(2,1)S(1)} %collective-permute-done.refs_3_.refs_7_), channel_id=1, source_target_pairs={{0,4},{1,5},{2,6},{3,7},{4,0},{5,1},{6,2},{7,3},{8,12},{9,13},{10,... | collective-permute-start | bytes 245768 | tf_op jit(solution)/shard_map/ppermute | solution.py:27
  14.2 4.6 %collective-permute-start.6 = (bf16[2,16,1280]{2,1,0:T(8,128)(2,1)S(1)}, bf16[2,16,1280]{2,1,0:T(8,128)(2,1)S(1)}, u32[]{:S(2)}, u32[]{:S(2)}) collective-permute-start(bf16[2,16,1280]{2,1,0:T(8,128)(2,1)S(1)} %collective-permute-done.refs_3_.refs_7_), channel_id=1, source_target_pairs={{0,2},{1,3},{2,0},{3,1},{4,6},{5,7},{6,4},{7,5},{8,10},{9,11},{10,... | collective-permute-start | bytes 245768 | tf_op jit(solution)/shard_map/ppermute | solution.py:27
  19.9 4.5 %collective-permute-start.7 = (f32[128,896]{1,0:T(8,128)S(1)}, f32[128,896]{1,0:T(8,128)S(1)}, u32[]{:S(2)}, u32[]{:S(2)}) collective-permute-start(f32[128,896]{1,0:T(8,128)S(1)} %get-tuple-element.14), channel_id=1, source_target_pairs={{0,8},{8,0},{16,24},{24,16},{32,40},{40,32},{48,56},{56,48},{64,72... | collective-permute-start | bytes 1376264 | tf_op jit(solution)/shard_map/ppermute | solution.py:23
  24.5 4.0 %collective-permute-start.10 = (bf16[32,896]{1,0:T(8,128)(2,1)S(1)}, bf16[32,896]{1,0:T(8,128)(2,1)S(1)}, u32[]{:S(2)}, u32[]{:S(2)}) collective-permute-start(bf16[32,896]{1,0:T(8,128)(2,1)S(1)} %get-tuple-element.18), channel_id=1, source_target_pairs={{0,16},{8,24},{16,0},{24,8},{32,48},{40,56},{48,32},{56,40},{64,80... | collective-permute-start | bytes 172040 | tf_op jit(solution)/shard_map/ppermute | solution.py:23
  25.9 4.2 %collective-permute-start.8 = (bf16[32,896]{1,0:T(8,128)(2,1)S(1)}, bf16[32,896]{1,0:T(8,128)(2,1)S(1)}, u32[]{:S(2)}, u32[]{:S(2)}) collective-permute-start(bf16[32,896]{1,0:T(8,128)(2,1)S(1)} %get-tuple-element.17), channel_id=1, source_target_pairs={{0,48},{8,56},{16,32},{24,40},{32,16},{40,24},{48,0},{56,8},{64,11... | collective-permute-start | bytes 172040 | tf_op jit(solution)/shard_map/ppermute | solution.py:23
  27.8 4.5 %collective-permute-start.9 = (bf16[32,896]{1,0:T(8,128)(2,1)S(1)}, bf16[32,896]{1,0:T(8,128)(2,1)S(1)}, u32[]{:S(2)}, u32[]{:S(2)}) collective-permute-start(bf16[32,896]{1,0:T(8,128)(2,1)S(1)} %get-tuple-element.19), channel_id=1, source_target_pairs={{0,32},{8,40},{16,48},{24,56},{32,0},{40,8},{48,16},{56,24},{64,96... | collective-permute-start | bytes 172040 | tf_op jit(solution)/shard_map/ppermute | solution.py:23
  32.4 4.9 %collective-permute-start.11 = (bf16[32,896]{1,0:T(8,128)(2,1)S(1)}, bf16[32,896]{1,0:T(8,128)(2,1)S(1)}, u32[]{:S(2)}, u32[]{:S(2)}) collective-permute-start(bf16[32,896]{1,0:T(8,128)(2,1)S(1)} %fusion.2), channel_id=1, source_target_pairs={{0,192},{8,200},{16,208},{24,216},{32,224},{40,232},{48,240},{56,2... | collective-permute-start | bytes 172040 | tf_op jit(solution)/shard_map/ppermute | solution.py:23
  34.1 5.1 %collective-permute-start.12 = (bf16[32,896]{1,0:T(8,128)(2,1)S(1)}, bf16[32,896]{1,0:T(8,128)(2,1)S(1)}, u32[]{:S(2)}, u32[]{:S(2)}) collective-permute-start(bf16[32,896]{1,0:T(8,128)(2,1)S(1)} %fusion.2), channel_id=1, source_target_pairs={{0,128},{8,136},{16,144},{24,152},{32,160},{40,168},{48,176},{56,1... | collective-permute-start | bytes 172040 | tf_op jit(solution)/shard_map/ppermute | solution.py:23
  34.4 4.8 %collective-permute-start.13 = (bf16[32,896]{1,0:T(8,128)(2,1)S(1)}, bf16[32,896]{1,0:T(8,128)(2,1)S(1)}, u32[]{:S(2)}, u32[]{:S(2)}) collective-permute-start(bf16[32,896]{1,0:T(8,128)(2,1)S(1)} %fusion.2), channel_id=1, source_target_pairs={{0,64},{8,72},{16,80},{24,88},{32,96},{40,104},{48,112},{56,120},{... | collective-permute-start | bytes 172040 | tf_op jit(solution)/shard_map/ppermute | solution.py:23
  39.3 4.0 %collective-permute-start.14 = (bf16[32,896]{1,0:T(8,128)(2,1)S(1)}, bf16[32,896]{1,0:T(8,128)(2,1)S(1)}, u32[]{:S(2)}, u32[]{:S(2)}) collective-permute-start(bf16[32,896]{1,0:T(8,128)(2,1)S(1)} %add_convert_fusion), channel_id=1, source_target_pairs={{0,16},{8,24},{16,0},{24,8},{32,48},{40,56},{48,32},{56,40},{64,80... | collective-permute-start | bytes 172040 | tf_op jit(solution)/shard_map/ppermute | solution.py:23
  39.8 4.5 %collective-permute-start.15 = (bf16[32,896]{1,0:T(8,128)(2,1)S(1)}, bf16[32,896]{1,0:T(8,128)(2,1)S(1)}, u32[]{:S(2)}, u32[]{:S(2)}) collective-permute-start(bf16[32,896]{1,0:T(8,128)(2,1)S(1)} %add_convert_fusion), channel_id=1, source_target_pairs={{0,32},{8,40},{16,48},{24,56},{32,0},{40,8},{48,16},{56,24},{64,96... | collective-permute-start | bytes 172040 | tf_op jit(solution)/shard_map/ppermute | solution.py:23
  41.7 4.2 %collective-permute-start.16 = (bf16[32,896]{1,0:T(8,128)(2,1)S(1)}, bf16[32,896]{1,0:T(8,128)(2,1)S(1)}, u32[]{:S(2)}, u32[]{:S(2)}) collective-permute-start(bf16[32,896]{1,0:T(8,128)(2,1)S(1)} %add_convert_fusion), channel_id=1, source_target_pairs={{0,48},{8,56},{16,32},{24,40},{32,16},{40,24},{48,0},{56,8},{64,11... | collective-permute-start | bytes 172040 | tf_op jit(solution)/shard_map/ppermute | solution.py:23
  46.0 5.5 %collective-permute-start.17 = (bf16[4,32,896]{2,1,0:T(8,128)(2,1)S(1)}, bf16[4,32,896]{2,1,0:T(8,128)(2,1)S(1)}, u32[]{:S(2)}, u32[]{:S(2)}) collective-permute-start(bf16[4,32,896]{2,1,0:T(8,128)(2,1)S(1)} %pad_maximum_fusion.own_ref), channel_id=1, source_target_pairs={{0,8},{8,0},{16,24},{24,16},{32,40},{40,32},{48,56},{56,48},{64,72... | collective-permute-start | bytes 688136 | tf_op jit(solution)/shard_map/ppermute | solution.py:23

commit v4 on v3

--- a/solution.py
+++ b/solution.py
@@ -13,6 +13,7 @@
 NPW_DEV = 1280
 NB_DEV = 896
 CHUNK = 32
+SLOTS = (0, 2, 3, 1)
 BLOCK_PW = 640
 BF16 = jnp.bfloat16
 F32 = jnp.float32
@@ -239,8 +240,8 @@
     core_ref, y_ref, own_ref, other_ref, turned_ref, out_ref, right_ref, result_ref, sem
 ):
     core, y = core_ref[0], y_ref[0]
-    for s in range(4):
-        at = jnp.bitwise_xor(y, s) * CHUNK
+    for s, slot in enumerate(SLOTS):
+        at = jnp.bitwise_xor(y, slot) * CHUNK
         own_at = pl.multiple_of(core * NP + at, CHUNK)
         other_at = pl.multiple_of((1 - core) * NP + at, CHUNK)
         right_ref[pl.ds(own_at, CHUNK), :] = own_ref[s]
@@ -294,14 +295,13 @@
     total = (keep + over_pw(send, 1)).reshape(4, CHUNK, NB_DEV)
 
     sums = total[0]
-    for arrived in [over_pw(total[s].astype(BF16), 2 * s) for s in (3, 2, 1)]:
+    for arrived in [over_pw(total[s].astype(BF16), 2 * s) for s in (3, 1, 2)]:
         sums = sums + arrived.astype(F32)
     sent = sums.astype(BF16)
     for arrived in [over_pw(sent, 8 * s) for s in (3, 2, 1)]:
         sums = sums + arrived.astype(F32)
     mine = sums.astype(BF16)
-    chunk = {s: over_pw(mine, 2 * s) for s in (3, 2, 1)}
-    own = jnp.stack([mine, chunk[1], chunk[2], chunk[3]])
+    own = jnp.stack([mine] + [over_pw(mine, 2 * s) for s in SLOTS[1:]])
     other = over_pw(own, 1)
     return spread_back(core, y, own, other, turned)
 

time: 54.4 us -> 53 us (0.974)
  starting transfers between devices: 33.3 us -> 30.8 us
  waiting for transfers between devices: 12.8 us -> 13.9 us
    ppermute x11, starting transfers between devices: 19 us -> 16.5 us  [over_pw(): return lax.ppermute(x, 'pw', [(i, i ^ bits) for i in range(32)])]
    ppermute x11, waiting for transfers between devices: 12.1 us -> 13.1 us  [over_pw(): return lax.ppermute(x, 'pw', [(i, i ^ bits) for i in range(32)])]
  transfers between devices with their start and end apart: 18 -> 18, of which waited for: 9 -> 10; matrix products, arithmetic and copies ran while one was open for 0% -> 0% of each run, Pallas kernels for 7% -> 7%
where the time goes in v4:
time: 53 us; the launch traced here: 52.9 us
  starting transfers between devices  30.8 us (58%)
  waiting for transfers between devices  13.9 us (26%)
  Pallas kernels  7.7 us (15%)
    ppermute x11, starting transfers between devices, over_pw(): return lax.ppermute(x, 'pw', [(i, i ^ bits) for i in range(32)])  16.5 us
    ppermute x7, starting transfers between devices, over_band(): return lax.ppermute(x, 'band', [(i, i ^ bits) for i in range(8)])  14.3 us
    ppermute x11, waiting for transfers between devices, over_pw(): return lax.ppermute(x, 'pw', [(i, i ^ bits) for i in range(32)])  13.1 us
    pallas_call x1, Pallas kernels, spread_back(): pl.pallas_call(spread_kernel, out_shape=jax.ShapeDtypeStruct((2, NPW_DEV,...  2.72 us
    pallas_call x1, Pallas kernels, ahead(): pl.pallas_call(ahead_kernel, out_shape=(jax.ShapeDtypeStruct((2, NP, 3 *...  2.34 us
    pallas_call x1, Pallas kernels, project_near(): pl.pallas_call(near_kernel, out_shape=jax.ShapeDtypeStruct((2, NP, NB_DEV...  1.17 us
    pallas_call x1, Pallas kernels, project_far(): pl.pallas_call(far_kernel, out_shape=(half, half), in_specs=[smem()] + [v...  1.14 us
  transfers between devices with their start and end apart: 18, of which 10 were waited for; matrix products, arithmetic and copies ran while one was open for 0% of the time, Pallas kernels for 7%

profile of v4, /device:TPU:1, one launch (start us, length us, event | category | flops | bytes accessed | tf_op | source)
XLA Modules:
  0.0 52.9 jit_solution(4123147814352314868)
XLA Ops:
  0.0 7.7 %collective-permute-start = (bf16[2,16,1280]{2,1,0:T(8,128)(2,1)}, bf16[2,16,1280]{2,1,0:T(8,128)(2,1)S(1)}, u32[]{:S(2)}, u32[]{:S(2)}) collective-permute-start(bf16[2,16,1280]{2,1,0:T(8,128)(2,1)} %refs_3_.3), channel_id=1, source_target_pairs={{0,1},{1,0},{2,3},{3,2},{4,5},{5,4},{6,7},{7,6},{8,9},{9,8},{10,11... | collective-permute-start | bytes 245768 | tf_op jit(solution)/shard_map/ppermute | solution.py:28
  7.7 2.5 %collective-permute-start.1 = (bf16[2,16,1280]{2,1,0:T(8,128)(2,1)}, bf16[2,16,1280]{2,1,0:T(8,128)(2,1)S(1)}, u32[]{:S(2)}, u32[]{:S(2)}) collective-permute-start(bf16[2,16,1280]{2,1,0:T(8,128)(2,1)} %refs_3_.3), channel_id=1, source_target_pairs={{0,6},{1,7},{2,4},{3,5},{4,2},{5,3},{6,0},{7,1},{8,14},{9,15},{10,... | collective-permute-start | bytes 245768 | tf_op jit(solution)/shard_map/ppermute | solution.py:28
  10.2 0.5 collective-permute-start.2
  10.7 0.3 collective-permute-start.3
  11.0 0.1 shard_map.55.pick_ref
  11.1 2.6 %collective-permute-start.4 = (bf16[2,16,1280]{2,1,0:T(8,128)(2,1)S(1)}, bf16[2,16,1280]{2,1,0:T(8,128)(2,1)S(1)}, u32[]{:S(2)}, u32[]{:S(2)}) collective-permute-start(bf16[2,16,1280]{2,1,0:T(8,128)(2,1)S(1)} %collective-permute-done.refs_3_.refs_7_), channel_id=1, source_target_pairs={{0,6},{1,7},{2,4},{3,5},{4,2},{5,3},{6,0},{7,1},{8,14},{9,15},{10,... | collective-permute-start | bytes 245768 | tf_op jit(solution)/shard_map/ppermute | solution.py:28
  13.7 0.5 collective-permute-start.5
  14.2 0.3 collective-permute-start.6
  14.5 2.3 %shard_map.56 = (bf16[2,128,192]{2,1,0:T(8,128)(2,1)S(1)}, bf16[2,1280,896]{2,1,0:T(8,128)(2,1)S(1)}) custom-call(bf16[2,128,128]{2,1,0:T(8,128)(2,1)S(1)} %shard_map.55.pick_ref, s32[12]{0:T(128)S(1)} %copy-done.2, s32[12]{0:T(128)S(1)} %copy-done.3, f32[12,13,13]{2,1,0:T(8,128)S(1)} %copy-done.1, bf16[2,1280,896]{2,1,0:T(8,128)(2,1)} %waves_hbm.1), custom_call_target="tpu_custom_call" | custom-call | flops 2000000000 | bytes 8388608 | tf_op jit(solution)/shard_map/pallas_call | solution.py:128
  16.9 1.2 %shard_map.57.near_ref = f32[2,128,896]{2,1,0:T(8,128)S(1)} custom-call(bf16[2,128,192]{2,1,0:T(8,128)(2,1)S(1)} %get-tuple-element.11.left_ref, bf16[2,1280,896]{2,1,0:T(8,128)(2,1)S(1)} %get-tuple-element.12.waves_ref, bf16[2,16,1280]{2,1,0:T(8,128)(2,1)S(1)} %collective-permute-done.1.refs_0_, bf16[2,16,1280]{2,1,0:T(8,128)(2,1)S(1)} %collective-permute-done.2.refs_1_, ...), custom_call_target="tpu_custom_call" | custom-call | flops 587202560 | bytes 6291456 | tf_op jit(solution)/shard_map/pallas_call | solution.py:172
  18.1 0.7 %collective-permute-done.5.refs_1_.refs_5_ = bf16[2,16,1280]{2,1,0:T(8,128)(2,1)S(1)} collective-permute-done((bf16[2,16,1280]{2,1,0:T(8,128)(2,1)S(1)}, bf16[2,16,1280]{2,1,0:T(8,128)(2,1)S(1)}, u32[]{:S(2)}, u32[]{:S(2)}) %collective-permute-start.5) | collective-permute-done | bytes 81952 | tf_op jit(solution)/shard_map/ppermute | solution.py:28
  18.8 1.1 %shard_map.58 = (f32[128,896]{1,0:T(8,128)S(1)}, f32[128,896]{1,0:T(8,128)S(1)}) custom-call(s32[1]{0:T(128)} %bitcast.core_ref, f32[2,128,896]{2,1,0:T(8,128)S(1)} %shard_map.57.near_ref, bf16[2,128,192]{2,1,0:T(8,128)(2,1)S(1)} %get-tuple-element.11.left_ref, bf16[2,1280,896]{2,1,0:T(8,128)(2,1)S(1)} %get-tuple-element.12.waves_ref, ...), custom_call_target="tpu_custom_call" | custom-call | flops 587202560 | bytes 6291456 | tf_op jit(solution)/shard_map/pallas_call | solution.py:202
  19.9 3.0 %collective-permute-start.7 = (f32[128,896]{1,0:T(8,128)S(1)}, f32[128,896]{1,0:T(8,128)S(1)}, u32[]{:S(2)}, u32[]{:S(2)}) collective-permute-start(f32[128,896]{1,0:T(8,128)S(1)} %get-tuple-element.14), channel_id=1, source_target_pairs={{0,8},{8,0},{16,24},{24,16},{32,40},{40,32},{48,56},{56,48},{64,72... | collective-permute-start | bytes 1376264 | tf_op jit(solution)/shard_map/ppermute | solution.py:24
  23.0 1.4 %collective-permute-done.7 = f32[128,896]{1,0:T(8,128)S(1)} collective-permute-done((f32[128,896]{1,0:T(8,128)S(1)}, f32[128,896]{1,0:T(8,128)S(1)}, u32[]{:S(2)}, u32[]{:S(2)}) %collective-permute-start.7) | collective-permute-done | bytes 458784 | tf_op jit(solution)/shard_map/ppermute | solution.py:24
  24.5 3.0 %collective-permute-start.10 = (bf16[32,896]{1,0:T(8,128)(2,1)S(1)}, bf16[32,896]{1,0:T(8,128)(2,1)S(1)}, u32[]{:S(2)}, u32[]{:S(2)}) collective-permute-start(bf16[32,896]{1,0:T(8,128)(2,1)S(1)} %get-tuple-element.18), channel_id=1, source_target_pairs={{0,32},{8,40},{16,48},{24,56},{32,0},{40,8},{48,16},{56,24},{64,96... | collective-permute-start | bytes 172040 | tf_op jit(solution)/shard_map/ppermute | solution.py:24
  27.5 0.8 %collective-permute-start.8 = (bf16[32,896]{1,0:T(8,128)(2,1)S(1)}, bf16[32,896]{1,0:T(8,128)(2,1)S(1)}, u32[]{:S(2)}, u32[]{:S(2)}) collective-permute-start(bf16[32,896]{1,0:T(8,128)(2,1)S(1)} %get-tuple-element.17), channel_id=1, source_target_pairs={{0,48},{8,56},{16,32},{24,40},{32,16},{40,24},{48,0},{56,8},{64,11... | collective-permute-start | bytes 172040 | tf_op jit(solution)/shard_map/ppermute | solution.py:24
  28.3 0.8 %collective-permute-done.10 = bf16[32,896]{1,0:T(8,128)(2,1)S(1)} collective-permute-done((bf16[32,896]{1,0:T(8,128)(2,1)S(1)}, bf16[32,896]{1,0:T(8,128)(2,1)S(1)}, u32[]{:S(2)}, u32[]{:S(2)}) %collective-permute-start.10) | collective-permute-done | bytes 57376 | tf_op jit(solution)/shard_map/ppermute | solution.py:24
  29.1 2.6 %collective-permute-done.8 = bf16[32,896]{1,0:T(8,128)(2,1)S(1)} collective-permute-done((bf16[32,896]{1,0:T(8,128)(2,1)S(1)}, bf16[32,896]{1,0:T(8,128)(2,1)S(1)}, u32[]{:S(2)}, u32[]{:S(2)}) %collective-permute-start.8) | collective-permute-done | bytes 57376 | tf_op jit(solution)/shard_map/ppermute | solution.py:24
  31.8 1.7 %collective-permute-start.11 = (bf16[32,896]{1,0:T(8,128)(2,1)S(1)}, bf16[32,896]{1,0:T(8,128)(2,1)S(1)}, u32[]{:S(2)}, u32[]{:S(2)}) collective-permute-start(bf16[32,896]{1,0:T(8,128)(2,1)S(1)} %fusion.2), channel_id=1, source_target_pairs={{0,192},{8,200},{16,208},{24,216},{32,224},{40,232},{48,240},{56,2... | collective-permute-start | bytes 172040 | tf_op jit(solution)/shard_map/ppermute | solution.py:24
  33.5 0.3 collective-permute-start.12
  33.8 1.6 %collective-permute-start.13 = (bf16[32,896]{1,0:T(8,128)(2,1)S(1)}, bf16[32,896]{1,0:T(8,128)(2,1)S(1)}, u32[]{:S(2)}, u32[]{:S(2)}) collective-permute-start(bf16[32,896]{1,0:T(8,128)(2,1)S(1)} %fusion.2), channel_id=1, source_target_pairs={{0,64},{8,72},{16,80},{24,88},{32,96},{40,104},{48,112},{56,120},{... | collective-permute-start | bytes 172040 | tf_op jit(solution)/shard_map/ppermute | solution.py:24
  35.4 1.3 %collective-permute-done.11 = bf16[32,896]{1,0:T(8,128)(2,1)S(1)} collective-permute-done((bf16[32,896]{1,0:T(8,128)(2,1)S(1)}, bf16[32,896]{1,0:T(8,128)(2,1)S(1)}, u32[]{:S(2)}, u32[]{:S(2)}) %collective-permute-start.11) | collective-permute-done | bytes 57376 | tf_op jit(solution)/shard_map/ppermute | solution.py:24
  36.7 2.5 %collective-permute-done.12 = bf16[32,896]{1,0:T(8,128)(2,1)S(1)} collective-permute-done((bf16[32,896]{1,0:T(8,128)(2,1)S(1)}, bf16[32,896]{1,0:T(8,128)(2,1)S(1)}, u32[]{:S(2)}, u32[]{:S(2)}) %collective-permute-start.12) | collective-permute-done | bytes 57376 | tf_op jit(solution)/shard_map/ppermute | solution.py:24
  39.3 1.7 %collective-permute-start.14 = (bf16[32,896]{1,0:T(8,128)(2,1)S(1)}, bf16[32,896]{1,0:T(8,128)(2,1)S(1)}, u32[]{:S(2)}, u32[]{:S(2)}) collective-permute-start(bf16[32,896]{1,0:T(8,128)(2,1)S(1)} %add_convert_fusion), channel_id=1, source_target_pairs={{0,32},{8,40},{16,48},{24,56},{32,0},{40,8},{48,16},{56,24},{64,96... | collective-permute-start | bytes 172040 | tf_op jit(solution)/shard_map/ppermute | solution.py:24
  41.0 2.1 %collective-permute-start.15 = (bf16[32,896]{1,0:T(8,128)(2,1)S(1)}, bf16[32,896]{1,0:T(8,128)(2,1)S(1)}, u32[]{:S(2)}, u32[]{:S(2)}) collective-permute-start(bf16[32,896]{1,0:T(8,128)(2,1)S(1)} %add_convert_fusion), channel_id=1, source_target_pairs={{0,48},{8,56},{16,32},{24,40},{32,16},{40,24},{48,0},{56,8},{64,11... | collective-permute-start | bytes 172040 | tf_op jit(solution)/shard_map/ppermute | solution.py:24
  43.2 0.8 %collective-permute-done.14 = bf16[32,896]{1,0:T(8,128)(2,1)S(1)} collective-permute-done((bf16[32,896]{1,0:T(8,128)(2,1)S(1)}, bf16[32,896]{1,0:T(8,128)(2,1)S(1)}, u32[]{:S(2)}, u32[]{:S(2)}) %collective-permute-start.14) | collective-permute-done | bytes 57376 | tf_op jit(solution)/shard_map/ppermute | solution.py:24
  43.9 1.3 %collective-permute-done.15 = bf16[32,896]{1,0:T(8,128)(2,1)S(1)} collective-permute-done((bf16[32,896]{1,0:T(8,128)(2,1)S(1)}, bf16[32,896]{1,0:T(8,128)(2,1)S(1)}, u32[]{:S(2)}, u32[]{:S(2)}) %collective-permute-start.15) | collective-permute-done | bytes 57376 | tf_op jit(solution)/shard_map/ppermute | solution.py:24
  45.3 1.4 %collective-permute-done.16 = bf16[32,896]{1,0:T(8,128)(2,1)S(1)} collective-permute-done((bf16[32,896]{1,0:T(8,128)(2,1)S(1)}, bf16[32,896]{1,0:T(8,128)(2,1)S(1)}, u32[]{:S(2)}, u32[]{:S(2)}) %collective-permute-start.16) | collective-permute-done | bytes 57376 | tf_op jit(solution)/shard_map/ppermute | solution.py:24
  46.7 2.2 %collective-permute-start.17 = (bf16[4,32,896]{2,1,0:T(8,128)(2,1)S(1)}, bf16[4,32,896]{2,1,0:T(8,128)(2,1)S(1)}, u32[]{:S(2)}, u32[]{:S(2)}) collective-permute-start(bf16[4,32,896]{2,1,0:T(8,128)(2,1)S(1)} %pad_maximum_fusion.own_ref), channel_id=1, source_target_pairs={{0,8},{8,0},{16,24},{24,16},{32,40},{40,32},{48,56},{56,48},{64,72... | collective-permute-start | bytes 688136 | tf_op jit(solution)/shard_map/ppermute | solution.py:24
  48.9 0.2 shard_map.59.turned_ref
  49.1 0.9 %collective-permute-done.17.other_ref = bf16[4,32,896]{2,1,0:T(8,128)(2,1)S(1)} collective-permute-done((bf16[4,32,896]{2,1,0:T(8,128)(2,1)S(1)}, bf16[4,32,896]{2,1,0:T(8,128)(2,1)S(1)}, u32[]{:S(2)}, u32[]{:S(2)}) %collective-permute-start.17) | collective-permute-done | bytes 229408 | tf_op jit(solution)/shard_map/ppermute | solution.py:24
  50.0 2.7 %shard_map.60 = bf16[2,1280,896]{2,1,0:T(8,128)(2,1)} custom-call(s32[1]{0:T(128)} %bitcast.core_ref, s32[1]{0:T(128)} %bitcast.1.y_ref, bf16[4,32,896]{2,1,0:T(8,128)(2,1)S(1)} %pad_maximum_fusion.own_ref, bf16[4,32,896]{2,1,0:T(8,128)(2,1)S(1)} %collective-permute-done.17.other_ref, bf16[2,1280,256]{2,1,0:T(8,128)(2,1)S(1)} %shard_map.59.turned_ref), custom_call_target="tpu_custom_call" | custom-call | flops 1174405120 | bytes 6291456 | tf_op jit(solution)/shard_map/pallas_call | solution.py:267
  (23 shorter events, 0.3 us)
Async XLA Ops:
  0.0 11.1 %collective-permute-start = (bf16[2,16,1280]{2,1,0:T(8,128)(2,1)}, bf16[2,16,1280]{2,1,0:T(8,128)(2,1)S(1)}, u32[]{:S(2)}, u32[]{:S(2)}) collective-permute-start(bf16[2,16,1280]{2,1,0:T(8,128)(2,1)} %refs_3_.3), channel_id=1, source_target_pairs={{0,1},{1,0},{2,3},{3,2},{4,5},{5,4},{6,7},{7,6},{8,9},{9,8},{10,11... | collective-permute-start | bytes 245768 | tf_op jit(solution)/shard_map/ppermute | solution.py:28
  7.7 6.5 %collective-permute-start.1 = (bf16[2,16,1280]{2,1,0:T(8,128)(2,1)}, bf16[2,16,1280]{2,1,0:T(8,128)(2,1)S(1)}, u32[]{:S(2)}, u32[]{:S(2)}) collective-permute-start(bf16[2,16,1280]{2,1,0:T(8,128)(2,1)} %refs_3_.3), channel_id=1, source_target_pairs={{0,6},{1,7},{2,4},{3,5},{4,2},{5,3},{6,0},{7,1},{8,14},{9,15},{10,... | collective-permute-start | bytes 245768 | tf_op jit(solution)/shard_map/ppermute | solution.py:28
  10.2 6.6 %collective-permute-start.2 = (bf16[2,16,1280]{2,1,0:T(8,128)(2,1)}, bf16[2,16,1280]{2,1,0:T(8,128)(2,1)S(1)}, u32[]{:S(2)}, u32[]{:S(2)}) collective-permute-start(bf16[2,16,1280]{2,1,0:T(8,128)(2,1)} %refs_3_.3), channel_id=1, source_target_pairs={{0,4},{1,5},{2,6},{3,7},{4,0},{5,1},{6,2},{7,3},{8,12},{9,13},{10,... | collective-permute-start | bytes 245768 | tf_op jit(solution)/shard_map/ppermute | solution.py:28
  10.7 6.1 %collective-permute-start.3 = (bf16[2,16,1280]{2,1,0:T(8,128)(2,1)}, bf16[2,16,1280]{2,1,0:T(8,128)(2,1)S(1)}, u32[]{:S(2)}, u32[]{:S(2)}) collective-permute-start(bf16[2,16,1280]{2,1,0:T(8,128)(2,1)} %refs_3_.3), channel_id=1, source_target_pairs={{0,2},{1,3},{2,0},{3,1},{4,6},{5,7},{6,4},{7,5},{8,10},{9,11},{10,... | collective-permute-start | bytes 245768 | tf_op jit(solution)/shard_map/ppermute | solution.py:28
  11.0 3.5 %copy-start.1 = (f32[12,13,13]{2,1,0:T(8,128)S(1)}, f32[12,13,13]{2,1,0:T(8,128)}, u32[]{:S(2)}) copy-start(f32[12,13,13]{2,1,0:T(8,128)} %coupling_hbm.1) | copy-start | bytes 24340
  11.0 3.5 %copy-start.2 = (s32[12]{0:T(128)S(1)}, s32[12]{0:T(128)}, u32[]{:S(2)}) copy-start(s32[12]{0:T(128)} %offsets_hbm.1) | copy-start | bytes 148
  11.0 3.5 %copy-start.3 = (s32[12]{0:T(128)S(1)}, s32[12]{0:T(128)}, u32[]{:S(2)}) copy-start(s32[12]{0:T(128)} %counts_hbm.1) | copy-start | bytes 148
  11.1 5.8 %copy-start = (bf16[2,16,1280]{2,1,0:T(8,128)(2,1)S(1)}, bf16[2,16,1280]{2,1,0:T(8,128)(2,1)}, u32[]{:S(2)}) copy-start(bf16[2,16,1280]{2,1,0:T(8,128)(2,1)} %refs_3_.3) | copy-start | bytes 245764
  11.1 6.9 %collective-permute-start.4 = (bf16[2,16,1280]{2,1,0:T(8,128)(2,1)S(1)}, bf16[2,16,1280]{2,1,0:T(8,128)(2,1)S(1)}, u32[]{:S(2)}, u32[]{:S(2)}) collective-permute-start(bf16[2,16,1280]{2,1,0:T(8,128)(2,1)S(1)} %collective-permute-done.refs_3_.refs_7_), channel_id=1, source_target_pairs={{0,6},{1,7},{2,4},{3,5},{4,2},{5,3},{6,0},{7,1},{8,14},{9,15},{10,... | collective-permute-start | bytes 245768 | tf_op jit(solution)/shard_map/ppermute | solution.py:28
  13.7 5.1 %collective-permute-start.5 = (bf16[2,16,1280]{2,1,0:T(8,128)(2,1)S(1)}, bf16[2,16,1280]{2,1,0:T(8,128)(2,1)S(1)}, u32[]{:S(2)}, u32[]{:S(2)}) collective-permute-start(bf16[2,16,1280]{2,1,0:T(8,128)(2,1)S(1)} %collective-permute-done.refs_3_.refs_7_), channel_id=1, source_target_pairs={{0,4},{1,5},{2,6},{3,7},{4,0},{5,1},{6,2},{7,3},{8,12},{9,13},{10,... | collective-permute-start | bytes 245768 | tf_op jit(solution)/shard_map/ppermute | solution.py:28
  14.2 4.6 %collective-permute-start.6 = (bf16[2,16,1280]{2,1,0:T(8,128)(2,1)S(1)}, bf16[2,16,1280]{2,1,0:T(8,128)(2,1)S(1)}, u32[]{:S(2)}, u32[]{:S(2)}) collective-permute-start(bf16[2,16,1280]{2,1,0:T(8,128)(2,1)S(1)} %collective-permute-done.refs_3_.refs_7_), channel_id=1, source_target_pairs={{0,2},{1,3},{2,0},{3,1},{4,6},{5,7},{6,4},{7,5},{8,10},{9,11},{10,... | collective-permute-start | bytes 245768 | tf_op jit(solution)/shard_map/ppermute | solution.py:28
  19.9 4.5 %collective-permute-start.7 = (f32[128,896]{1,0:T(8,128)S(1)}, f32[128,896]{1,0:T(8,128)S(1)}, u32[]{:S(2)}, u32[]{:S(2)}) collective-permute-start(f32[128,896]{1,0:T(8,128)S(1)} %get-tuple-element.14), channel_id=1, source_target_pairs={{0,8},{8,0},{16,24},{24,16},{32,40},{40,32},{48,56},{56,48},{64,72... | collective-permute-start | bytes 1376264 | tf_op jit(solution)/shard_map/ppermute | solution.py:24
  24.5 4.6 %collective-permute-start.10 = (bf16[32,896]{1,0:T(8,128)(2,1)S(1)}, bf16[32,896]{1,0:T(8,128)(2,1)S(1)}, u32[]{:S(2)}, u32[]{:S(2)}) collective-permute-start(bf16[32,896]{1,0:T(8,128)(2,1)S(1)} %get-tuple-element.18), channel_id=1, source_target_pairs={{0,32},{8,40},{16,48},{24,56},{32,0},{40,8},{48,16},{56,24},{64,96... | collective-permute-start | bytes 172040 | tf_op jit(solution)/shard_map/ppermute | solution.py:24
  27.5 4.2 %collective-permute-start.8 = (bf16[32,896]{1,0:T(8,128)(2,1)S(1)}, bf16[32,896]{1,0:T(8,128)(2,1)S(1)}, u32[]{:S(2)}, u32[]{:S(2)}) collective-permute-start(bf16[32,896]{1,0:T(8,128)(2,1)S(1)} %get-tuple-element.17), channel_id=1, source_target_pairs={{0,48},{8,56},{16,32},{24,40},{32,16},{40,24},{48,0},{56,8},{64,11... | collective-permute-start | bytes 172040 | tf_op jit(solution)/shard_map/ppermute | solution.py:24
  28.3 3.5 %collective-permute-start.9 = (bf16[32,896]{1,0:T(8,128)(2,1)S(1)}, bf16[32,896]{1,0:T(8,128)(2,1)S(1)}, u32[]{:S(2)}, u32[]{:S(2)}) collective-permute-start(bf16[32,896]{1,0:T(8,128)(2,1)S(1)} %get-tuple-element.19), channel_id=1, source_target_pairs={{0,16},{8,24},{16,0},{24,8},{32,48},{40,56},{48,32},{56,40},{64,80... | collective-permute-start | bytes 172040 | tf_op jit(solution)/shard_map/ppermute | solution.py:24
  31.8 4.9 %collective-permute-start.11 = (bf16[32,896]{1,0:T(8,128)(2,1)S(1)}, bf16[32,896]{1,0:T(8,128)(2,1)S(1)}, u32[]{:S(2)}, u32[]{:S(2)}) collective-permute-start(bf16[32,896]{1,0:T(8,128)(2,1)S(1)} %fusion.2), channel_id=1, source_target_pairs={{0,192},{8,200},{16,208},{24,216},{32,224},{40,232},{48,240},{56,2... | collective-permute-start | bytes 172040 | tf_op jit(solution)/shard_map/ppermute | solution.py:24
  33.5 5.7 %collective-permute-start.12 = (bf16[32,896]{1,0:T(8,128)(2,1)S(1)}, bf16[32,896]{1,0:T(8,128)(2,1)S(1)}, u32[]{:S(2)}, u32[]{:S(2)}) collective-permute-start(bf16[32,896]{1,0:T(8,128)(2,1)S(1)} %fusion.2), channel_id=1, source_target_pairs={{0,128},{8,136},{16,144},{24,152},{32,160},{40,168},{48,176},{56,1... | collective-permute-start | bytes 172040 | tf_op jit(solution)/shard_map/ppermute | solution.py:24
  33.8 5.5 %collective-permute-start.13 = (bf16[32,896]{1,0:T(8,128)(2,1)S(1)}, bf16[32,896]{1,0:T(8,128)(2,1)S(1)}, u32[]{:S(2)}, u32[]{:S(2)}) collective-permute-start(bf16[32,896]{1,0:T(8,128)(2,1)S(1)} %fusion.2), channel_id=1, source_target_pairs={{0,64},{8,72},{16,80},{24,88},{32,96},{40,104},{48,112},{56,120},{... | collective-permute-start | bytes 172040 | tf_op jit(solution)/shard_map/ppermute | solution.py:24
  39.3 4.6 %collective-permute-start.14 = (bf16[32,896]{1,0:T(8,128)(2,1)S(1)}, bf16[32,896]{1,0:T(8,128)(2,1)S(1)}, u32[]{:S(2)}, u32[]{:S(2)}) collective-permute-start(bf16[32,896]{1,0:T(8,128)(2,1)S(1)} %add_convert_fusion), channel_id=1, source_target_pairs={{0,32},{8,40},{16,48},{24,56},{32,0},{40,8},{48,16},{56,24},{64,96... | collective-permute-start | bytes 172040 | tf_op jit(solution)/shard_map/ppermute | solution.py:24
  41.0 4.2 %collective-permute-start.15 = (bf16[32,896]{1,0:T(8,128)(2,1)S(1)}, bf16[32,896]{1,0:T(8,128)(2,1)S(1)}, u32[]{:S(2)}, u32[]{:S(2)}) collective-permute-start(bf16[32,896]{1,0:T(8,128)(2,1)S(1)} %add_convert_fusion), channel_id=1, source_target_pairs={{0,48},{8,56},{16,32},{24,40},{32,16},{40,24},{48,0},{56,8},{64,11... | collective-permute-start | bytes 172040 | tf_op jit(solution)/shard_map/ppermute | solution.py:24
  43.2 3.5 %collective-permute-start.16 = (bf16[32,896]{1,0:T(8,128)(2,1)S(1)}, bf16[32,896]{1,0:T(8,128)(2,1)S(1)}, u32[]{:S(2)}, u32[]{:S(2)}) collective-permute-start(bf16[32,896]{1,0:T(8,128)(2,1)S(1)} %add_convert_fusion), channel_id=1, source_target_pairs={{0,16},{8,24},{16,0},{24,8},{32,48},{40,56},{48,32},{56,40},{64,80... | collective-permute-start | bytes 172040 | tf_op jit(solution)/shard_map/ppermute | solution.py:24
  46.7 3.3 %collective-permute-start.17 = (bf16[4,32,896]{2,1,0:T(8,128)(2,1)S(1)}, bf16[4,32,896]{2,1,0:T(8,128)(2,1)S(1)}, u32[]{:S(2)}, u32[]{:S(2)}) collective-permute-start(bf16[4,32,896]{2,1,0:T(8,128)(2,1)S(1)} %pad_maximum_fusion.own_ref), channel_id=1, source_target_pairs={{0,8},{8,0},{16,24},{24,16},{32,40},{40,32},{48,56},{56,48},{64,72... | collective-permute-start | bytes 688136 | tf_op jit(solution)/shard_map/ppermute | solution.py:24

commit v5 on v4

--- a/solution.py
+++ b/solution.py
@@ -14,7 +14,7 @@
 NB_DEV = 896
 CHUNK = 32
 SLOTS = (0, 2, 3, 1)
-BLOCK_PW = 640
+BLOCK_PW = 320
 BF16 = jnp.bfloat16
 F32 = jnp.float32
 MIB = 1024 * 1024
@@ -298,7 +298,7 @@
     for arrived in [over_pw(total[s].astype(BF16), 2 * s) for s in (3, 1, 2)]:
         sums = sums + arrived.astype(F32)
     sent = sums.astype(BF16)
-    for arrived in [over_pw(sent, 8 * s) for s in (3, 2, 1)]:
+    for arrived in [over_pw(sent, 8 * s) for s in (3, 1, 2)]:
         sums = sums + arrived.astype(F32)
     mine = sums.astype(BF16)
     own = jnp.stack([mine] + [over_pw(mine, 2 * s) for s in SLOTS[1:]])

time: 53 us -> 52.4 us (0.989)
  transfers between devices with their start and end apart: 18 -> 18, of which waited for: 10 -> 11; matrix products, arithmetic and copies ran while one was open for 0% -> 0% of each run, Pallas kernels for 7% -> 7%
where the time goes in v5:
time: 52.4 us; the launch traced here: 52.3 us
  starting transfers between devices  30.7 us (59%)
  waiting for transfers between devices  13.5 us (26%)
  Pallas kernels  7.56 us (14%)
    ppermute x11, starting transfers between devices, over_pw(): return lax.ppermute(x, 'pw', [(i, i ^ bits) for i in range(32)])  16.4 us
    ppermute x7, starting transfers between devices, over_band(): return lax.ppermute(x, 'band', [(i, i ^ bits) for i in range(8)])  14.3 us
    ppermute x11, waiting for transfers between devices, over_pw(): return lax.ppermute(x, 'pw', [(i, i ^ bits) for i in range(32)])  12.8 us
    pallas_call x1, Pallas kernels, spread_back(): pl.pallas_call(spread_kernel, out_shape=jax.ShapeDtypeStruct((2, NPW_DEV,...  2.58 us
    pallas_call x1, Pallas kernels, ahead(): pl.pallas_call(ahead_kernel, out_shape=(jax.ShapeDtypeStruct((2, NP, 3 *...  2.34 us
    pallas_call x1, Pallas kernels, project_near(): pl.pallas_call(near_kernel, out_shape=jax.ShapeDtypeStruct((2, NP, NB_DEV...  1.17 us
    pallas_call x1, Pallas kernels, project_far(): pl.pallas_call(far_kernel, out_shape=(half, half), in_specs=[smem()] + [v...  1.14 us
  transfers between devices with their start and end apart: 18, of which 11 were waited for; matrix products, arithmetic and copies ran while one was open for 0% of the time, Pallas kernels for 7%

profile of v5, /device:TPU:1, one launch (start us, length us, event | category | flops | bytes accessed | tf_op | source)
XLA Modules:
  0.0 52.3 jit_solution(11188630388284802447)
XLA Ops:
  0.0 7.7 %collective-permute-start = (bf16[2,16,1280]{2,1,0:T(8,128)(2,1)}, bf16[2,16,1280]{2,1,0:T(8,128)(2,1)S(1)}, u32[]{:S(2)}, u32[]{:S(2)}) collective-permute-start(bf16[2,16,1280]{2,1,0:T(8,128)(2,1)} %refs_3_.3), channel_id=1, source_target_pairs={{0,1},{1,0},{2,3},{3,2},{4,5},{5,4},{6,7},{7,6},{8,9},{9,8},{10,11... | collective-permute-start | bytes 245768 | tf_op jit(solution)/shard_map/ppermute | solution.py:28
  7.7 2.5 %collective-permute-start.1 = (bf16[2,16,1280]{2,1,0:T(8,128)(2,1)}, bf16[2,16,1280]{2,1,0:T(8,128)(2,1)S(1)}, u32[]{:S(2)}, u32[]{:S(2)}) collective-permute-start(bf16[2,16,1280]{2,1,0:T(8,128)(2,1)} %refs_3_.3), channel_id=1, source_target_pairs={{0,6},{1,7},{2,4},{3,5},{4,2},{5,3},{6,0},{7,1},{8,14},{9,15},{10,... | collective-permute-start | bytes 245768 | tf_op jit(solution)/shard_map/ppermute | solution.py:28
  10.2 0.5 collective-permute-start.2
  10.7 0.3 collective-permute-start.3
  11.1 2.6 %collective-permute-start.4 = (bf16[2,16,1280]{2,1,0:T(8,128)(2,1)S(1)}, bf16[2,16,1280]{2,1,0:T(8,128)(2,1)S(1)}, u32[]{:S(2)}, u32[]{:S(2)}) collective-permute-start(bf16[2,16,1280]{2,1,0:T(8,128)(2,1)S(1)} %collective-permute-done.refs_3_.refs_7_), channel_id=1, source_target_pairs={{0,6},{1,7},{2,4},{3,5},{4,2},{5,3},{6,0},{7,1},{8,14},{9,15},{10,... | collective-permute-start | bytes 245768 | tf_op jit(solution)/shard_map/ppermute | solution.py:28
  13.7 0.5 collective-permute-start.5
  14.2 0.3 collective-permute-start.6
  14.5 2.3 %shard_map.56 = (bf16[2,128,192]{2,1,0:T(8,128)(2,1)S(1)}, bf16[2,1280,896]{2,1,0:T(8,128)(2,1)S(1)}) custom-call(bf16[2,128,128]{2,1,0:T(8,128)(2,1)S(1)} %shard_map.55.pick_ref, s32[12]{0:T(128)S(1)} %copy-done.2, s32[12]{0:T(128)S(1)} %copy-done.3, f32[12,13,13]{2,1,0:T(8,128)S(1)} %copy-done.1, bf16[2,1280,896]{2,1,0:T(8,128)(2,1)} %waves_hbm.1), custom_call_target="tpu_custom_call" | custom-call | flops 2000000000 | bytes 8388608 | tf_op jit(solution)/shard_map/pallas_call | solution.py:128
  16.9 1.2 %shard_map.57.near_ref = f32[2,128,896]{2,1,0:T(8,128)S(1)} custom-call(bf16[2,128,192]{2,1,0:T(8,128)(2,1)S(1)} %get-tuple-element.11.left_ref, bf16[2,1280,896]{2,1,0:T(8,128)(2,1)S(1)} %get-tuple-element.12.waves_ref, bf16[2,16,1280]{2,1,0:T(8,128)(2,1)S(1)} %collective-permute-done.1.refs_0_, bf16[2,16,1280]{2,1,0:T(8,128)(2,1)S(1)} %collective-permute-done.2.refs_1_, ...), custom_call_target="tpu_custom_call" | custom-call | flops 587202560 | bytes 6291456 | tf_op jit(solution)/shard_map/pallas_call | solution.py:172
  18.1 0.7 %collective-permute-done.5.refs_1_.refs_5_ = bf16[2,16,1280]{2,1,0:T(8,128)(2,1)S(1)} collective-permute-done((bf16[2,16,1280]{2,1,0:T(8,128)(2,1)S(1)}, bf16[2,16,1280]{2,1,0:T(8,128)(2,1)S(1)}, u32[]{:S(2)}, u32[]{:S(2)}) %collective-permute-start.5) | collective-permute-done | bytes 81952 | tf_op jit(solution)/shard_map/ppermute | solution.py:28
  18.8 1.1 %shard_map.58 = (f32[128,896]{1,0:T(8,128)S(1)}, f32[128,896]{1,0:T(8,128)S(1)}) custom-call(s32[1]{0:T(128)} %bitcast.core_ref, f32[2,128,896]{2,1,0:T(8,128)S(1)} %shard_map.57.near_ref, bf16[2,128,192]{2,1,0:T(8,128)(2,1)S(1)} %get-tuple-element.11.left_ref, bf16[2,1280,896]{2,1,0:T(8,128)(2,1)S(1)} %get-tuple-element.12.waves_ref, ...), custom_call_target="tpu_custom_call" | custom-call | flops 587202560 | bytes 6291456 | tf_op jit(solution)/shard_map/pallas_call | solution.py:202
  19.9 3.0 %collective-permute-start.7 = (f32[128,896]{1,0:T(8,128)S(1)}, f32[128,896]{1,0:T(8,128)S(1)}, u32[]{:S(2)}, u32[]{:S(2)}) collective-permute-start(f32[128,896]{1,0:T(8,128)S(1)} %get-tuple-element.14), channel_id=1, source_target_pairs={{0,8},{8,0},{16,24},{24,16},{32,40},{40,32},{48,56},{56,48},{64,72... | collective-permute-start | bytes 1376264 | tf_op jit(solution)/shard_map/ppermute | solution.py:24
  23.0 1.4 %collective-permute-done.7 = f32[128,896]{1,0:T(8,128)S(1)} collective-permute-done((f32[128,896]{1,0:T(8,128)S(1)}, f32[128,896]{1,0:T(8,128)S(1)}, u32[]{:S(2)}, u32[]{:S(2)}) %collective-permute-start.7) | collective-permute-done | bytes 458784 | tf_op jit(solution)/shard_map/ppermute | solution.py:24
  24.5 3.0 %collective-permute-start.10 = (bf16[32,896]{1,0:T(8,128)(2,1)S(1)}, bf16[32,896]{1,0:T(8,128)(2,1)S(1)}, u32[]{:S(2)}, u32[]{:S(2)}) collective-permute-start(bf16[32,896]{1,0:T(8,128)(2,1)S(1)} %get-tuple-element.18), channel_id=1, source_target_pairs={{0,32},{8,40},{16,48},{24,56},{32,0},{40,8},{48,16},{56,24},{64,96... | collective-permute-start | bytes 172040 | tf_op jit(solution)/shard_map/ppermute | solution.py:24
  27.5 0.8 %collective-permute-start.8 = (bf16[32,896]{1,0:T(8,128)(2,1)S(1)}, bf16[32,896]{1,0:T(8,128)(2,1)S(1)}, u32[]{:S(2)}, u32[]{:S(2)}) collective-permute-start(bf16[32,896]{1,0:T(8,128)(2,1)S(1)} %get-tuple-element.17), channel_id=1, source_target_pairs={{0,48},{8,56},{16,32},{24,40},{32,16},{40,24},{48,0},{56,8},{64,11... | collective-permute-start | bytes 172040 | tf_op jit(solution)/shard_map/ppermute | solution.py:24
  28.3 0.8 %collective-permute-done.10 = bf16[32,896]{1,0:T(8,128)(2,1)S(1)} collective-permute-done((bf16[32,896]{1,0:T(8,128)(2,1)S(1)}, bf16[32,896]{1,0:T(8,128)(2,1)S(1)}, u32[]{:S(2)}, u32[]{:S(2)}) %collective-permute-start.10) | collective-permute-done | bytes 57376 | tf_op jit(solution)/shard_map/ppermute | solution.py:24
  29.1 2.6 %collective-permute-done.8 = bf16[32,896]{1,0:T(8,128)(2,1)S(1)} collective-permute-done((bf16[32,896]{1,0:T(8,128)(2,1)S(1)}, bf16[32,896]{1,0:T(8,128)(2,1)S(1)}, u32[]{:S(2)}, u32[]{:S(2)}) %collective-permute-start.8) | collective-permute-done | bytes 57376 | tf_op jit(solution)/shard_map/ppermute | solution.py:24
  31.8 1.7 %collective-permute-start.11 = (bf16[32,896]{1,0:T(8,128)(2,1)S(1)}, bf16[32,896]{1,0:T(8,128)(2,1)S(1)}, u32[]{:S(2)}, u32[]{:S(2)}) collective-permute-start(bf16[32,896]{1,0:T(8,128)(2,1)S(1)} %fusion.2), channel_id=1, source_target_pairs={{0,192},{8,200},{16,208},{24,216},{32,224},{40,232},{48,240},{56,2... | collective-permute-start | bytes 172040 | tf_op jit(solution)/shard_map/ppermute | solution.py:24
  33.5 0.3 collective-permute-start.12
  33.8 1.6 %collective-permute-start.13 = (bf16[32,896]{1,0:T(8,128)(2,1)S(1)}, bf16[32,896]{1,0:T(8,128)(2,1)S(1)}, u32[]{:S(2)}, u32[]{:S(2)}) collective-permute-start(bf16[32,896]{1,0:T(8,128)(2,1)S(1)} %fusion.2), channel_id=1, source_target_pairs={{0,128},{8,136},{16,144},{24,152},{32,160},{40,168},{48,176},{56,1... | collective-permute-start | bytes 172040 | tf_op jit(solution)/shard_map/ppermute | solution.py:24
  35.4 1.4 %collective-permute-done.11 = bf16[32,896]{1,0:T(8,128)(2,1)S(1)} collective-permute-done((bf16[32,896]{1,0:T(8,128)(2,1)S(1)}, bf16[32,896]{1,0:T(8,128)(2,1)S(1)}, u32[]{:S(2)}, u32[]{:S(2)}) %collective-permute-start.11) | collective-permute-done | bytes 57376 | tf_op jit(solution)/shard_map/ppermute | solution.py:24
  36.8 0.4 collective-permute-done.12
  37.2 2.4 %collective-permute-done.13 = bf16[32,896]{1,0:T(8,128)(2,1)S(1)} collective-permute-done((bf16[32,896]{1,0:T(8,128)(2,1)S(1)}, bf16[32,896]{1,0:T(8,128)(2,1)S(1)}, u32[]{:S(2)}, u32[]{:S(2)}) %collective-permute-start.13) | collective-permute-done | bytes 57376 | tf_op jit(solution)/shard_map/ppermute | solution.py:24
  39.8 2.3 %collective-permute-start.15 = (bf16[32,896]{1,0:T(8,128)(2,1)S(1)}, bf16[32,896]{1,0:T(8,128)(2,1)S(1)}, u32[]{:S(2)}, u32[]{:S(2)}) collective-permute-start(bf16[32,896]{1,0:T(8,128)(2,1)S(1)} %add_convert_fusion), channel_id=1, source_target_pairs={{0,48},{8,56},{16,32},{24,40},{32,16},{40,24},{48,0},{56,8},{64,11... | collective-permute-start | bytes 172040 | tf_op jit(solution)/shard_map/ppermute | solution.py:24
  42.1 0.3 collective-permute-start.16
  42.4 2.0 %collective-permute-done.14 = bf16[32,896]{1,0:T(8,128)(2,1)S(1)} collective-permute-done((bf16[32,896]{1,0:T(8,128)(2,1)S(1)}, bf16[32,896]{1,0:T(8,128)(2,1)S(1)}, u32[]{:S(2)}, u32[]{:S(2)}) %collective-permute-start.14) | collective-permute-done | bytes 57376 | tf_op jit(solution)/shard_map/ppermute | solution.py:24
  44.4 0.5 collective-permute-done.15
  44.9 0.3 collective-permute-done.16
  45.2 3.2 %collective-permute-start.17 = (bf16[4,32,896]{2,1,0:T(8,128)(2,1)S(1)}, bf16[4,32,896]{2,1,0:T(8,128)(2,1)S(1)}, u32[]{:S(2)}, u32[]{:S(2)}) collective-permute-start(bf16[4,32,896]{2,1,0:T(8,128)(2,1)S(1)} %pad_maximum_fusion.own_ref), channel_id=1, source_target_pairs={{0,8},{8,0},{16,24},{24,16},{32,40},{40,32},{48,56},{56,48},{64,72... | collective-permute-start | bytes 688136 | tf_op jit(solution)/shard_map/ppermute | solution.py:24
  48.4 0.2 shard_map.59.turned_ref
  48.7 0.9 %collective-permute-done.17.other_ref = bf16[4,32,896]{2,1,0:T(8,128)(2,1)S(1)} collective-permute-done((bf16[4,32,896]{2,1,0:T(8,128)(2,1)S(1)}, bf16[4,32,896]{2,1,0:T(8,128)(2,1)S(1)}, u32[]{:S(2)}, u32[]{:S(2)}) %collective-permute-start.17) | collective-permute-done | bytes 229408 | tf_op jit(solution)/shard_map/ppermute | solution.py:24
  49.6 2.6 %shard_map.60 = bf16[2,1280,896]{2,1,0:T(8,128)(2,1)} custom-call(s32[1]{0:T(128)} %bitcast.core_ref, s32[1]{0:T(128)} %bitcast.1.y_ref, bf16[4,32,896]{2,1,0:T(8,128)(2,1)S(1)} %pad_maximum_fusion.own_ref, bf16[4,32,896]{2,1,0:T(8,128)(2,1)S(1)} %collective-permute-done.17.other_ref, bf16[2,1280,256]{2,1,0:T(8,128)(2,1)S(1)} %shard_map.59.turned_ref), custom_call_target="tpu_custom_call" | custom-call | flops 1174405120 | bytes 6291456 | tf_op jit(solution)/shard_map/pallas_call | solution.py:267
  (23 shorter events, 0.4 us)
Async XLA Ops:
  0.0 11.1 %collective-permute-start = (bf16[2,16,1280]{2,1,0:T(8,128)(2,1)}, bf16[2,16,1280]{2,1,0:T(8,128)(2,1)S(1)}, u32[]{:S(2)}, u32[]{:S(2)}) collective-permute-start(bf16[2,16,1280]{2,1,0:T(8,128)(2,1)} %refs_3_.3), channel_id=1, source_target_pairs={{0,1},{1,0},{2,3},{3,2},{4,5},{5,4},{6,7},{7,6},{8,9},{9,8},{10,11... | collective-permute-start | bytes 245768 | tf_op jit(solution)/shard_map/ppermute | solution.py:28
  7.7 6.5 %collective-permute-start.1 = (bf16[2,16,1280]{2,1,0:T(8,128)(2,1)}, bf16[2,16,1280]{2,1,0:T(8,128)(2,1)S(1)}, u32[]{:S(2)}, u32[]{:S(2)}) collective-permute-start(bf16[2,16,1280]{2,1,0:T(8,128)(2,1)} %refs_3_.3), channel_id=1, source_target_pairs={{0,6},{1,7},{2,4},{3,5},{4,2},{5,3},{6,0},{7,1},{8,14},{9,15},{10,... | collective-permute-start | bytes 245768 | tf_op jit(solution)/shard_map/ppermute | solution.py:28
  10.2 6.6 %collective-permute-start.2 = (bf16[2,16,1280]{2,1,0:T(8,128)(2,1)}, bf16[2,16,1280]{2,1,0:T(8,128)(2,1)S(1)}, u32[]{:S(2)}, u32[]{:S(2)}) collective-permute-start(bf16[2,16,1280]{2,1,0:T(8,128)(2,1)} %refs_3_.3), channel_id=1, source_target_pairs={{0,4},{1,5},{2,6},{3,7},{4,0},{5,1},{6,2},{7,3},{8,12},{9,13},{10,... | collective-permute-start | bytes 245768 | tf_op jit(solution)/shard_map/ppermute | solution.py:28
  10.7 6.1 %collective-permute-start.3 = (bf16[2,16,1280]{2,1,0:T(8,128)(2,1)}, bf16[2,16,1280]{2,1,0:T(8,128)(2,1)S(1)}, u32[]{:S(2)}, u32[]{:S(2)}) collective-permute-start(bf16[2,16,1280]{2,1,0:T(8,128)(2,1)} %refs_3_.3), channel_id=1, source_target_pairs={{0,2},{1,3},{2,0},{3,1},{4,6},{5,7},{6,4},{7,5},{8,10},{9,11},{10,... | collective-permute-start | bytes 245768 | tf_op jit(solution)/shard_map/ppermute | solution.py:28
  11.0 3.5 %copy-start.1 = (f32[12,13,13]{2,1,0:T(8,128)S(1)}, f32[12,13,13]{2,1,0:T(8,128)}, u32[]{:S(2)}) copy-start(f32[12,13,13]{2,1,0:T(8,128)} %coupling_hbm.1) | copy-start | bytes 24340
  11.0 3.5 %copy-start.2 = (s32[12]{0:T(128)S(1)}, s32[12]{0:T(128)}, u32[]{:S(2)}) copy-start(s32[12]{0:T(128)} %offsets_hbm.1) | copy-start | bytes 148
  11.0 3.5 %copy-start.3 = (s32[12]{0:T(128)S(1)}, s32[12]{0:T(128)}, u32[]{:S(2)}) copy-start(s32[12]{0:T(128)} %counts_hbm.1) | copy-start | bytes 148
  11.1 5.8 %copy-start = (bf16[2,16,1280]{2,1,0:T(8,128)(2,1)S(1)}, bf16[2,16,1280]{2,1,0:T(8,128)(2,1)}, u32[]{:S(2)}) copy-start(bf16[2,16,1280]{2,1,0:T(8,128)(2,1)} %refs_3_.3) | copy-start | bytes 245764
  11.1 6.9 %collective-permute-start.4 = (bf16[2,16,1280]{2,1,0:T(8,128)(2,1)S(1)}, bf16[2,16,1280]{2,1,0:T(8,128)(2,1)S(1)}, u32[]{:S(2)}, u32[]{:S(2)}) collective-permute-start(bf16[2,16,1280]{2,1,0:T(8,128)(2,1)S(1)} %collective-permute-done.refs_3_.refs_7_), channel_id=1, source_target_pairs={{0,6},{1,7},{2,4},{3,5},{4,2},{5,3},{6,0},{7,1},{8,14},{9,15},{10,... | collective-permute-start | bytes 245768 | tf_op jit(solution)/shard_map/ppermute | solution.py:28
  13.7 5.1 %collective-permute-start.5 = (bf16[2,16,1280]{2,1,0:T(8,128)(2,1)S(1)}, bf16[2,16,1280]{2,1,0:T(8,128)(2,1)S(1)}, u32[]{:S(2)}, u32[]{:S(2)}) collective-permute-start(bf16[2,16,1280]{2,1,0:T(8,128)(2,1)S(1)} %collective-permute-done.refs_3_.refs_7_), channel_id=1, source_target_pairs={{0,4},{1,5},{2,6},{3,7},{4,0},{5,1},{6,2},{7,3},{8,12},{9,13},{10,... | collective-permute-start | bytes 245768 | tf_op jit(solution)/shard_map/ppermute | solution.py:28
  14.2 4.6 %collective-permute-start.6 = (bf16[2,16,1280]{2,1,0:T(8,128)(2,1)S(1)}, bf16[2,16,1280]{2,1,0:T(8,128)(2,1)S(1)}, u32[]{:S(2)}, u32[]{:S(2)}) collective-permute-start(bf16[2,16,1280]{2,1,0:T(8,128)(2,1)S(1)} %collective-permute-done.refs_3_.refs_7_), channel_id=1, source_target_pairs={{0,2},{1,3},{2,0},{3,1},{4,6},{5,7},{6,4},{7,5},{8,10},{9,11},{10,... | collective-permute-start | bytes 245768 | tf_op jit(solution)/shard_map/ppermute | solution.py:28
  19.9 4.5 %collective-permute-start.7 = (f32[128,896]{1,0:T(8,128)S(1)}, f32[128,896]{1,0:T(8,128)S(1)}, u32[]{:S(2)}, u32[]{:S(2)}) collective-permute-start(f32[128,896]{1,0:T(8,128)S(1)} %get-tuple-element.14), channel_id=1, source_target_pairs={{0,8},{8,0},{16,24},{24,16},{32,40},{40,32},{48,56},{56,48},{64,72... | collective-permute-start | bytes 1376264 | tf_op jit(solution)/shard_map/ppermute | solution.py:24
  24.5 4.6 %collective-permute-start.10 = (bf16[32,896]{1,0:T(8,128)(2,1)S(1)}, bf16[32,896]{1,0:T(8,128)(2,1)S(1)}, u32[]{:S(2)}, u32[]{:S(2)}) collective-permute-start(bf16[32,896]{1,0:T(8,128)(2,1)S(1)} %get-tuple-element.18), channel_id=1, source_target_pairs={{0,32},{8,40},{16,48},{24,56},{32,0},{40,8},{48,16},{56,24},{64,96... | collective-permute-start | bytes 172040 | tf_op jit(solution)/shard_map/ppermute | solution.py:24
  27.5 4.2 %collective-permute-start.8 = (bf16[32,896]{1,0:T(8,128)(2,1)S(1)}, bf16[32,896]{1,0:T(8,128)(2,1)S(1)}, u32[]{:S(2)}, u32[]{:S(2)}) collective-permute-start(bf16[32,896]{1,0:T(8,128)(2,1)S(1)} %get-tuple-element.17), channel_id=1, source_target_pairs={{0,48},{8,56},{16,32},{24,40},{32,16},{40,24},{48,0},{56,8},{64,11... | collective-permute-start | bytes 172040 | tf_op jit(solution)/shard_map/ppermute | solution.py:24
  28.3 3.5 %collective-permute-start.9 = (bf16[32,896]{1,0:T(8,128)(2,1)S(1)}, bf16[32,896]{1,0:T(8,128)(2,1)S(1)}, u32[]{:S(2)}, u32[]{:S(2)}) collective-permute-start(bf16[32,896]{1,0:T(8,128)(2,1)S(1)} %get-tuple-element.19), channel_id=1, source_target_pairs={{0,16},{8,24},{16,0},{24,8},{32,48},{40,56},{48,32},{56,40},{64,80... | collective-permute-start | bytes 172040 | tf_op jit(solution)/shard_map/ppermute | solution.py:24
  31.8 5.0 %collective-permute-start.11 = (bf16[32,896]{1,0:T(8,128)(2,1)S(1)}, bf16[32,896]{1,0:T(8,128)(2,1)S(1)}, u32[]{:S(2)}, u32[]{:S(2)}) collective-permute-start(bf16[32,896]{1,0:T(8,128)(2,1)S(1)} %fusion.2), channel_id=1, source_target_pairs={{0,192},{8,200},{16,208},{24,216},{32,224},{40,232},{48,240},{56,2... | collective-permute-start | bytes 172040 | tf_op jit(solution)/shard_map/ppermute | solution.py:24
  33.5 3.7 %collective-permute-start.12 = (bf16[32,896]{1,0:T(8,128)(2,1)S(1)}, bf16[32,896]{1,0:T(8,128)(2,1)S(1)}, u32[]{:S(2)}, u32[]{:S(2)}) collective-permute-start(bf16[32,896]{1,0:T(8,128)(2,1)S(1)} %fusion.2), channel_id=1, source_target_pairs={{0,64},{8,72},{16,80},{24,88},{32,96},{40,104},{48,112},{56,120},{... | collective-permute-start | bytes 172040 | tf_op jit(solution)/shard_map/ppermute | solution.py:24
  33.8 5.8 %collective-permute-start.13 = (bf16[32,896]{1,0:T(8,128)(2,1)S(1)}, bf16[32,896]{1,0:T(8,128)(2,1)S(1)}, u32[]{:S(2)}, u32[]{:S(2)}) collective-permute-start(bf16[32,896]{1,0:T(8,128)(2,1)S(1)} %fusion.2), channel_id=1, source_target_pairs={{0,128},{8,136},{16,144},{24,152},{32,160},{40,168},{48,176},{56,1... | collective-permute-start | bytes 172040 | tf_op jit(solution)/shard_map/ppermute | solution.py:24
  39.7 4.7 %collective-permute-start.14 = (bf16[32,896]{1,0:T(8,128)(2,1)S(1)}, bf16[32,896]{1,0:T(8,128)(2,1)S(1)}, u32[]{:S(2)}, u32[]{:S(2)}) collective-permute-start(bf16[32,896]{1,0:T(8,128)(2,1)S(1)} %add_convert_fusion), channel_id=1, source_target_pairs={{0,32},{8,40},{16,48},{24,56},{32,0},{40,8},{48,16},{56,24},{64,96... | collective-permute-start | bytes 172040 | tf_op jit(solution)/shard_map/ppermute | solution.py:24
  39.8 5.1 %collective-permute-start.15 = (bf16[32,896]{1,0:T(8,128)(2,1)S(1)}, bf16[32,896]{1,0:T(8,128)(2,1)S(1)}, u32[]{:S(2)}, u32[]{:S(2)}) collective-permute-start(bf16[32,896]{1,0:T(8,128)(2,1)S(1)} %add_convert_fusion), channel_id=1, source_target_pairs={{0,48},{8,56},{16,32},{24,40},{32,16},{40,24},{48,0},{56,8},{64,11... | collective-permute-start | bytes 172040 | tf_op jit(solution)/shard_map/ppermute | solution.py:24
  42.1 3.1 %collective-permute-start.16 = (bf16[32,896]{1,0:T(8,128)(2,1)S(1)}, bf16[32,896]{1,0:T(8,128)(2,1)S(1)}, u32[]{:S(2)}, u32[]{:S(2)}) collective-permute-start(bf16[32,896]{1,0:T(8,128)(2,1)S(1)} %add_convert_fusion), channel_id=1, source_target_pairs={{0,16},{8,24},{16,0},{24,8},{32,48},{40,56},{48,32},{56,40},{64,80... | collective-permute-start | bytes 172040 | tf_op jit(solution)/shard_map/ppermute | solution.py:24
  45.2 4.3 %collective-permute-start.17 = (bf16[4,32,896]{2,1,0:T(8,128)(2,1)S(1)}, bf16[4,32,896]{2,1,0:T(8,128)(2,1)S(1)}, u32[]{:S(2)}, u32[]{:S(2)}) collective-permute-start(bf16[4,32,896]{2,1,0:T(8,128)(2,1)S(1)} %pad_maximum_fusion.own_ref), channel_id=1, source_target_pairs={{0,8},{8,0},{16,24},{24,16},{32,40},{40,32},{48,56},{56,48},{64,72... | collective-permute-start | bytes 688136 | tf_op jit(solution)/shard_map/ppermute | solution.py:24

commit v6 on v5

--- a/solution.py
+++ b/solution.py
@@ -186,7 +186,7 @@
     def sums(out_refs):
         parts = coupled_parts(1, pieces, left_ref, waves_ref, rows_ref)
         for k in range(2):
-            out_refs[k][...] = parts[k] + near_ref[k]
+            out_refs[k][...] = (parts[k] + near_ref[k]).astype(out_refs[k].dtype)
 
     @pl.when(core_ref[0] == 0)
     def _():
@@ -198,10 +198,10 @@
 
 
 def project_far(core, near, left, waves, pieces):
-    half = jax.ShapeDtypeStruct((NP, NB_DEV), F32)
+    halves = [jax.ShapeDtypeStruct((NP, NB_DEV), dtype) for dtype in (F32, BF16)]
     return pl.pallas_call(
         far_kernel,
-        out_shape=(half, half),
+        out_shape=halves,
         in_specs=[smem()] + [vmem()] * 7,
         out_specs=(vmem(), vmem()),
         scratch_shapes=[pltpu.VMEM((NP, NPW_DEV), BF16)],
@@ -236,16 +236,16 @@
     )(*pieces)
 
 
-def spread_kernel(
-    core_ref, y_ref, own_ref, other_ref, turned_ref, out_ref, right_ref, result_ref, sem
-):
+def spread_kernel(core_ref, y_ref, *refs):
+    own_ref, other_ref = refs[:4], refs[4:8]
+    turned_ref, out_ref, right_ref, result_ref, sem = refs[8:]
     core, y = core_ref[0], y_ref[0]
     for s, slot in enumerate(SLOTS):
         at = jnp.bitwise_xor(y, slot) * CHUNK
         own_at = pl.multiple_of(core * NP + at, CHUNK)
         other_at = pl.multiple_of((1 - core) * NP + at, CHUNK)
-        right_ref[pl.ds(own_at, CHUNK), :] = own_ref[s]
-        right_ref[pl.ds(other_at, CHUNK), :] = other_ref[s]
+        right_ref[pl.ds(own_at, CHUNK), :] = own_ref[s][...]
+        right_ref[pl.ds(other_at, CHUNK), :] = other_ref[s][...]
     right = right_ref[...]
     copies = []
     for k in range(2):
@@ -267,7 +267,7 @@
     return pl.pallas_call(
         spread_kernel,
         out_shape=jax.ShapeDtypeStruct((2, NPW_DEV, NB_DEV), BF16),
-        in_specs=[smem(), smem()] + [vmem()] * 3,
+        in_specs=[smem(), smem()] + [vmem()] * 9,
         out_specs=pl.BlockSpec(memory_space=pltpu.HBM),
         scratch_shapes=[
             pltpu.VMEM((2 * NP, NB_DEV), BF16),
@@ -276,7 +276,7 @@
         ],
         compiler_params=params(16),
         cost_estimate=cost(8 * NP * NPW_DEV * NB_DEV, 6 * MIB),
-    )(core, y, own, other, turned)
+    )(core, y, *own, *other, turned)
 
 
 def shards(waves, projectors, coupling, offsets, counts):
@@ -292,7 +292,7 @@
     sums = project_near(left, waves, near)
     keep, send = project_far(core, sums, left, waves, far)
     turned = turn(near + far)
-    total = (keep + over_pw(send, 1)).reshape(4, CHUNK, NB_DEV)
+    total = (keep + over_pw(send, 1).astype(F32)).reshape(4, CHUNK, NB_DEV)
 
     sums = total[0]
     for arrived in [over_pw(total[s].astype(BF16), 2 * s) for s in (3, 1, 2)]:
@@ -301,8 +301,8 @@
     for arrived in [over_pw(sent, 8 * s) for s in (3, 1, 2)]:
         sums = sums + arrived.astype(F32)
     mine = sums.astype(BF16)
-    own = jnp.stack([mine] + [over_pw(mine, 2 * s) for s in SLOTS[1:]])
-    other = over_pw(own, 1)
+    own = [mine] + [over_pw(mine, 2 * s) for s in SLOTS[1:]]
+    other = [over_pw(chunk, 1) for chunk in own]
     return spread_back(core, y, own, other, turned)
 
 

time: 52.4 us -> 52.1 us (level)
  waiting for transfers between devices: 13.5 us -> 10.5 us
  starting transfers between devices: 30.7 us -> 33.4 us
    ppermute x11 -> x14, waiting for transfers between devices: 12.8 us -> 9.75 us  [over_pw(): return lax.ppermute(x, 'pw', [(i, i ^ bits) for i in range(32)])]
    ppermute x11 -> x14, starting transfers between devices: 16.4 us -> 19.1 us  [over_pw(): return lax.ppermute(x, 'pw', [(i, i ^ bits) for i in range(32)])]
  transfers between devices with their start and end apart: 18 -> 21, of which waited for: 11 -> 9; matrix products, arithmetic and copies ran while one was open for 0% -> 0% of each run, Pallas kernels for 7% -> 7%
where the time goes in v6:
time: 52.1 us; the launch traced here: 51.9 us
  starting transfers between devices  33.4 us (64%)
  waiting for transfers between devices  10.5 us (20%)
  Pallas kernels  7.56 us (15%)
    ppermute x14, starting transfers between devices, over_pw(): return lax.ppermute(x, 'pw', [(i, i ^ bits) for i in range(32)])  19.1 us
    ppermute x7, starting transfers between devices, over_band(): return lax.ppermute(x, 'band', [(i, i ^ bits) for i in range(8)])  14.3 us
    ppermute x14, waiting for transfers between devices, over_pw(): return lax.ppermute(x, 'pw', [(i, i ^ bits) for i in range(32)])  9.75 us
    pallas_call x1, Pallas kernels, spread_back(): pl.pallas_call(spread_kernel, out_shape=jax.ShapeDtypeStruct((2, NPW_DEV,...  2.58 us
    pallas_call x1, Pallas kernels, ahead(): pl.pallas_call(ahead_kernel, out_shape=(jax.ShapeDtypeStruct((2, NP, 3 *...  2.34 us
    pallas_call x1, Pallas kernels, project_near(): pl.pallas_call(near_kernel, out_shape=jax.ShapeDtypeStruct((2, NP, NB_DEV...  1.17 us
    pallas_call x1, Pallas kernels, project_far(): pl.pallas_call(far_kernel, out_shape=halves, in_specs=[smem()] + [vmem()]...  1.15 us
  transfers between devices with their start and end apart: 21, of which 9 were waited for; matrix products, arithmetic and copies ran while one was open for 0% of the time, Pallas kernels for 7%

profile of v6, /device:TPU:1, one launch (start us, length us, event | category | flops | bytes accessed | tf_op | source)
XLA Modules:
  0.0 51.9 jit_solution(10106088362475858589)
XLA Ops:
  0.0 7.7 %collective-permute-start = (bf16[2,16,1280]{2,1,0:T(8,128)(2,1)}, bf16[2,16,1280]{2,1,0:T(8,128)(2,1)S(1)}, u32[]{:S(2)}, u32[]{:S(2)}) collective-permute-start(bf16[2,16,1280]{2,1,0:T(8,128)(2,1)} %refs_3_.3), channel_id=1, source_target_pairs={{0,1},{1,0},{2,3},{3,2},{4,5},{5,4},{6,7},{7,6},{8,9},{9,8},{10,11... | collective-permute-start | bytes 245768 | tf_op jit(solution)/shard_map/ppermute | solution.py:28
  7.7 2.5 %collective-permute-start.1 = (bf16[2,16,1280]{2,1,0:T(8,128)(2,1)}, bf16[2,16,1280]{2,1,0:T(8,128)(2,1)S(1)}, u32[]{:S(2)}, u32[]{:S(2)}) collective-permute-start(bf16[2,16,1280]{2,1,0:T(8,128)(2,1)} %refs_3_.3), channel_id=1, source_target_pairs={{0,6},{1,7},{2,4},{3,5},{4,2},{5,3},{6,0},{7,1},{8,14},{9,15},{10,... | collective-permute-start | bytes 245768 | tf_op jit(solution)/shard_map/ppermute | solution.py:28
  10.2 0.5 %collective-permute-start.2 = (bf16[2,16,1280]{2,1,0:T(8,128)(2,1)}, bf16[2,16,1280]{2,1,0:T(8,128)(2,1)S(1)}, u32[]{:S(2)}, u32[]{:S(2)}) collective-permute-start(bf16[2,16,1280]{2,1,0:T(8,128)(2,1)} %refs_3_.3), channel_id=1, source_target_pairs={{0,4},{1,5},{2,6},{3,7},{4,0},{5,1},{6,2},{7,3},{8,12},{9,13},{10,... | collective-permute-start | bytes 245768 | tf_op jit(solution)/shard_map/ppermute | solution.py:28
  10.7 0.3 collective-permute-start.3
  11.1 2.6 %collective-permute-start.4 = (bf16[2,16,1280]{2,1,0:T(8,128)(2,1)S(1)}, bf16[2,16,1280]{2,1,0:T(8,128)(2,1)S(1)}, u32[]{:S(2)}, u32[]{:S(2)}) collective-permute-start(bf16[2,16,1280]{2,1,0:T(8,128)(2,1)S(1)} %collective-permute-done.refs_3_.refs_7_), channel_id=1, source_target_pairs={{0,6},{1,7},{2,4},{3,5},{4,2},{5,3},{6,0},{7,1},{8,14},{9,15},{10,... | collective-permute-start | bytes 245768 | tf_op jit(solution)/shard_map/ppermute | solution.py:28
  13.7 0.5 %collective-permute-start.5 = (bf16[2,16,1280]{2,1,0:T(8,128)(2,1)S(1)}, bf16[2,16,1280]{2,1,0:T(8,128)(2,1)S(1)}, u32[]{:S(2)}, u32[]{:S(2)}) collective-permute-start(bf16[2,16,1280]{2,1,0:T(8,128)(2,1)S(1)} %collective-permute-done.refs_3_.refs_7_), channel_id=1, source_target_pairs={{0,4},{1,5},{2,6},{3,7},{4,0},{5,1},{6,2},{7,3},{8,12},{9,13},{10,... | collective-permute-start | bytes 245768 | tf_op jit(solution)/shard_map/ppermute | solution.py:28
  14.2 0.3 collective-permute-start.6
  14.5 2.3 %shard_map.56 = (bf16[2,128,192]{2,1,0:T(8,128)(2,1)S(1)}, bf16[2,1280,896]{2,1,0:T(8,128)(2,1)S(1)}) custom-call(bf16[2,128,128]{2,1,0:T(8,128)(2,1)S(1)} %shard_map.55.pick_ref, s32[12]{0:T(128)S(1)} %copy-done.2, s32[12]{0:T(128)S(1)} %copy-done.3, f32[12,13,13]{2,1,0:T(8,128)S(1)} %copy-done.1, bf16[2,1280,896]{2,1,0:T(8,128)(2,1)} %waves_hbm.1), custom_call_target="tpu_custom_call" | custom-call | flops 2000000000 | bytes 8388608 | tf_op jit(solution)/shard_map/pallas_call | solution.py:128
  16.9 1.2 %shard_map.57.near_ref = f32[2,128,896]{2,1,0:T(8,128)S(1)} custom-call(bf16[2,128,192]{2,1,0:T(8,128)(2,1)S(1)} %get-tuple-element.11.left_ref, bf16[2,1280,896]{2,1,0:T(8,128)(2,1)S(1)} %get-tuple-element.12.waves_ref, bf16[2,16,1280]{2,1,0:T(8,128)(2,1)S(1)} %collective-permute-done.1.refs_0_, bf16[2,16,1280]{2,1,0:T(8,128)(2,1)S(1)} %collective-permute-done.2.refs_1_, ...), custom_call_target="tpu_custom_call" | custom-call | flops 587202560 | bytes 6291456 | tf_op jit(solution)/shard_map/pallas_call | solution.py:172
  18.1 0.7 %collective-permute-done.5.refs_1_.refs_5_ = bf16[2,16,1280]{2,1,0:T(8,128)(2,1)S(1)} collective-permute-done((bf16[2,16,1280]{2,1,0:T(8,128)(2,1)S(1)}, bf16[2,16,1280]{2,1,0:T(8,128)(2,1)S(1)}, u32[]{:S(2)}, u32[]{:S(2)}) %collective-permute-start.5) | collective-permute-done | bytes 81952 | tf_op jit(solution)/shard_map/ppermute | solution.py:28
  18.8 1.1 %shard_map.58 = (f32[128,896]{1,0:T(8,128)S(1)}, bf16[128,896]{1,0:T(8,128)(2,1)S(1)}) custom-call(s32[1]{0:T(128)} %bitcast.core_ref, f32[2,128,896]{2,1,0:T(8,128)S(1)} %shard_map.57.near_ref, bf16[2,128,192]{2,1,0:T(8,128)(2,1)S(1)} %get-tuple-element.11.left_ref, bf16[2,1280,896]{2,1,0:T(8,128)(2,1)S(1)} %get-tuple-element.12.waves_ref, ...), custom_call_target="tpu_custom_call" | custom-call | flops 587202560 | bytes 6291456 | tf_op jit(solution)/shard_map/pallas_call | solution.py:202
  19.9 3.0 %collective-permute-start.7 = (bf16[128,896]{1,0:T(8,128)(2,1)S(1)}, bf16[128,896]{1,0:T(8,128)(2,1)S(1)}, u32[]{:S(2)}, u32[]{:S(2)}) collective-permute-start(bf16[128,896]{1,0:T(8,128)(2,1)S(1)} %get-tuple-element.14), channel_id=1, source_target_pairs={{0,8},{8,0},{16,24},{24,16},{32,40},{40,32},{48,56},{56,48},{64,72... | collective-permute-start | bytes 688136 | tf_op jit(solution)/shard_map/ppermute | solution.py:24
  23.0 1.1 %collective-permute-done.7 = bf16[128,896]{1,0:T(8,128)(2,1)S(1)} collective-permute-done((bf16[128,896]{1,0:T(8,128)(2,1)S(1)}, bf16[128,896]{1,0:T(8,128)(2,1)S(1)}, u32[]{:S(2)}, u32[]{:S(2)}) %collective-permute-start.7) | collective-permute-done | bytes 229408 | tf_op jit(solution)/shard_map/ppermute | solution.py:24
  24.2 3.0 %collective-permute-start.10 = (bf16[32,896]{1,0:T(8,128)(2,1)S(1)}, bf16[32,896]{1,0:T(8,128)(2,1)S(1)}, u32[]{:S(2)}, u32[]{:S(2)}) collective-permute-start(bf16[32,896]{1,0:T(8,128)(2,1)S(1)} %get-tuple-element.18), channel_id=1, source_target_pairs={{0,32},{8,40},{16,48},{24,56},{32,0},{40,8},{48,16},{56,24},{64,96... | collective-permute-start | bytes 172040 | tf_op jit(solution)/shard_map/ppermute | solution.py:24
  27.2 0.8 %collective-permute-start.8 = (bf16[32,896]{1,0:T(8,128)(2,1)S(1)}, bf16[32,896]{1,0:T(8,128)(2,1)S(1)}, u32[]{:S(2)}, u32[]{:S(2)}) collective-permute-start(bf16[32,896]{1,0:T(8,128)(2,1)S(1)} %get-tuple-element.17), channel_id=1, source_target_pairs={{0,48},{8,56},{16,32},{24,40},{32,16},{40,24},{48,0},{56,8},{64,11... | collective-permute-start | bytes 172040 | tf_op jit(solution)/shard_map/ppermute | solution.py:24
  27.9 0.8 %collective-permute-done.10 = bf16[32,896]{1,0:T(8,128)(2,1)S(1)} collective-permute-done((bf16[32,896]{1,0:T(8,128)(2,1)S(1)}, bf16[32,896]{1,0:T(8,128)(2,1)S(1)}, u32[]{:S(2)}, u32[]{:S(2)}) %collective-permute-start.10) | collective-permute-done | bytes 57376 | tf_op jit(solution)/shard_map/ppermute | solution.py:24
  28.8 2.6 %collective-permute-done.8 = bf16[32,896]{1,0:T(8,128)(2,1)S(1)} collective-permute-done((bf16[32,896]{1,0:T(8,128)(2,1)S(1)}, bf16[32,896]{1,0:T(8,128)(2,1)S(1)}, u32[]{:S(2)}, u32[]{:S(2)}) %collective-permute-start.8) | collective-permute-done | bytes 57376 | tf_op jit(solution)/shard_map/ppermute | solution.py:24
  31.4 1.7 %collective-permute-start.11 = (bf16[32,896]{1,0:T(8,128)(2,1)S(1)}, bf16[32,896]{1,0:T(8,128)(2,1)S(1)}, u32[]{:S(2)}, u32[]{:S(2)}) collective-permute-start(bf16[32,896]{1,0:T(8,128)(2,1)S(1)} %fusion.2), channel_id=1, source_target_pairs={{0,192},{8,200},{16,208},{24,216},{32,224},{40,232},{48,240},{56,2... | collective-permute-start | bytes 172040 | tf_op jit(solution)/shard_map/ppermute | solution.py:24
  33.2 0.3 collective-permute-start.12
  33.5 1.6 %collective-permute-start.13 = (bf16[32,896]{1,0:T(8,128)(2,1)S(1)}, bf16[32,896]{1,0:T(8,128)(2,1)S(1)}, u32[]{:S(2)}, u32[]{:S(2)}) collective-permute-start(bf16[32,896]{1,0:T(8,128)(2,1)S(1)} %fusion.2), channel_id=1, source_target_pairs={{0,128},{8,136},{16,144},{24,152},{32,160},{40,168},{48,176},{56,1... | collective-permute-start | bytes 172040 | tf_op jit(solution)/shard_map/ppermute | solution.py:24
  35.1 1.4 %collective-permute-done.11 = bf16[32,896]{1,0:T(8,128)(2,1)S(1)} collective-permute-done((bf16[32,896]{1,0:T(8,128)(2,1)S(1)}, bf16[32,896]{1,0:T(8,128)(2,1)S(1)}, u32[]{:S(2)}, u32[]{:S(2)}) %collective-permute-start.11) | collective-permute-done | bytes 57376 | tf_op jit(solution)/shard_map/ppermute | solution.py:24
  36.5 0.4 collective-permute-done.12
  36.9 2.4 %collective-permute-done.13 = bf16[32,896]{1,0:T(8,128)(2,1)S(1)} collective-permute-done((bf16[32,896]{1,0:T(8,128)(2,1)S(1)}, bf16[32,896]{1,0:T(8,128)(2,1)S(1)}, u32[]{:S(2)}, u32[]{:S(2)}) %collective-permute-start.13) | collective-permute-done | bytes 57376 | tf_op jit(solution)/shard_map/ppermute | solution.py:24
  39.4 2.3 %collective-permute-start.15 = (bf16[32,896]{1,0:T(8,128)(2,1)S(1)}, bf16[32,896]{1,0:T(8,128)(2,1)S(1)}, u32[]{:S(2)}, u32[]{:S(2)}) collective-permute-start(bf16[32,896]{1,0:T(8,128)(2,1)S(1)} %add_convert_fusion.refs_0_), channel_id=1, source_target_pairs={{0,48},{8,56},{16,32},{24,40},{32,16},{40,24},{48,0},{56,8},{64,11... | collective-permute-start | bytes 172040 | tf_op jit(solution)/shard_map/ppermute | solution.py:24
  41.7 0.3 collective-permute-start.16
  42.0 2.5 %collective-permute-start.17 = (bf16[32,896]{1,0:T(8,128)(2,1)S(1)}, bf16[32,896]{1,0:T(8,128)(2,1)S(1)}, u32[]{:S(2)}, u32[]{:S(2)}) collective-permute-start(bf16[32,896]{1,0:T(8,128)(2,1)S(1)} %add_convert_fusion.refs_0_), channel_id=1, source_target_pairs={{0,8},{8,0},{16,24},{24,16},{32,40},{40,32},{48,56},{56,48},{64,72... | collective-permute-start | bytes 172040 | tf_op jit(solution)/shard_map/ppermute | solution.py:24
  44.5 2.2 %collective-permute-start.18 = (bf16[32,896]{1,0:T(8,128)(2,1)S(1)}, bf16[32,896]{1,0:T(8,128)(2,1)S(1)}, u32[]{:S(2)}, u32[]{:S(2)}) collective-permute-start(bf16[32,896]{1,0:T(8,128)(2,1)S(1)} %collective-permute-done.14.refs_1_), channel_id=1, source_target_pairs={{0,8},{8,0},{16,24},{24,16},{32,40},{40,32},{48,56},{56,48},{64,72... | collective-permute-start | bytes 172040 | tf_op jit(solution)/shard_map/ppermute | solution.py:24
  46.7 1.2 %collective-permute-start.19 = (bf16[32,896]{1,0:T(8,128)(2,1)S(1)}, bf16[32,896]{1,0:T(8,128)(2,1)S(1)}, u32[]{:S(2)}, u32[]{:S(2)}) collective-permute-start(bf16[32,896]{1,0:T(8,128)(2,1)S(1)} %collective-permute-done.15.refs_2_), channel_id=1, source_target_pairs={{0,8},{8,0},{16,24},{24,16},{32,40},{40,32},{48,56},{56,48},{64,72... | collective-permute-start | bytes 172040 | tf_op jit(solution)/shard_map/ppermute | solution.py:24
  48.0 0.2 shard_map.59.refs_8_
  48.2 0.6 %collective-permute-done.19.refs_6_ = bf16[32,896]{1,0:T(8,128)(2,1)S(1)} collective-permute-done((bf16[32,896]{1,0:T(8,128)(2,1)S(1)}, bf16[32,896]{1,0:T(8,128)(2,1)S(1)}, u32[]{:S(2)}, u32[]{:S(2)}) %collective-permute-start.19) | collective-permute-done | bytes 57376 | tf_op jit(solution)/shard_map/ppermute | solution.py:24
  48.8 0.4 collective-permute-done.20.refs_7_
  49.2 2.6 %shard_map.60 = bf16[2,1280,896]{2,1,0:T(8,128)(2,1)} custom-call(s32[1]{0:T(128)} %bitcast.core_ref, s32[1]{0:T(128)} %bitcast.1.y_ref, bf16[32,896]{1,0:T(8,128)(2,1)S(1)} %add_convert_fusion.refs_0_, bf16[32,896]{1,0:T(8,128)(2,1)S(1)} %collective-permute-done.14.refs_1_, bf16[32,896]{1,0:T(8,128)(2,1)S(1)} %collective-permute-done.15.refs_2_, ...), custom_call_target="tpu_custom_call" | custom-call | flops 1174405120 | bytes 6291456 | tf_op jit(solution)/shard_map/pallas_call | solution.py:267
  (28 shorter events, 0.4 us)
Async XLA Ops:
  0.0 11.1 %collective-permute-start = (bf16[2,16,1280]{2,1,0:T(8,128)(2,1)}, bf16[2,16,1280]{2,1,0:T(8,128)(2,1)S(1)}, u32[]{:S(2)}, u32[]{:S(2)}) collective-permute-start(bf16[2,16,1280]{2,1,0:T(8,128)(2,1)} %refs_3_.3), channel_id=1, source_target_pairs={{0,1},{1,0},{2,3},{3,2},{4,5},{5,4},{6,7},{7,6},{8,9},{9,8},{10,11... | collective-permute-start | bytes 245768 | tf_op jit(solution)/shard_map/ppermute | solution.py:28
  7.7 6.5 %collective-permute-start.1 = (bf16[2,16,1280]{2,1,0:T(8,128)(2,1)}, bf16[2,16,1280]{2,1,0:T(8,128)(2,1)S(1)}, u32[]{:S(2)}, u32[]{:S(2)}) collective-permute-start(bf16[2,16,1280]{2,1,0:T(8,128)(2,1)} %refs_3_.3), channel_id=1, source_target_pairs={{0,6},{1,7},{2,4},{3,5},{4,2},{5,3},{6,0},{7,1},{8,14},{9,15},{10,... | collective-permute-start | bytes 245768 | tf_op jit(solution)/shard_map/ppermute | solution.py:28
  10.2 6.6 %collective-permute-start.2 = (bf16[2,16,1280]{2,1,0:T(8,128)(2,1)}, bf16[2,16,1280]{2,1,0:T(8,128)(2,1)S(1)}, u32[]{:S(2)}, u32[]{:S(2)}) collective-permute-start(bf16[2,16,1280]{2,1,0:T(8,128)(2,1)} %refs_3_.3), channel_id=1, source_target_pairs={{0,4},{1,5},{2,6},{3,7},{4,0},{5,1},{6,2},{7,3},{8,12},{9,13},{10,... | collective-permute-start | bytes 245768 | tf_op jit(solution)/shard_map/ppermute | solution.py:28
  10.7 6.1 %collective-permute-start.3 = (bf16[2,16,1280]{2,1,0:T(8,128)(2,1)}, bf16[2,16,1280]{2,1,0:T(8,128)(2,1)S(1)}, u32[]{:S(2)}, u32[]{:S(2)}) collective-permute-start(bf16[2,16,1280]{2,1,0:T(8,128)(2,1)} %refs_3_.3), channel_id=1, source_target_pairs={{0,2},{1,3},{2,0},{3,1},{4,6},{5,7},{6,4},{7,5},{8,10},{9,11},{10,... | collective-permute-start | bytes 245768 | tf_op jit(solution)/shard_map/ppermute | solution.py:28
  11.0 3.5 %copy-start.1 = (f32[12,13,13]{2,1,0:T(8,128)S(1)}, f32[12,13,13]{2,1,0:T(8,128)}, u32[]{:S(2)}) copy-start(f32[12,13,13]{2,1,0:T(8,128)} %coupling_hbm.1) | copy-start | bytes 24340
  11.0 3.5 %copy-start.2 = (s32[12]{0:T(128)S(1)}, s32[12]{0:T(128)}, u32[]{:S(2)}) copy-start(s32[12]{0:T(128)} %offsets_hbm.1) | copy-start | bytes 148
  11.0 3.5 %copy-start.3 = (s32[12]{0:T(128)S(1)}, s32[12]{0:T(128)}, u32[]{:S(2)}) copy-start(s32[12]{0:T(128)} %counts_hbm.1) | copy-start | bytes 148
  11.1 5.8 %copy-start = (bf16[2,16,1280]{2,1,0:T(8,128)(2,1)S(1)}, bf16[2,16,1280]{2,1,0:T(8,128)(2,1)}, u32[]{:S(2)}) copy-start(bf16[2,16,1280]{2,1,0:T(8,128)(2,1)} %refs_3_.3) | copy-start | bytes 245764
  11.1 6.9 %collective-permute-start.4 = (bf16[2,16,1280]{2,1,0:T(8,128)(2,1)S(1)}, bf16[2,16,1280]{2,1,0:T(8,128)(2,1)S(1)}, u32[]{:S(2)}, u32[]{:S(2)}) collective-permute-start(bf16[2,16,1280]{2,1,0:T(8,128)(2,1)S(1)} %collective-permute-done.refs_3_.refs_7_), channel_id=1, source_target_pairs={{0,6},{1,7},{2,4},{3,5},{4,2},{5,3},{6,0},{7,1},{8,14},{9,15},{10,... | collective-permute-start | bytes 245768 | tf_op jit(solution)/shard_map/ppermute | solution.py:28
  13.7 5.1 %collective-permute-start.5 = (bf16[2,16,1280]{2,1,0:T(8,128)(2,1)S(1)}, bf16[2,16,1280]{2,1,0:T(8,128)(2,1)S(1)}, u32[]{:S(2)}, u32[]{:S(2)}) collective-permute-start(bf16[2,16,1280]{2,1,0:T(8,128)(2,1)S(1)} %collective-permute-done.refs_3_.refs_7_), channel_id=1, source_target_pairs={{0,4},{1,5},{2,6},{3,7},{4,0},{5,1},{6,2},{7,3},{8,12},{9,13},{10,... | collective-permute-start | bytes 245768 | tf_op jit(solution)/shard_map/ppermute | solution.py:28
  14.2 4.6 %collective-permute-start.6 = (bf16[2,16,1280]{2,1,0:T(8,128)(2,1)S(1)}, bf16[2,16,1280]{2,1,0:T(8,128)(2,1)S(1)}, u32[]{:S(2)}, u32[]{:S(2)}) collective-permute-start(bf16[2,16,1280]{2,1,0:T(8,128)(2,1)S(1)} %collective-permute-done.refs_3_.refs_7_), channel_id=1, source_target_pairs={{0,2},{1,3},{2,0},{3,1},{4,6},{5,7},{6,4},{7,5},{8,10},{9,11},{10,... | collective-permute-start | bytes 245768 | tf_op jit(solution)/shard_map/ppermute | solution.py:28
  19.9 4.1 %collective-permute-start.7 = (bf16[128,896]{1,0:T(8,128)(2,1)S(1)}, bf16[128,896]{1,0:T(8,128)(2,1)S(1)}, u32[]{:S(2)}, u32[]{:S(2)}) collective-permute-start(bf16[128,896]{1,0:T(8,128)(2,1)S(1)} %get-tuple-element.14), channel_id=1, source_target_pairs={{0,8},{8,0},{16,24},{24,16},{32,40},{40,32},{48,56},{56,48},{64,72... | collective-permute-start | bytes 688136 | tf_op jit(solution)/shard_map/ppermute | solution.py:24
  24.2 4.6 %collective-permute-start.10 = (bf16[32,896]{1,0:T(8,128)(2,1)S(1)}, bf16[32,896]{1,0:T(8,128)(2,1)S(1)}, u32[]{:S(2)}, u32[]{:S(2)}) collective-permute-start(bf16[32,896]{1,0:T(8,128)(2,1)S(1)} %get-tuple-element.18), channel_id=1, source_target_pairs={{0,32},{8,40},{16,48},{24,56},{32,0},{40,8},{48,16},{56,24},{64,96... | collective-permute-start | bytes 172040 | tf_op jit(solution)/shard_map/ppermute | solution.py:24
  27.2 4.2 %collective-permute-start.8 = (bf16[32,896]{1,0:T(8,128)(2,1)S(1)}, bf16[32,896]{1,0:T(8,128)(2,1)S(1)}, u32[]{:S(2)}, u32[]{:S(2)}) collective-permute-start(bf16[32,896]{1,0:T(8,128)(2,1)S(1)} %get-tuple-element.17), channel_id=1, source_target_pairs={{0,48},{8,56},{16,32},{24,40},{32,16},{40,24},{48,0},{56,8},{64,11... | collective-permute-start | bytes 172040 | tf_op jit(solution)/shard_map/ppermute | solution.py:24
  27.9 3.5 %collective-permute-start.9 = (bf16[32,896]{1,0:T(8,128)(2,1)S(1)}, bf16[32,896]{1,0:T(8,128)(2,1)S(1)}, u32[]{:S(2)}, u32[]{:S(2)}) collective-permute-start(bf16[32,896]{1,0:T(8,128)(2,1)S(1)} %get-tuple-element.19), channel_id=1, source_target_pairs={{0,16},{8,24},{16,0},{24,8},{32,48},{40,56},{48,32},{56,40},{64,80... | collective-permute-start | bytes 172040 | tf_op jit(solution)/shard_map/ppermute | solution.py:24
  31.4 5.0 %collective-permute-start.11 = (bf16[32,896]{1,0:T(8,128)(2,1)S(1)}, bf16[32,896]{1,0:T(8,128)(2,1)S(1)}, u32[]{:S(2)}, u32[]{:S(2)}) collective-permute-start(bf16[32,896]{1,0:T(8,128)(2,1)S(1)} %fusion.2), channel_id=1, source_target_pairs={{0,192},{8,200},{16,208},{24,216},{32,224},{40,232},{48,240},{56,2... | collective-permute-start | bytes 172040 | tf_op jit(solution)/shard_map/ppermute | solution.py:24
  33.2 3.7 %collective-permute-start.12 = (bf16[32,896]{1,0:T(8,128)(2,1)S(1)}, bf16[32,896]{1,0:T(8,128)(2,1)S(1)}, u32[]{:S(2)}, u32[]{:S(2)}) collective-permute-start(bf16[32,896]{1,0:T(8,128)(2,1)S(1)} %fusion.2), channel_id=1, source_target_pairs={{0,64},{8,72},{16,80},{24,88},{32,96},{40,104},{48,112},{56,120},{... | collective-permute-start | bytes 172040 | tf_op jit(solution)/shard_map/ppermute | solution.py:24
  33.5 5.8 %collective-permute-start.13 = (bf16[32,896]{1,0:T(8,128)(2,1)S(1)}, bf16[32,896]{1,0:T(8,128)(2,1)S(1)}, u32[]{:S(2)}, u32[]{:S(2)}) collective-permute-start(bf16[32,896]{1,0:T(8,128)(2,1)S(1)} %fusion.2), channel_id=1, source_target_pairs={{0,128},{8,136},{16,144},{24,152},{32,160},{40,168},{48,176},{56,1... | collective-permute-start | bytes 172040 | tf_op jit(solution)/shard_map/ppermute | solution.py:24
  39.3 5.2 %collective-permute-start.14 = (bf16[32,896]{1,0:T(8,128)(2,1)S(1)}, bf16[32,896]{1,0:T(8,128)(2,1)S(1)}, u32[]{:S(2)}, u32[]{:S(2)}) collective-permute-start(bf16[32,896]{1,0:T(8,128)(2,1)S(1)} %add_convert_fusion.refs_0_), channel_id=1, source_target_pairs={{0,32},{8,40},{16,48},{24,56},{32,0},{40,8},{48,16},{56,24},{64,96... | collective-permute-start | bytes 172040 | tf_op jit(solution)/shard_map/ppermute | solution.py:24
  39.4 7.3 %collective-permute-start.15 = (bf16[32,896]{1,0:T(8,128)(2,1)S(1)}, bf16[32,896]{1,0:T(8,128)(2,1)S(1)}, u32[]{:S(2)}, u32[]{:S(2)}) collective-permute-start(bf16[32,896]{1,0:T(8,128)(2,1)S(1)} %add_convert_fusion.refs_0_), channel_id=1, source_target_pairs={{0,48},{8,56},{16,32},{24,40},{32,16},{40,24},{48,0},{56,8},{64,11... | collective-permute-start | bytes 172040 | tf_op jit(solution)/shard_map/ppermute | solution.py:24
  41.7 6.2 %collective-permute-start.16 = (bf16[32,896]{1,0:T(8,128)(2,1)S(1)}, bf16[32,896]{1,0:T(8,128)(2,1)S(1)}, u32[]{:S(2)}, u32[]{:S(2)}) collective-permute-start(bf16[32,896]{1,0:T(8,128)(2,1)S(1)} %add_convert_fusion.refs_0_), channel_id=1, source_target_pairs={{0,16},{8,24},{16,0},{24,8},{32,48},{40,56},{48,32},{56,40},{64,80... | collective-permute-start | bytes 172040 | tf_op jit(solution)/shard_map/ppermute | solution.py:24
  42.0 6.2 %collective-permute-start.17 = (bf16[32,896]{1,0:T(8,128)(2,1)S(1)}, bf16[32,896]{1,0:T(8,128)(2,1)S(1)}, u32[]{:S(2)}, u32[]{:S(2)}) collective-permute-start(bf16[32,896]{1,0:T(8,128)(2,1)S(1)} %add_convert_fusion.refs_0_), channel_id=1, source_target_pairs={{0,8},{8,0},{16,24},{24,16},{32,40},{40,32},{48,56},{56,48},{64,72... | collective-permute-start | bytes 172040 | tf_op jit(solution)/shard_map/ppermute | solution.py:24
  44.5 3.7 %collective-permute-start.18 = (bf16[32,896]{1,0:T(8,128)(2,1)S(1)}, bf16[32,896]{1,0:T(8,128)(2,1)S(1)}, u32[]{:S(2)}, u32[]{:S(2)}) collective-permute-start(bf16[32,896]{1,0:T(8,128)(2,1)S(1)} %collective-permute-done.14.refs_1_), channel_id=1, source_target_pairs={{0,8},{8,0},{16,24},{24,16},{32,40},{40,32},{48,56},{56,48},{64,72... | collective-permute-start | bytes 172040 | tf_op jit(solution)/shard_map/ppermute | solution.py:24
  46.7 2.1 %collective-permute-start.19 = (bf16[32,896]{1,0:T(8,128)(2,1)S(1)}, bf16[32,896]{1,0:T(8,128)(2,1)S(1)}, u32[]{:S(2)}, u32[]{:S(2)}) collective-permute-start(bf16[32,896]{1,0:T(8,128)(2,1)S(1)} %collective-permute-done.15.refs_2_), channel_id=1, source_target_pairs={{0,8},{8,0},{16,24},{24,16},{32,40},{40,32},{48,56},{56,48},{64,72... | collective-permute-start | bytes 172040 | tf_op jit(solution)/shard_map/ppermute | solution.py:24
  48.0 1.2 %collective-permute-start.20 = (bf16[32,896]{1,0:T(8,128)(2,1)S(1)}, bf16[32,896]{1,0:T(8,128)(2,1)S(1)}, u32[]{:S(2)}, u32[]{:S(2)}) collective-permute-start(bf16[32,896]{1,0:T(8,128)(2,1)S(1)} %collective-permute-done.16.refs_3_), channel_id=1, source_target_pairs={{0,8},{8,0},{16,24},{24,16},{32,40},{40,32},{48,56},{56,48},{64,72... | collective-permute-start | bytes 172040 | tf_op jit(solution)/shard_map/ppermute | solution.py:24

commit v7 on v6

--- a/solution.py
+++ b/solution.py
@@ -242,8 +242,9 @@
     core, y = core_ref[0], y_ref[0]
     for s, slot in enumerate(SLOTS):
         at = jnp.bitwise_xor(y, slot) * CHUNK
-        own_at = pl.multiple_of(core * NP + at, CHUNK)
-        other_at = pl.multiple_of((1 - core) * NP + at, CHUNK)
+        half = core if slot % 2 == 0 else 1 - core
+        own_at = pl.multiple_of(half * NP + at, CHUNK)
+        other_at = pl.multiple_of((1 - half) * NP + at, CHUNK)
         right_ref[pl.ds(own_at, CHUNK), :] = own_ref[s][...]
         right_ref[pl.ds(other_at, CHUNK), :] = other_ref[s][...]
     right = right_ref[...]
@@ -301,7 +302,7 @@
     for arrived in [over_pw(sent, 8 * s) for s in (3, 1, 2)]:
         sums = sums + arrived.astype(F32)
     mine = sums.astype(BF16)
-    own = [mine] + [over_pw(mine, 2 * s) for s in SLOTS[1:]]
+    own = [mine] + [over_pw(mine, 2 * s + s % 2) for s in SLOTS[1:]]
     other = [over_pw(chunk, 1) for chunk in own]
     return spread_back(core, y, own, other, turned)
 

time: 52.1 us -> 51.5 us (0.988)
  starting transfers between devices: 33.4 us -> 32.8 us
    ppermute x14, starting transfers between devices: 19.1 us -> 18.5 us  [over_pw(): return lax.ppermute(x, 'pw', [(i, i ^ bits) for i in range(32)])]
where the time goes in v7:
time: 51.5 us; the launch traced here: 51.4 us
  starting transfers between devices  32.8 us (64%)
  waiting for transfers between devices  10.5 us (20%)
  Pallas kernels  7.56 us (15%)
    ppermute x14, starting transfers between devices, over_pw(): return lax.ppermute(x, 'pw', [(i, i ^ bits) for i in range(32)])  18.5 us
    ppermute x7, starting transfers between devices, over_band(): return lax.ppermute(x, 'band', [(i, i ^ bits) for i in range(8)])  14.3 us
    ppermute x14, waiting for transfers between devices, over_pw(): return lax.ppermute(x, 'pw', [(i, i ^ bits) for i in range(32)])  9.75 us
    pallas_call x1, Pallas kernels, spread_back(): pl.pallas_call(spread_kernel, out_shape=jax.ShapeDtypeStruct((2, NPW_DEV,...  2.58 us
    pallas_call x1, Pallas kernels, ahead(): pl.pallas_call(ahead_kernel, out_shape=(jax.ShapeDtypeStruct((2, NP, 3 *...  2.34 us
    pallas_call x1, Pallas kernels, project_near(): pl.pallas_call(near_kernel, out_shape=jax.ShapeDtypeStruct((2, NP, NB_DEV...  1.17 us
    pallas_call x1, Pallas kernels, project_far(): pl.pallas_call(far_kernel, out_shape=halves, in_specs=[smem()] + [vmem()]...  1.15 us
  transfers between devices with their start and end apart: 21, of which 9 were waited for; matrix products, arithmetic and copies ran while one was open for 0% of the time, Pallas kernels for 7%

profile of v7, /device:TPU:1, one launch (start us, length us, event | category | flops | bytes accessed | tf_op | source)
XLA Modules:
  0.0 51.4 jit_solution(5261716892697143924)
XLA Ops:
  0.0 7.7 %collective-permute-start = (bf16[2,16,1280]{2,1,0:T(8,128)(2,1)}, bf16[2,16,1280]{2,1,0:T(8,128)(2,1)S(1)}, u32[]{:S(2)}, u32[]{:S(2)}) collective-permute-start(bf16[2,16,1280]{2,1,0:T(8,128)(2,1)} %refs_3_.3), channel_id=1, source_target_pairs={{0,1},{1,0},{2,3},{3,2},{4,5},{5,4},{6,7},{7,6},{8,9},{9,8},{10,11... | collective-permute-start | bytes 245768 | tf_op jit(solution)/shard_map/ppermute | solution.py:28
  7.7 2.5 %collective-permute-start.1 = (bf16[2,16,1280]{2,1,0:T(8,128)(2,1)}, bf16[2,16,1280]{2,1,0:T(8,128)(2,1)S(1)}, u32[]{:S(2)}, u32[]{:S(2)}) collective-permute-start(bf16[2,16,1280]{2,1,0:T(8,128)(2,1)} %refs_3_.3), channel_id=1, source_target_pairs={{0,6},{1,7},{2,4},{3,5},{4,2},{5,3},{6,0},{7,1},{8,14},{9,15},{10,... | collective-permute-start | bytes 245768 | tf_op jit(solution)/shard_map/ppermute | solution.py:28
  10.2 0.5 %collective-permute-start.2 = (bf16[2,16,1280]{2,1,0:T(8,128)(2,1)}, bf16[2,16,1280]{2,1,0:T(8,128)(2,1)S(1)}, u32[]{:S(2)}, u32[]{:S(2)}) collective-permute-start(bf16[2,16,1280]{2,1,0:T(8,128)(2,1)} %refs_3_.3), channel_id=1, source_target_pairs={{0,4},{1,5},{2,6},{3,7},{4,0},{5,1},{6,2},{7,3},{8,12},{9,13},{10,... | collective-permute-start | bytes 245768 | tf_op jit(solution)/shard_map/ppermute | solution.py:28
  10.7 0.3 collective-permute-start.3
  11.1 2.6 %collective-permute-start.4 = (bf16[2,16,1280]{2,1,0:T(8,128)(2,1)S(1)}, bf16[2,16,1280]{2,1,0:T(8,128)(2,1)S(1)}, u32[]{:S(2)}, u32[]{:S(2)}) collective-permute-start(bf16[2,16,1280]{2,1,0:T(8,128)(2,1)S(1)} %collective-permute-done.refs_3_.refs_7_), channel_id=1, source_target_pairs={{0,6},{1,7},{2,4},{3,5},{4,2},{5,3},{6,0},{7,1},{8,14},{9,15},{10,... | collective-permute-start | bytes 245768 | tf_op jit(solution)/shard_map/ppermute | solution.py:28
  13.7 0.5 %collective-permute-start.5 = (bf16[2,16,1280]{2,1,0:T(8,128)(2,1)S(1)}, bf16[2,16,1280]{2,1,0:T(8,128)(2,1)S(1)}, u32[]{:S(2)}, u32[]{:S(2)}) collective-permute-start(bf16[2,16,1280]{2,1,0:T(8,128)(2,1)S(1)} %collective-permute-done.refs_3_.refs_7_), channel_id=1, source_target_pairs={{0,4},{1,5},{2,6},{3,7},{4,0},{5,1},{6,2},{7,3},{8,12},{9,13},{10,... | collective-permute-start | bytes 245768 | tf_op jit(solution)/shard_map/ppermute | solution.py:28
  14.2 0.3 collective-permute-start.6
  14.5 2.3 %shard_map.56 = (bf16[2,128,192]{2,1,0:T(8,128)(2,1)S(1)}, bf16[2,1280,896]{2,1,0:T(8,128)(2,1)S(1)}) custom-call(bf16[2,128,128]{2,1,0:T(8,128)(2,1)S(1)} %shard_map.55.pick_ref, s32[12]{0:T(128)S(1)} %copy-done.2, s32[12]{0:T(128)S(1)} %copy-done.3, f32[12,13,13]{2,1,0:T(8,128)S(1)} %copy-done.1, bf16[2,1280,896]{2,1,0:T(8,128)(2,1)} %waves_hbm.1), custom_call_target="tpu_custom_call" | custom-call | flops 2000000000 | bytes 8388608 | tf_op jit(solution)/shard_map/pallas_call | solution.py:128
  16.9 1.2 %shard_map.57.near_ref = f32[2,128,896]{2,1,0:T(8,128)S(1)} custom-call(bf16[2,128,192]{2,1,0:T(8,128)(2,1)S(1)} %get-tuple-element.11.left_ref, bf16[2,1280,896]{2,1,0:T(8,128)(2,1)S(1)} %get-tuple-element.12.waves_ref, bf16[2,16,1280]{2,1,0:T(8,128)(2,1)S(1)} %collective-permute-done.1.refs_0_, bf16[2,16,1280]{2,1,0:T(8,128)(2,1)S(1)} %collective-permute-done.2.refs_1_, ...), custom_call_target="tpu_custom_call" | custom-call | flops 587202560 | bytes 6291456 | tf_op jit(solution)/shard_map/pallas_call | solution.py:172
  18.1 0.7 %collective-permute-done.5.refs_1_.refs_5_ = bf16[2,16,1280]{2,1,0:T(8,128)(2,1)S(1)} collective-permute-done((bf16[2,16,1280]{2,1,0:T(8,128)(2,1)S(1)}, bf16[2,16,1280]{2,1,0:T(8,128)(2,1)S(1)}, u32[]{:S(2)}, u32[]{:S(2)}) %collective-permute-start.5) | collective-permute-done | bytes 81952 | tf_op jit(solution)/shard_map/ppermute | solution.py:28
  18.8 1.1 %shard_map.58 = (f32[128,896]{1,0:T(8,128)S(1)}, bf16[128,896]{1,0:T(8,128)(2,1)S(1)}) custom-call(s32[1]{0:T(128)} %bitcast.core_ref, f32[2,128,896]{2,1,0:T(8,128)S(1)} %shard_map.57.near_ref, bf16[2,128,192]{2,1,0:T(8,128)(2,1)S(1)} %get-tuple-element.11.left_ref, bf16[2,1280,896]{2,1,0:T(8,128)(2,1)S(1)} %get-tuple-element.12.waves_ref, ...), custom_call_target="tpu_custom_call" | custom-call | flops 587202560 | bytes 6291456 | tf_op jit(solution)/shard_map/pallas_call | solution.py:202
  19.9 3.0 %collective-permute-start.7 = (bf16[128,896]{1,0:T(8,128)(2,1)S(1)}, bf16[128,896]{1,0:T(8,128)(2,1)S(1)}, u32[]{:S(2)}, u32[]{:S(2)}) collective-permute-start(bf16[128,896]{1,0:T(8,128)(2,1)S(1)} %get-tuple-element.14), channel_id=1, source_target_pairs={{0,8},{8,0},{16,24},{24,16},{32,40},{40,32},{48,56},{56,48},{64,72... | collective-permute-start | bytes 688136 | tf_op jit(solution)/shard_map/ppermute | solution.py:24
  23.0 1.1 %collective-permute-done.7 = bf16[128,896]{1,0:T(8,128)(2,1)S(1)} collective-permute-done((bf16[128,896]{1,0:T(8,128)(2,1)S(1)}, bf16[128,896]{1,0:T(8,128)(2,1)S(1)}, u32[]{:S(2)}, u32[]{:S(2)}) %collective-permute-start.7) | collective-permute-done | bytes 229408 | tf_op jit(solution)/shard_map/ppermute | solution.py:24
  24.2 3.0 %collective-permute-start.10 = (bf16[32,896]{1,0:T(8,128)(2,1)S(1)}, bf16[32,896]{1,0:T(8,128)(2,1)S(1)}, u32[]{:S(2)}, u32[]{:S(2)}) collective-permute-start(bf16[32,896]{1,0:T(8,128)(2,1)S(1)} %get-tuple-element.18), channel_id=1, source_target_pairs={{0,32},{8,40},{16,48},{24,56},{32,0},{40,8},{48,16},{56,24},{64,96... | collective-permute-start | bytes 172040 | tf_op jit(solution)/shard_map/ppermute | solution.py:24
  27.2 0.8 %collective-permute-start.8 = (bf16[32,896]{1,0:T(8,128)(2,1)S(1)}, bf16[32,896]{1,0:T(8,128)(2,1)S(1)}, u32[]{:S(2)}, u32[]{:S(2)}) collective-permute-start(bf16[32,896]{1,0:T(8,128)(2,1)S(1)} %get-tuple-element.17), channel_id=1, source_target_pairs={{0,48},{8,56},{16,32},{24,40},{32,16},{40,24},{48,0},{56,8},{64,11... | collective-permute-start | bytes 172040 | tf_op jit(solution)/shard_map/ppermute | solution.py:24
  27.9 0.8 %collective-permute-done.10 = bf16[32,896]{1,0:T(8,128)(2,1)S(1)} collective-permute-done((bf16[32,896]{1,0:T(8,128)(2,1)S(1)}, bf16[32,896]{1,0:T(8,128)(2,1)S(1)}, u32[]{:S(2)}, u32[]{:S(2)}) %collective-permute-start.10) | collective-permute-done | bytes 57376 | tf_op jit(solution)/shard_map/ppermute | solution.py:24
  28.8 2.6 %collective-permute-done.8 = bf16[32,896]{1,0:T(8,128)(2,1)S(1)} collective-permute-done((bf16[32,896]{1,0:T(8,128)(2,1)S(1)}, bf16[32,896]{1,0:T(8,128)(2,1)S(1)}, u32[]{:S(2)}, u32[]{:S(2)}) %collective-permute-start.8) | collective-permute-done | bytes 57376 | tf_op jit(solution)/shard_map/ppermute | solution.py:24
  31.4 1.7 %collective-permute-start.11 = (bf16[32,896]{1,0:T(8,128)(2,1)S(1)}, bf16[32,896]{1,0:T(8,128)(2,1)S(1)}, u32[]{:S(2)}, u32[]{:S(2)}) collective-permute-start(bf16[32,896]{1,0:T(8,128)(2,1)S(1)} %fusion.2), channel_id=1, source_target_pairs={{0,192},{8,200},{16,208},{24,216},{32,224},{40,232},{48,240},{56,2... | collective-permute-start | bytes 172040 | tf_op jit(solution)/shard_map/ppermute | solution.py:24
  33.2 0.3 collective-permute-start.12
  33.5 1.6 %collective-permute-start.13 = (bf16[32,896]{1,0:T(8,128)(2,1)S(1)}, bf16[32,896]{1,0:T(8,128)(2,1)S(1)}, u32[]{:S(2)}, u32[]{:S(2)}) collective-permute-start(bf16[32,896]{1,0:T(8,128)(2,1)S(1)} %fusion.2), channel_id=1, source_target_pairs={{0,128},{8,136},{16,144},{24,152},{32,160},{40,168},{48,176},{56,1... | collective-permute-start | bytes 172040 | tf_op jit(solution)/shard_map/ppermute | solution.py:24
  35.1 1.4 %collective-permute-done.11 = bf16[32,896]{1,0:T(8,128)(2,1)S(1)} collective-permute-done((bf16[32,896]{1,0:T(8,128)(2,1)S(1)}, bf16[32,896]{1,0:T(8,128)(2,1)S(1)}, u32[]{:S(2)}, u32[]{:S(2)}) %collective-permute-start.11) | collective-permute-done | bytes 57376 | tf_op jit(solution)/shard_map/ppermute | solution.py:24
  36.5 0.4 collective-permute-done.12
  36.9 2.4 %collective-permute-done.13 = bf16[32,896]{1,0:T(8,128)(2,1)S(1)} collective-permute-done((bf16[32,896]{1,0:T(8,128)(2,1)S(1)}, bf16[32,896]{1,0:T(8,128)(2,1)S(1)}, u32[]{:S(2)}, u32[]{:S(2)}) %collective-permute-start.13) | collective-permute-done | bytes 57376 | tf_op jit(solution)/shard_map/ppermute | solution.py:24
  39.4 3.9 %collective-permute-start.15 = (bf16[32,896]{1,0:T(8,128)(2,1)S(1)}, bf16[32,896]{1,0:T(8,128)(2,1)S(1)}, u32[]{:S(2)}, u32[]{:S(2)}) collective-permute-start(bf16[32,896]{1,0:T(8,128)(2,1)S(1)} %add_convert_fusion.refs_0_), channel_id=1, source_target_pairs={{0,56},{8,48},{16,40},{24,32},{32,24},{40,16},{48,8},{56,0},{64,12... | collective-permute-start | bytes 172040 | tf_op jit(solution)/shard_map/ppermute | solution.py:24
  43.3 0.2 collective-permute-start.16
  43.5 0.7 %collective-permute-start.17 = (bf16[32,896]{1,0:T(8,128)(2,1)S(1)}, bf16[32,896]{1,0:T(8,128)(2,1)S(1)}, u32[]{:S(2)}, u32[]{:S(2)}) collective-permute-start(bf16[32,896]{1,0:T(8,128)(2,1)S(1)} %add_convert_fusion.refs_0_), channel_id=1, source_target_pairs={{0,8},{8,0},{16,24},{24,16},{32,40},{40,32},{48,56},{56,48},{64,72... | collective-permute-start | bytes 172040 | tf_op jit(solution)/shard_map/ppermute | solution.py:24
  44.2 2.5 %collective-permute-start.18 = (bf16[32,896]{1,0:T(8,128)(2,1)S(1)}, bf16[32,896]{1,0:T(8,128)(2,1)S(1)}, u32[]{:S(2)}, u32[]{:S(2)}) collective-permute-start(bf16[32,896]{1,0:T(8,128)(2,1)S(1)} %collective-permute-done.14.refs_1_), channel_id=1, source_target_pairs={{0,8},{8,0},{16,24},{24,16},{32,40},{40,32},{48,56},{56,48},{64,72... | collective-permute-start | bytes 172040 | tf_op jit(solution)/shard_map/ppermute | solution.py:24
  46.7 0.7 %collective-permute-start.19 = (bf16[32,896]{1,0:T(8,128)(2,1)S(1)}, bf16[32,896]{1,0:T(8,128)(2,1)S(1)}, u32[]{:S(2)}, u32[]{:S(2)}) collective-permute-start(bf16[32,896]{1,0:T(8,128)(2,1)S(1)} %collective-permute-done.15.refs_2_), channel_id=1, source_target_pairs={{0,8},{8,0},{16,24},{24,16},{32,40},{40,32},{48,56},{56,48},{64,72... | collective-permute-start | bytes 172040 | tf_op jit(solution)/shard_map/ppermute | solution.py:24
  47.4 0.2 shard_map.59.refs_8_
  47.6 0.6 %collective-permute-done.19.refs_6_ = bf16[32,896]{1,0:T(8,128)(2,1)S(1)} collective-permute-done((bf16[32,896]{1,0:T(8,128)(2,1)S(1)}, bf16[32,896]{1,0:T(8,128)(2,1)S(1)}, u32[]{:S(2)}, u32[]{:S(2)}) %collective-permute-start.19) | collective-permute-done | bytes 57376 | tf_op jit(solution)/shard_map/ppermute | solution.py:24
  48.3 0.4 collective-permute-done.20.refs_7_
  48.6 2.6 %shard_map.60 = bf16[2,1280,896]{2,1,0:T(8,128)(2,1)} custom-call(s32[1]{0:T(128)} %bitcast.core_ref, s32[1]{0:T(128)} %bitcast.1.y_ref, bf16[32,896]{1,0:T(8,128)(2,1)S(1)} %add_convert_fusion.refs_0_, bf16[32,896]{1,0:T(8,128)(2,1)S(1)} %collective-permute-done.14.refs_1_, bf16[32,896]{1,0:T(8,128)(2,1)S(1)} %collective-permute-done.15.refs_2_, ...), custom_call_target="tpu_custom_call" | custom-call | flops 1174405120 | bytes 6291456 | tf_op jit(solution)/shard_map/pallas_call | solution.py:268
  (28 shorter events, 0.4 us)
Async XLA Ops:
  0.0 11.1 %collective-permute-start = (bf16[2,16,1280]{2,1,0:T(8,128)(2,1)}, bf16[2,16,1280]{2,1,0:T(8,128)(2,1)S(1)}, u32[]{:S(2)}, u32[]{:S(2)}) collective-permute-start(bf16[2,16,1280]{2,1,0:T(8,128)(2,1)} %refs_3_.3), channel_id=1, source_target_pairs={{0,1},{1,0},{2,3},{3,2},{4,5},{5,4},{6,7},{7,6},{8,9},{9,8},{10,11... | collective-permute-start | bytes 245768 | tf_op jit(solution)/shard_map/ppermute | solution.py:28
  7.7 6.5 %collective-permute-start.1 = (bf16[2,16,1280]{2,1,0:T(8,128)(2,1)}, bf16[2,16,1280]{2,1,0:T(8,128)(2,1)S(1)}, u32[]{:S(2)}, u32[]{:S(2)}) collective-permute-start(bf16[2,16,1280]{2,1,0:T(8,128)(2,1)} %refs_3_.3), channel_id=1, source_target_pairs={{0,6},{1,7},{2,4},{3,5},{4,2},{5,3},{6,0},{7,1},{8,14},{9,15},{10,... | collective-permute-start | bytes 245768 | tf_op jit(solution)/shard_map/ppermute | solution.py:28
  10.2 6.6 %collective-permute-start.2 = (bf16[2,16,1280]{2,1,0:T(8,128)(2,1)}, bf16[2,16,1280]{2,1,0:T(8,128)(2,1)S(1)}, u32[]{:S(2)}, u32[]{:S(2)}) collective-permute-start(bf16[2,16,1280]{2,1,0:T(8,128)(2,1)} %refs_3_.3), channel_id=1, source_target_pairs={{0,4},{1,5},{2,6},{3,7},{4,0},{5,1},{6,2},{7,3},{8,12},{9,13},{10,... | collective-permute-start | bytes 245768 | tf_op jit(solution)/shard_map/ppermute | solution.py:28
  10.7 6.1 %collective-permute-start.3 = (bf16[2,16,1280]{2,1,0:T(8,128)(2,1)}, bf16[2,16,1280]{2,1,0:T(8,128)(2,1)S(1)}, u32[]{:S(2)}, u32[]{:S(2)}) collective-permute-start(bf16[2,16,1280]{2,1,0:T(8,128)(2,1)} %refs_3_.3), channel_id=1, source_target_pairs={{0,2},{1,3},{2,0},{3,1},{4,6},{5,7},{6,4},{7,5},{8,10},{9,11},{10,... | collective-permute-start | bytes 245768 | tf_op jit(solution)/shard_map/ppermute | solution.py:28
  11.0 3.5 %copy-start.1 = (f32[12,13,13]{2,1,0:T(8,128)S(1)}, f32[12,13,13]{2,1,0:T(8,128)}, u32[]{:S(2)}) copy-start(f32[12,13,13]{2,1,0:T(8,128)} %coupling_hbm.1) | copy-start | bytes 24340
  11.0 3.5 %copy-start.2 = (s32[12]{0:T(128)S(1)}, s32[12]{0:T(128)}, u32[]{:S(2)}) copy-start(s32[12]{0:T(128)} %offsets_hbm.1) | copy-start | bytes 148
  11.0 3.5 %copy-start.3 = (s32[12]{0:T(128)S(1)}, s32[12]{0:T(128)}, u32[]{:S(2)}) copy-start(s32[12]{0:T(128)} %counts_hbm.1) | copy-start | bytes 148
  11.1 5.8 %copy-start = (bf16[2,16,1280]{2,1,0:T(8,128)(2,1)S(1)}, bf16[2,16,1280]{2,1,0:T(8,128)(2,1)}, u32[]{:S(2)}) copy-start(bf16[2,16,1280]{2,1,0:T(8,128)(2,1)} %refs_3_.3) | copy-start | bytes 245764
  11.1 6.9 %collective-permute-start.4 = (bf16[2,16,1280]{2,1,0:T(8,128)(2,1)S(1)}, bf16[2,16,1280]{2,1,0:T(8,128)(2,1)S(1)}, u32[]{:S(2)}, u32[]{:S(2)}) collective-permute-start(bf16[2,16,1280]{2,1,0:T(8,128)(2,1)S(1)} %collective-permute-done.refs_3_.refs_7_), channel_id=1, source_target_pairs={{0,6},{1,7},{2,4},{3,5},{4,2},{5,3},{6,0},{7,1},{8,14},{9,15},{10,... | collective-permute-start | bytes 245768 | tf_op jit(solution)/shard_map/ppermute | solution.py:28
  13.7 5.1 %collective-permute-start.5 = (bf16[2,16,1280]{2,1,0:T(8,128)(2,1)S(1)}, bf16[2,16,1280]{2,1,0:T(8,128)(2,1)S(1)}, u32[]{:S(2)}, u32[]{:S(2)}) collective-permute-start(bf16[2,16,1280]{2,1,0:T(8,128)(2,1)S(1)} %collective-permute-done.refs_3_.refs_7_), channel_id=1, source_target_pairs={{0,4},{1,5},{2,6},{3,7},{4,0},{5,1},{6,2},{7,3},{8,12},{9,13},{10,... | collective-permute-start | bytes 245768 | tf_op jit(solution)/shard_map/ppermute | solution.py:28
  14.2 4.6 %collective-permute-start.6 = (bf16[2,16,1280]{2,1,0:T(8,128)(2,1)S(1)}, bf16[2,16,1280]{2,1,0:T(8,128)(2,1)S(1)}, u32[]{:S(2)}, u32[]{:S(2)}) collective-permute-start(bf16[2,16,1280]{2,1,0:T(8,128)(2,1)S(1)} %collective-permute-done.refs_3_.refs_7_), channel_id=1, source_target_pairs={{0,2},{1,3},{2,0},{3,1},{4,6},{5,7},{6,4},{7,5},{8,10},{9,11},{10,... | collective-permute-start | bytes 245768 | tf_op jit(solution)/shard_map/ppermute | solution.py:28
  19.9 4.1 %collective-permute-start.7 = (bf16[128,896]{1,0:T(8,128)(2,1)S(1)}, bf16[128,896]{1,0:T(8,128)(2,1)S(1)}, u32[]{:S(2)}, u32[]{:S(2)}) collective-permute-start(bf16[128,896]{1,0:T(8,128)(2,1)S(1)} %get-tuple-element.14), channel_id=1, source_target_pairs={{0,8},{8,0},{16,24},{24,16},{32,40},{40,32},{48,56},{56,48},{64,72... | collective-permute-start | bytes 688136 | tf_op jit(solution)/shard_map/ppermute | solution.py:24
  24.2 4.6 %collective-permute-start.10 = (bf16[32,896]{1,0:T(8,128)(2,1)S(1)}, bf16[32,896]{1,0:T(8,128)(2,1)S(1)}, u32[]{:S(2)}, u32[]{:S(2)}) collective-permute-start(bf16[32,896]{1,0:T(8,128)(2,1)S(1)} %get-tuple-element.18), channel_id=1, source_target_pairs={{0,32},{8,40},{16,48},{24,56},{32,0},{40,8},{48,16},{56,24},{64,96... | collective-permute-start | bytes 172040 | tf_op jit(solution)/shard_map/ppermute | solution.py:24
  27.2 4.2 %collective-permute-start.8 = (bf16[32,896]{1,0:T(8,128)(2,1)S(1)}, bf16[32,896]{1,0:T(8,128)(2,1)S(1)}, u32[]{:S(2)}, u32[]{:S(2)}) collective-permute-start(bf16[32,896]{1,0:T(8,128)(2,1)S(1)} %get-tuple-element.17), channel_id=1, source_target_pairs={{0,48},{8,56},{16,32},{24,40},{32,16},{40,24},{48,0},{56,8},{64,11... | collective-permute-start | bytes 172040 | tf_op jit(solution)/shard_map/ppermute | solution.py:24
  27.9 3.5 %collective-permute-start.9 = (bf16[32,896]{1,0:T(8,128)(2,1)S(1)}, bf16[32,896]{1,0:T(8,128)(2,1)S(1)}, u32[]{:S(2)}, u32[]{:S(2)}) collective-permute-start(bf16[32,896]{1,0:T(8,128)(2,1)S(1)} %get-tuple-element.19), channel_id=1, source_target_pairs={{0,16},{8,24},{16,0},{24,8},{32,48},{40,56},{48,32},{56,40},{64,80... | collective-permute-start | bytes 172040 | tf_op jit(solution)/shard_map/ppermute | solution.py:24
  31.4 5.0 %collective-permute-start.11 = (bf16[32,896]{1,0:T(8,128)(2,1)S(1)}, bf16[32,896]{1,0:T(8,128)(2,1)S(1)}, u32[]{:S(2)}, u32[]{:S(2)}) collective-permute-start(bf16[32,896]{1,0:T(8,128)(2,1)S(1)} %fusion.2), channel_id=1, source_target_pairs={{0,192},{8,200},{16,208},{24,216},{32,224},{40,232},{48,240},{56,2... | collective-permute-start | bytes 172040 | tf_op jit(solution)/shard_map/ppermute | solution.py:24
  33.2 3.7 %collective-permute-start.12 = (bf16[32,896]{1,0:T(8,128)(2,1)S(1)}, bf16[32,896]{1,0:T(8,128)(2,1)S(1)}, u32[]{:S(2)}, u32[]{:S(2)}) collective-permute-start(bf16[32,896]{1,0:T(8,128)(2,1)S(1)} %fusion.2), channel_id=1, source_target_pairs={{0,64},{8,72},{16,80},{24,88},{32,96},{40,104},{48,112},{56,120},{... | collective-permute-start | bytes 172040 | tf_op jit(solution)/shard_map/ppermute | solution.py:24
  33.5 5.8 %collective-permute-start.13 = (bf16[32,896]{1,0:T(8,128)(2,1)S(1)}, bf16[32,896]{1,0:T(8,128)(2,1)S(1)}, u32[]{:S(2)}, u32[]{:S(2)}) collective-permute-start(bf16[32,896]{1,0:T(8,128)(2,1)S(1)} %fusion.2), channel_id=1, source_target_pairs={{0,128},{8,136},{16,144},{24,152},{32,160},{40,168},{48,176},{56,1... | collective-permute-start | bytes 172040 | tf_op jit(solution)/shard_map/ppermute | solution.py:24
  39.3 4.9 %collective-permute-start.14 = (bf16[32,896]{1,0:T(8,128)(2,1)S(1)}, bf16[32,896]{1,0:T(8,128)(2,1)S(1)}, u32[]{:S(2)}, u32[]{:S(2)}) collective-permute-start(bf16[32,896]{1,0:T(8,128)(2,1)S(1)} %add_convert_fusion.refs_0_), channel_id=1, source_target_pairs={{0,32},{8,40},{16,48},{24,56},{32,0},{40,8},{48,16},{56,24},{64,96... | collective-permute-start | bytes 172040 | tf_op jit(solution)/shard_map/ppermute | solution.py:24
  39.4 7.3 %collective-permute-start.15 = (bf16[32,896]{1,0:T(8,128)(2,1)S(1)}, bf16[32,896]{1,0:T(8,128)(2,1)S(1)}, u32[]{:S(2)}, u32[]{:S(2)}) collective-permute-start(bf16[32,896]{1,0:T(8,128)(2,1)S(1)} %add_convert_fusion.refs_0_), channel_id=1, source_target_pairs={{0,56},{8,48},{16,40},{24,32},{32,24},{40,16},{48,8},{56,0},{64,12... | collective-permute-start | bytes 172040 | tf_op jit(solution)/shard_map/ppermute | solution.py:24
  43.3 4.1 %collective-permute-start.16 = (bf16[32,896]{1,0:T(8,128)(2,1)S(1)}, bf16[32,896]{1,0:T(8,128)(2,1)S(1)}, u32[]{:S(2)}, u32[]{:S(2)}) collective-permute-start(bf16[32,896]{1,0:T(8,128)(2,1)S(1)} %add_convert_fusion.refs_0_), channel_id=1, source_target_pairs={{0,24},{8,16},{16,8},{24,0},{32,56},{40,48},{48,40},{56,32},{64,88... | collective-permute-start | bytes 172040 | tf_op jit(solution)/shard_map/ppermute | solution.py:24
  43.5 4.1 %collective-permute-start.17 = (bf16[32,896]{1,0:T(8,128)(2,1)S(1)}, bf16[32,896]{1,0:T(8,128)(2,1)S(1)}, u32[]{:S(2)}, u32[]{:S(2)}) collective-permute-start(bf16[32,896]{1,0:T(8,128)(2,1)S(1)} %add_convert_fusion.refs_0_), channel_id=1, source_target_pairs={{0,8},{8,0},{16,24},{24,16},{32,40},{40,32},{48,56},{56,48},{64,72... | collective-permute-start | bytes 172040 | tf_op jit(solution)/shard_map/ppermute | solution.py:24
  44.2 3.4 %collective-permute-start.18 = (bf16[32,896]{1,0:T(8,128)(2,1)S(1)}, bf16[32,896]{1,0:T(8,128)(2,1)S(1)}, u32[]{:S(2)}, u32[]{:S(2)}) collective-permute-start(bf16[32,896]{1,0:T(8,128)(2,1)S(1)} %collective-permute-done.14.refs_1_), channel_id=1, source_target_pairs={{0,8},{8,0},{16,24},{24,16},{32,40},{40,32},{48,56},{56,48},{64,72... | collective-permute-start | bytes 172040 | tf_op jit(solution)/shard_map/ppermute | solution.py:24
  46.7 1.6 %collective-permute-start.19 = (bf16[32,896]{1,0:T(8,128)(2,1)S(1)}, bf16[32,896]{1,0:T(8,128)(2,1)S(1)}, u32[]{:S(2)}, u32[]{:S(2)}) collective-permute-start(bf16[32,896]{1,0:T(8,128)(2,1)S(1)} %collective-permute-done.15.refs_2_), channel_id=1, source_target_pairs={{0,8},{8,0},{16,24},{24,16},{32,40},{40,32},{48,56},{56,48},{64,72... | collective-permute-start | bytes 172040 | tf_op jit(solution)/shard_map/ppermute | solution.py:24
  47.4 1.2 %collective-permute-start.20 = (bf16[32,896]{1,0:T(8,128)(2,1)S(1)}, bf16[32,896]{1,0:T(8,128)(2,1)S(1)}, u32[]{:S(2)}, u32[]{:S(2)}) collective-permute-start(bf16[32,896]{1,0:T(8,128)(2,1)S(1)} %collective-permute-done.16.refs_3_), channel_id=1, source_target_pairs={{0,8},{8,0},{16,24},{24,16},{32,40},{40,32},{48,56},{56,48},{64,72... | collective-permute-start | bytes 172040 | tf_op jit(solution)/shard_map/ppermute | solution.py:24

commit v8 on v7

--- a/solution.py
+++ b/solution.py
@@ -13,6 +13,7 @@
 NPW_DEV = 1280
 NB_DEV = 896
 CHUNK = 32
+ORDER = ((3, 2, 1, 0), (2, 3, 1, 0))
 SLOTS = (0, 2, 3, 1)
 BLOCK_PW = 320
 BF16 = jnp.bfloat16
@@ -147,7 +148,7 @@
 
 def coupled_parts(h, pieces, left_ref, waves_ref, rows_ref):
     for i, piece in enumerate(pieces):
-        at = (3 - i) * ROWS
+        at = ORDER[h][i] * ROWS
         rows_ref[pl.ds(at, ROWS), :] = piece[0]
         rows_ref[pl.ds(HALF + at, ROWS), :] = piece[1]
     rows = rows_ref[...]
@@ -213,7 +214,7 @@
 def turn_kernel(*refs):
     pieces, (out_ref, rows_ref) = refs[:8], refs[8:]
     for i, piece in enumerate(pieces):
-        at = (i // 4) * HALF + (3 - i % 4) * ROWS
+        at = (i // 4) * HALF + ORDER[i // 4][i % 4] * ROWS
         for k in range(2):
             rows_ref[pl.ds(k * NP + at, ROWS), :] = piece[k]
     turned = rows_ref[...].T
@@ -242,7 +243,7 @@
     core, y = core_ref[0], y_ref[0]
     for s, slot in enumerate(SLOTS):
         at = jnp.bitwise_xor(y, slot) * CHUNK
-        half = core if slot % 2 == 0 else 1 - core
+        half = core if slot == 0 else 1 - core
         own_at = pl.multiple_of(half * NP + at, CHUNK)
         other_at = pl.multiple_of((1 - half) * NP + at, CHUNK)
         right_ref[pl.ds(own_at, CHUNK), :] = own_ref[s][...]
@@ -286,7 +287,7 @@
 
     distant = over_band(projectors, 1)
     near = [over_band(projectors, bits) for bits in (6, 4, 2)] + [projectors]
-    far = [over_band(distant, bits) for bits in (6, 4, 2)] + [distant]
+    far = [over_band(distant, bits) for bits in (4, 6, 2)] + [distant]
     pick = gathered_order(y, band)
     pick, _ = lax.optimization_barrier((pick, distant))
     left, waves = ahead(pick, offsets, counts, coupling, waves)
@@ -302,7 +303,7 @@
     for arrived in [over_pw(sent, 8 * s) for s in (3, 1, 2)]:
         sums = sums + arrived.astype(F32)
     mine = sums.astype(BF16)
-    own = [mine] + [over_pw(mine, 2 * s + s % 2) for s in SLOTS[1:]]
+    own = [mine] + [over_pw(mine, 2 * s + 1) for s in SLOTS[1:]]
     other = [over_pw(chunk, 1) for chunk in own]
     return spread_back(core, y, own, other, turned)
 

time: 51.5 us -> 51.2 us (level)
  starting transfers between devices: 32.8 us -> 31.4 us
  waiting for transfers between devices: 10.5 us -> 11.7 us
    ppermute x14, starting transfers between devices: 18.5 us -> 16.7 us  [over_pw(): return lax.ppermute(x, 'pw', [(i, i ^ bits) for i in range(32)])]
    ppermute x14, waiting for transfers between devices: 9.75 us -> 11 us  [over_pw(): return lax.ppermute(x, 'pw', [(i, i ^ bits) for i in range(32)])]
  transfers between devices with their start and end apart: 21 -> 21, of which waited for: 9 -> 13; matrix products, arithmetic and copies ran while one was open for 0% -> 0% of each run, Pallas kernels for 7% -> 8%
where the time goes in v8:
time: 51.2 us; the launch traced here: 51.1 us
  starting transfers between devices  31.4 us (61%)
  waiting for transfers between devices  11.7 us (23%)
  Pallas kernels  7.57 us (15%)
    ppermute x14, starting transfers between devices, over_pw(): return lax.ppermute(x, 'pw', [(i, i ^ bits) for i in range(32)])  16.7 us
    ppermute x7, starting transfers between devices, over_band(): return lax.ppermute(x, 'band', [(i, i ^ bits) for i in range(8)])  14.7 us
    ppermute x14, waiting for transfers between devices, over_pw(): return lax.ppermute(x, 'pw', [(i, i ^ bits) for i in range(32)])  11 us
    pallas_call x1, Pallas kernels, spread_back(): pl.pallas_call(spread_kernel, out_shape=jax.ShapeDtypeStruct((2, NPW_DEV,...  2.58 us
    pallas_call x1, Pallas kernels, ahead(): pl.pallas_call(ahead_kernel, out_shape=(jax.ShapeDtypeStruct((2, NP, 3 *...  2.35 us
    pallas_call x1, Pallas kernels, project_near(): pl.pallas_call(near_kernel, out_shape=jax.ShapeDtypeStruct((2, NP, NB_DEV...  1.17 us
    pallas_call x1, Pallas kernels, project_far(): pl.pallas_call(far_kernel, out_shape=halves, in_specs=[smem()] + [vmem()]...  1.15 us
  transfers between devices with their start and end apart: 21, of which 13 were waited for; matrix products, arithmetic and copies ran while one was open for 0% of the time, Pallas kernels for 8%

profile of v8, /device:TPU:1, one launch (start us, length us, event | category | flops | bytes accessed | tf_op | source)
XLA Modules:
  0.0 51.1 jit_solution(18108342834271065071)
XLA Ops:
  0.0 7.7 %collective-permute-start = (bf16[2,16,1280]{2,1,0:T(8,128)(2,1)}, bf16[2,16,1280]{2,1,0:T(8,128)(2,1)S(1)}, u32[]{:S(2)}, u32[]{:S(2)}) collective-permute-start(bf16[2,16,1280]{2,1,0:T(8,128)(2,1)} %refs_3_.3), channel_id=1, source_target_pairs={{0,1},{1,0},{2,3},{3,2},{4,5},{5,4},{6,7},{7,6},{8,9},{9,8},{10,11... | collective-permute-start | bytes 245768 | tf_op jit(solution)/shard_map/ppermute | solution.py:29
  7.7 2.5 %collective-permute-start.1 = (bf16[2,16,1280]{2,1,0:T(8,128)(2,1)}, bf16[2,16,1280]{2,1,0:T(8,128)(2,1)S(1)}, u32[]{:S(2)}, u32[]{:S(2)}) collective-permute-start(bf16[2,16,1280]{2,1,0:T(8,128)(2,1)} %refs_3_.3), channel_id=1, source_target_pairs={{0,6},{1,7},{2,4},{3,5},{4,2},{5,3},{6,0},{7,1},{8,14},{9,15},{10,... | collective-permute-start | bytes 245768 | tf_op jit(solution)/shard_map/ppermute | solution.py:29
  10.2 0.5 %collective-permute-start.2 = (bf16[2,16,1280]{2,1,0:T(8,128)(2,1)}, bf16[2,16,1280]{2,1,0:T(8,128)(2,1)S(1)}, u32[]{:S(2)}, u32[]{:S(2)}) collective-permute-start(bf16[2,16,1280]{2,1,0:T(8,128)(2,1)} %refs_3_.3), channel_id=1, source_target_pairs={{0,4},{1,5},{2,6},{3,7},{4,0},{5,1},{6,2},{7,3},{8,12},{9,13},{10,... | collective-permute-start | bytes 245768 | tf_op jit(solution)/shard_map/ppermute | solution.py:29
  10.7 0.3 collective-permute-start.3
  11.1 2.8 %collective-permute-start.4 = (bf16[2,16,1280]{2,1,0:T(8,128)(2,1)S(1)}, bf16[2,16,1280]{2,1,0:T(8,128)(2,1)S(1)}, u32[]{:S(2)}, u32[]{:S(2)}) collective-permute-start(bf16[2,16,1280]{2,1,0:T(8,128)(2,1)S(1)} %collective-permute-done.refs_3_.refs_7_), channel_id=1, source_target_pairs={{0,4},{1,5},{2,6},{3,7},{4,0},{5,1},{6,2},{7,3},{8,12},{9,13},{10,... | collective-permute-start | bytes 245768 | tf_op jit(solution)/shard_map/ppermute | solution.py:29
  14.0 0.9 %collective-permute-start.5 = (bf16[2,16,1280]{2,1,0:T(8,128)(2,1)S(1)}, bf16[2,16,1280]{2,1,0:T(8,128)(2,1)S(1)}, u32[]{:S(2)}, u32[]{:S(2)}) collective-permute-start(bf16[2,16,1280]{2,1,0:T(8,128)(2,1)S(1)} %collective-permute-done.refs_3_.refs_7_), channel_id=1, source_target_pairs={{0,6},{1,7},{2,4},{3,5},{4,2},{5,3},{6,0},{7,1},{8,14},{9,15},{10,... | collective-permute-start | bytes 245768 | tf_op jit(solution)/shard_map/ppermute | solution.py:29
  14.9 2.3 %shard_map.56 = (bf16[2,128,192]{2,1,0:T(8,128)(2,1)S(1)}, bf16[2,1280,896]{2,1,0:T(8,128)(2,1)S(1)}) custom-call(bf16[2,128,128]{2,1,0:T(8,128)(2,1)S(1)} %shard_map.55.pick_ref, s32[12]{0:T(128)S(1)} %copy-done.2, s32[12]{0:T(128)S(1)} %copy-done.3, f32[12,13,13]{2,1,0:T(8,128)S(1)} %copy-done.1, bf16[2,1280,896]{2,1,0:T(8,128)(2,1)} %waves_hbm.1), custom_call_target="tpu_custom_call" | custom-call | flops 2000000000 | bytes 8388608 | tf_op jit(solution)/shard_map/pallas_call | solution.py:129
  17.2 1.2 %shard_map.57.near_ref = f32[2,128,896]{2,1,0:T(8,128)S(1)} custom-call(bf16[2,128,192]{2,1,0:T(8,128)(2,1)S(1)} %get-tuple-element.11.left_ref, bf16[2,1280,896]{2,1,0:T(8,128)(2,1)S(1)} %get-tuple-element.12.waves_ref, bf16[2,16,1280]{2,1,0:T(8,128)(2,1)S(1)} %collective-permute-done.1.refs_0_, bf16[2,16,1280]{2,1,0:T(8,128)(2,1)S(1)} %collective-permute-done.2.refs_1_, ...), custom_call_target="tpu_custom_call" | custom-call | flops 587202560 | bytes 6291456 | tf_op jit(solution)/shard_map/pallas_call | solution.py:173
  18.4 0.3 collective-permute-done.5.refs_1_.refs_5_
  18.7 0.3 collective-permute-done.6.refs_2_.refs_6_
  19.1 1.2 %shard_map.58 = (f32[128,896]{1,0:T(8,128)S(1)}, bf16[128,896]{1,0:T(8,128)(2,1)S(1)}) custom-call(s32[1]{0:T(128)} %bitcast.core_ref, f32[2,128,896]{2,1,0:T(8,128)S(1)} %shard_map.57.near_ref, bf16[2,128,192]{2,1,0:T(8,128)(2,1)S(1)} %get-tuple-element.11.left_ref, bf16[2,1280,896]{2,1,0:T(8,128)(2,1)S(1)} %get-tuple-element.12.waves_ref, ...), custom_call_target="tpu_custom_call" | custom-call | flops 587202560 | bytes 6291456 | tf_op jit(solution)/shard_map/pallas_call | solution.py:203
  20.2 2.9 %collective-permute-start.7 = (bf16[128,896]{1,0:T(8,128)(2,1)S(1)}, bf16[128,896]{1,0:T(8,128)(2,1)S(1)}, u32[]{:S(2)}, u32[]{:S(2)}) collective-permute-start(bf16[128,896]{1,0:T(8,128)(2,1)S(1)} %get-tuple-element.14), channel_id=1, source_target_pairs={{0,8},{8,0},{16,24},{24,16},{32,40},{40,32},{48,56},{56,48},{64,72... | collective-permute-start | bytes 688136 | tf_op jit(solution)/shard_map/ppermute | solution.py:25
  23.1 1.1 %collective-permute-done.7 = bf16[128,896]{1,0:T(8,128)(2,1)S(1)} collective-permute-done((bf16[128,896]{1,0:T(8,128)(2,1)S(1)}, bf16[128,896]{1,0:T(8,128)(2,1)S(1)}, u32[]{:S(2)}, u32[]{:S(2)}) %collective-permute-start.7) | collective-permute-done | bytes 229408 | tf_op jit(solution)/shard_map/ppermute | solution.py:25
  24.3 3.0 %collective-permute-start.10 = (bf16[32,896]{1,0:T(8,128)(2,1)S(1)}, bf16[32,896]{1,0:T(8,128)(2,1)S(1)}, u32[]{:S(2)}, u32[]{:S(2)}) collective-permute-start(bf16[32,896]{1,0:T(8,128)(2,1)S(1)} %get-tuple-element.18), channel_id=1, source_target_pairs={{0,32},{8,40},{16,48},{24,56},{32,0},{40,8},{48,16},{56,24},{64,96... | collective-permute-start | bytes 172040 | tf_op jit(solution)/shard_map/ppermute | solution.py:25
  27.3 0.8 %collective-permute-start.8 = (bf16[32,896]{1,0:T(8,128)(2,1)S(1)}, bf16[32,896]{1,0:T(8,128)(2,1)S(1)}, u32[]{:S(2)}, u32[]{:S(2)}) collective-permute-start(bf16[32,896]{1,0:T(8,128)(2,1)S(1)} %get-tuple-element.17), channel_id=1, source_target_pairs={{0,48},{8,56},{16,32},{24,40},{32,16},{40,24},{48,0},{56,8},{64,11... | collective-permute-start | bytes 172040 | tf_op jit(solution)/shard_map/ppermute | solution.py:25
  28.0 0.8 %collective-permute-done.10 = bf16[32,896]{1,0:T(8,128)(2,1)S(1)} collective-permute-done((bf16[32,896]{1,0:T(8,128)(2,1)S(1)}, bf16[32,896]{1,0:T(8,128)(2,1)S(1)}, u32[]{:S(2)}, u32[]{:S(2)}) %collective-permute-start.10) | collective-permute-done | bytes 57376 | tf_op jit(solution)/shard_map/ppermute | solution.py:25
  28.9 2.6 %collective-permute-done.8 = bf16[32,896]{1,0:T(8,128)(2,1)S(1)} collective-permute-done((bf16[32,896]{1,0:T(8,128)(2,1)S(1)}, bf16[32,896]{1,0:T(8,128)(2,1)S(1)}, u32[]{:S(2)}, u32[]{:S(2)}) %collective-permute-start.8) | collective-permute-done | bytes 57376 | tf_op jit(solution)/shard_map/ppermute | solution.py:25
  31.5 1.7 %collective-permute-start.11 = (bf16[32,896]{1,0:T(8,128)(2,1)S(1)}, bf16[32,896]{1,0:T(8,128)(2,1)S(1)}, u32[]{:S(2)}, u32[]{:S(2)}) collective-permute-start(bf16[32,896]{1,0:T(8,128)(2,1)S(1)} %fusion.2), channel_id=1, source_target_pairs={{0,192},{8,200},{16,208},{24,216},{32,224},{40,232},{48,240},{56,2... | collective-permute-start | bytes 172040 | tf_op jit(solution)/shard_map/ppermute | solution.py:25
  33.4 1.8 %collective-permute-start.13 = (bf16[32,896]{1,0:T(8,128)(2,1)S(1)}, bf16[32,896]{1,0:T(8,128)(2,1)S(1)}, u32[]{:S(2)}, u32[]{:S(2)}) collective-permute-start(bf16[32,896]{1,0:T(8,128)(2,1)S(1)} %fusion.2), channel_id=1, source_target_pairs={{0,128},{8,136},{16,144},{24,152},{32,160},{40,168},{48,176},{56,1... | collective-permute-start | bytes 172040 | tf_op jit(solution)/shard_map/ppermute | solution.py:25
  35.2 1.4 %collective-permute-done.11 = bf16[32,896]{1,0:T(8,128)(2,1)S(1)} collective-permute-done((bf16[32,896]{1,0:T(8,128)(2,1)S(1)}, bf16[32,896]{1,0:T(8,128)(2,1)S(1)}, u32[]{:S(2)}, u32[]{:S(2)}) %collective-permute-start.11) | collective-permute-done | bytes 57376 | tf_op jit(solution)/shard_map/ppermute | solution.py:25
  36.6 0.6 %collective-permute-done.12 = bf16[32,896]{1,0:T(8,128)(2,1)S(1)} collective-permute-done((bf16[32,896]{1,0:T(8,128)(2,1)S(1)}, bf16[32,896]{1,0:T(8,128)(2,1)S(1)}, u32[]{:S(2)}, u32[]{:S(2)}) %collective-permute-start.12) | collective-permute-done | bytes 57376 | tf_op jit(solution)/shard_map/ppermute | solution.py:25
  37.1 2.2 %collective-permute-done.13 = bf16[32,896]{1,0:T(8,128)(2,1)S(1)} collective-permute-done((bf16[32,896]{1,0:T(8,128)(2,1)S(1)}, bf16[32,896]{1,0:T(8,128)(2,1)S(1)}, u32[]{:S(2)}, u32[]{:S(2)}) %collective-permute-start.13) | collective-permute-done | bytes 57376 | tf_op jit(solution)/shard_map/ppermute | solution.py:25
  39.4 2.7 %collective-permute-start.14 = (bf16[32,896]{1,0:T(8,128)(2,1)S(1)}, bf16[32,896]{1,0:T(8,128)(2,1)S(1)}, u32[]{:S(2)}, u32[]{:S(2)}) collective-permute-start(bf16[32,896]{1,0:T(8,128)(2,1)S(1)} %add_convert_fusion.refs_0_), channel_id=1, source_target_pairs={{0,40},{8,32},{16,56},{24,48},{32,8},{40,0},{48,24},{56,16},{64,10... | collective-permute-start | bytes 172040 | tf_op jit(solution)/shard_map/ppermute | solution.py:25
  42.1 0.8 %collective-permute-start.15 = (bf16[32,896]{1,0:T(8,128)(2,1)S(1)}, bf16[32,896]{1,0:T(8,128)(2,1)S(1)}, u32[]{:S(2)}, u32[]{:S(2)}) collective-permute-start(bf16[32,896]{1,0:T(8,128)(2,1)S(1)} %add_convert_fusion.refs_0_), channel_id=1, source_target_pairs={{0,56},{8,48},{16,40},{24,32},{32,24},{40,16},{48,8},{56,0},{64,12... | collective-permute-start | bytes 172040 | tf_op jit(solution)/shard_map/ppermute | solution.py:25
  42.9 0.9 %collective-permute-start.16 = (bf16[32,896]{1,0:T(8,128)(2,1)S(1)}, bf16[32,896]{1,0:T(8,128)(2,1)S(1)}, u32[]{:S(2)}, u32[]{:S(2)}) collective-permute-start(bf16[32,896]{1,0:T(8,128)(2,1)S(1)} %add_convert_fusion.refs_0_), channel_id=1, source_target_pairs={{0,24},{8,16},{16,8},{24,0},{32,56},{40,48},{48,40},{56,32},{64,88... | collective-permute-start | bytes 172040 | tf_op jit(solution)/shard_map/ppermute | solution.py:25
  43.8 0.8 %collective-permute-done.14.refs_1_ = bf16[32,896]{1,0:T(8,128)(2,1)S(1)} collective-permute-done((bf16[32,896]{1,0:T(8,128)(2,1)S(1)}, bf16[32,896]{1,0:T(8,128)(2,1)S(1)}, u32[]{:S(2)}, u32[]{:S(2)}) %collective-permute-start.14) | collective-permute-done | bytes 57376 | tf_op jit(solution)/shard_map/ppermute | solution.py:25
  44.6 1.6 %collective-permute-start.18 = (bf16[32,896]{1,0:T(8,128)(2,1)S(1)}, bf16[32,896]{1,0:T(8,128)(2,1)S(1)}, u32[]{:S(2)}, u32[]{:S(2)}) collective-permute-start(bf16[32,896]{1,0:T(8,128)(2,1)S(1)} %collective-permute-done.14.refs_1_), channel_id=1, source_target_pairs={{0,8},{8,0},{16,24},{24,16},{32,40},{40,32},{48,56},{56,48},{64,72... | collective-permute-start | bytes 172040 | tf_op jit(solution)/shard_map/ppermute | solution.py:25
  46.2 0.7 %collective-permute-done.15.refs_2_ = bf16[32,896]{1,0:T(8,128)(2,1)S(1)} collective-permute-done((bf16[32,896]{1,0:T(8,128)(2,1)S(1)}, bf16[32,896]{1,0:T(8,128)(2,1)S(1)}, u32[]{:S(2)}, u32[]{:S(2)}) %collective-permute-start.15) | collective-permute-done | bytes 57376 | tf_op jit(solution)/shard_map/ppermute | solution.py:25
  47.1 0.4 collective-permute-start.20
  47.5 0.2 shard_map.59.refs_8_
  47.8 0.4 collective-permute-done.19.refs_6_
  48.4 2.6 %shard_map.60 = bf16[2,1280,896]{2,1,0:T(8,128)(2,1)} custom-call(s32[1]{0:T(128)} %bitcast.core_ref, s32[1]{0:T(128)} %bitcast.1.y_ref, bf16[32,896]{1,0:T(8,128)(2,1)S(1)} %add_convert_fusion.refs_0_, bf16[32,896]{1,0:T(8,128)(2,1)S(1)} %collective-permute-done.14.refs_1_, bf16[32,896]{1,0:T(8,128)(2,1)S(1)} %collective-permute-done.15.refs_2_, ...), custom_call_target="tpu_custom_call" | custom-call | flops 1174405120 | bytes 6291456 | tf_op jit(solution)/shard_map/pallas_call | solution.py:269
  (28 shorter events, 0.8 us)
Async XLA Ops:
  0.0 11.1 %collective-permute-start = (bf16[2,16,1280]{2,1,0:T(8,128)(2,1)}, bf16[2,16,1280]{2,1,0:T(8,128)(2,1)S(1)}, u32[]{:S(2)}, u32[]{:S(2)}) collective-permute-start(bf16[2,16,1280]{2,1,0:T(8,128)(2,1)} %refs_3_.3), channel_id=1, source_target_pairs={{0,1},{1,0},{2,3},{3,2},{4,5},{5,4},{6,7},{7,6},{8,9},{9,8},{10,11... | collective-permute-start | bytes 245768 | tf_op jit(solution)/shard_map/ppermute | solution.py:29
  7.7 7.1 %collective-permute-start.1 = (bf16[2,16,1280]{2,1,0:T(8,128)(2,1)}, bf16[2,16,1280]{2,1,0:T(8,128)(2,1)S(1)}, u32[]{:S(2)}, u32[]{:S(2)}) collective-permute-start(bf16[2,16,1280]{2,1,0:T(8,128)(2,1)} %refs_3_.3), channel_id=1, source_target_pairs={{0,6},{1,7},{2,4},{3,5},{4,2},{5,3},{6,0},{7,1},{8,14},{9,15},{10,... | collective-permute-start | bytes 245768 | tf_op jit(solution)/shard_map/ppermute | solution.py:29
  10.2 7.0 %collective-permute-start.2 = (bf16[2,16,1280]{2,1,0:T(8,128)(2,1)}, bf16[2,16,1280]{2,1,0:T(8,128)(2,1)S(1)}, u32[]{:S(2)}, u32[]{:S(2)}) collective-permute-start(bf16[2,16,1280]{2,1,0:T(8,128)(2,1)} %refs_3_.3), channel_id=1, source_target_pairs={{0,4},{1,5},{2,6},{3,7},{4,0},{5,1},{6,2},{7,3},{8,12},{9,13},{10,... | collective-permute-start | bytes 245768 | tf_op jit(solution)/shard_map/ppermute | solution.py:29
  10.7 6.5 %collective-permute-start.3 = (bf16[2,16,1280]{2,1,0:T(8,128)(2,1)}, bf16[2,16,1280]{2,1,0:T(8,128)(2,1)S(1)}, u32[]{:S(2)}, u32[]{:S(2)}) collective-permute-start(bf16[2,16,1280]{2,1,0:T(8,128)(2,1)} %refs_3_.3), channel_id=1, source_target_pairs={{0,2},{1,3},{2,0},{3,1},{4,6},{5,7},{6,4},{7,5},{8,10},{9,11},{10,... | collective-permute-start | bytes 245768 | tf_op jit(solution)/shard_map/ppermute | solution.py:29
  11.0 3.8 %copy-start.1 = (f32[12,13,13]{2,1,0:T(8,128)S(1)}, f32[12,13,13]{2,1,0:T(8,128)}, u32[]{:S(2)}) copy-start(f32[12,13,13]{2,1,0:T(8,128)} %coupling_hbm.1) | copy-start | bytes 24340
  11.0 3.8 %copy-start.2 = (s32[12]{0:T(128)S(1)}, s32[12]{0:T(128)}, u32[]{:S(2)}) copy-start(s32[12]{0:T(128)} %offsets_hbm.1) | copy-start | bytes 148
  11.0 3.9 %copy-start.3 = (s32[12]{0:T(128)S(1)}, s32[12]{0:T(128)}, u32[]{:S(2)}) copy-start(s32[12]{0:T(128)} %counts_hbm.1) | copy-start | bytes 148
  11.1 6.1 %copy-start = (bf16[2,16,1280]{2,1,0:T(8,128)(2,1)S(1)}, bf16[2,16,1280]{2,1,0:T(8,128)(2,1)}, u32[]{:S(2)}) copy-start(bf16[2,16,1280]{2,1,0:T(8,128)(2,1)} %refs_3_.3) | copy-start | bytes 245764
  11.1 7.3 %collective-permute-start.4 = (bf16[2,16,1280]{2,1,0:T(8,128)(2,1)S(1)}, bf16[2,16,1280]{2,1,0:T(8,128)(2,1)S(1)}, u32[]{:S(2)}, u32[]{:S(2)}) collective-permute-start(bf16[2,16,1280]{2,1,0:T(8,128)(2,1)S(1)} %collective-permute-done.refs_3_.refs_7_), channel_id=1, source_target_pairs={{0,4},{1,5},{2,6},{3,7},{4,0},{5,1},{6,2},{7,3},{8,12},{9,13},{10,... | collective-permute-start | bytes 245768 | tf_op jit(solution)/shard_map/ppermute | solution.py:29
  14.0 4.8 %collective-permute-start.5 = (bf16[2,16,1280]{2,1,0:T(8,128)(2,1)S(1)}, bf16[2,16,1280]{2,1,0:T(8,128)(2,1)S(1)}, u32[]{:S(2)}, u32[]{:S(2)}) collective-permute-start(bf16[2,16,1280]{2,1,0:T(8,128)(2,1)S(1)} %collective-permute-done.refs_3_.refs_7_), channel_id=1, source_target_pairs={{0,6},{1,7},{2,4},{3,5},{4,2},{5,3},{6,0},{7,1},{8,14},{9,15},{10,... | collective-permute-start | bytes 245768 | tf_op jit(solution)/shard_map/ppermute | solution.py:29
  14.8 4.2 %collective-permute-start.6 = (bf16[2,16,1280]{2,1,0:T(8,128)(2,1)S(1)}, bf16[2,16,1280]{2,1,0:T(8,128)(2,1)S(1)}, u32[]{:S(2)}, u32[]{:S(2)}) collective-permute-start(bf16[2,16,1280]{2,1,0:T(8,128)(2,1)S(1)} %collective-permute-done.refs_3_.refs_7_), channel_id=1, source_target_pairs={{0,2},{1,3},{2,0},{3,1},{4,6},{5,7},{6,4},{7,5},{8,10},{9,11},{10,... | collective-permute-start | bytes 245768 | tf_op jit(solution)/shard_map/ppermute | solution.py:29
  20.2 4.0 %collective-permute-start.7 = (bf16[128,896]{1,0:T(8,128)(2,1)S(1)}, bf16[128,896]{1,0:T(8,128)(2,1)S(1)}, u32[]{:S(2)}, u32[]{:S(2)}) collective-permute-start(bf16[128,896]{1,0:T(8,128)(2,1)S(1)} %get-tuple-element.14), channel_id=1, source_target_pairs={{0,8},{8,0},{16,24},{24,16},{32,40},{40,32},{48,56},{56,48},{64,72... | collective-permute-start | bytes 688136 | tf_op jit(solution)/shard_map/ppermute | solution.py:25
  24.3 4.6 %collective-permute-start.10 = (bf16[32,896]{1,0:T(8,128)(2,1)S(1)}, bf16[32,896]{1,0:T(8,128)(2,1)S(1)}, u32[]{:S(2)}, u32[]{:S(2)}) collective-permute-start(bf16[32,896]{1,0:T(8,128)(2,1)S(1)} %get-tuple-element.18), channel_id=1, source_target_pairs={{0,32},{8,40},{16,48},{24,56},{32,0},{40,8},{48,16},{56,24},{64,96... | collective-permute-start | bytes 172040 | tf_op jit(solution)/shard_map/ppermute | solution.py:25
  27.3 4.2 %collective-permute-start.8 = (bf16[32,896]{1,0:T(8,128)(2,1)S(1)}, bf16[32,896]{1,0:T(8,128)(2,1)S(1)}, u32[]{:S(2)}, u32[]{:S(2)}) collective-permute-start(bf16[32,896]{1,0:T(8,128)(2,1)S(1)} %get-tuple-element.17), channel_id=1, source_target_pairs={{0,48},{8,56},{16,32},{24,40},{32,16},{40,24},{48,0},{56,8},{64,11... | collective-permute-start | bytes 172040 | tf_op jit(solution)/shard_map/ppermute | solution.py:25
  28.0 3.5 %collective-permute-start.9 = (bf16[32,896]{1,0:T(8,128)(2,1)S(1)}, bf16[32,896]{1,0:T(8,128)(2,1)S(1)}, u32[]{:S(2)}, u32[]{:S(2)}) collective-permute-start(bf16[32,896]{1,0:T(8,128)(2,1)S(1)} %get-tuple-element.19), channel_id=1, source_target_pairs={{0,16},{8,24},{16,0},{24,8},{32,48},{40,56},{48,32},{56,40},{64,80... | collective-permute-start | bytes 172040 | tf_op jit(solution)/shard_map/ppermute | solution.py:25
  31.5 5.0 %collective-permute-start.11 = (bf16[32,896]{1,0:T(8,128)(2,1)S(1)}, bf16[32,896]{1,0:T(8,128)(2,1)S(1)}, u32[]{:S(2)}, u32[]{:S(2)}) collective-permute-start(bf16[32,896]{1,0:T(8,128)(2,1)S(1)} %fusion.2), channel_id=1, source_target_pairs={{0,192},{8,200},{16,208},{24,216},{32,224},{40,232},{48,240},{56,2... | collective-permute-start | bytes 172040 | tf_op jit(solution)/shard_map/ppermute | solution.py:25
  33.3 3.9 %collective-permute-start.12 = (bf16[32,896]{1,0:T(8,128)(2,1)S(1)}, bf16[32,896]{1,0:T(8,128)(2,1)S(1)}, u32[]{:S(2)}, u32[]{:S(2)}) collective-permute-start(bf16[32,896]{1,0:T(8,128)(2,1)S(1)} %fusion.2), channel_id=1, source_target_pairs={{0,64},{8,72},{16,80},{24,88},{32,96},{40,104},{48,112},{56,120},{... | collective-permute-start | bytes 172040 | tf_op jit(solution)/shard_map/ppermute | solution.py:25
  33.4 5.9 %collective-permute-start.13 = (bf16[32,896]{1,0:T(8,128)(2,1)S(1)}, bf16[32,896]{1,0:T(8,128)(2,1)S(1)}, u32[]{:S(2)}, u32[]{:S(2)}) collective-permute-start(bf16[32,896]{1,0:T(8,128)(2,1)S(1)} %fusion.2), channel_id=1, source_target_pairs={{0,128},{8,136},{16,144},{24,152},{32,160},{40,168},{48,176},{56,1... | collective-permute-start | bytes 172040 | tf_op jit(solution)/shard_map/ppermute | solution.py:25
  39.4 5.2 %collective-permute-start.14 = (bf16[32,896]{1,0:T(8,128)(2,1)S(1)}, bf16[32,896]{1,0:T(8,128)(2,1)S(1)}, u32[]{:S(2)}, u32[]{:S(2)}) collective-permute-start(bf16[32,896]{1,0:T(8,128)(2,1)S(1)} %add_convert_fusion.refs_0_), channel_id=1, source_target_pairs={{0,40},{8,32},{16,56},{24,48},{32,8},{40,0},{48,24},{56,16},{64,10... | collective-permute-start | bytes 172040 | tf_op jit(solution)/shard_map/ppermute | solution.py:25
  42.1 4.8 %collective-permute-start.15 = (bf16[32,896]{1,0:T(8,128)(2,1)S(1)}, bf16[32,896]{1,0:T(8,128)(2,1)S(1)}, u32[]{:S(2)}, u32[]{:S(2)}) collective-permute-start(bf16[32,896]{1,0:T(8,128)(2,1)S(1)} %add_convert_fusion.refs_0_), channel_id=1, source_target_pairs={{0,56},{8,48},{16,40},{24,32},{32,24},{40,16},{48,8},{56,0},{64,12... | collective-permute-start | bytes 172040 | tf_op jit(solution)/shard_map/ppermute | solution.py:25
  42.9 4.2 %collective-permute-start.16 = (bf16[32,896]{1,0:T(8,128)(2,1)S(1)}, bf16[32,896]{1,0:T(8,128)(2,1)S(1)}, u32[]{:S(2)}, u32[]{:S(2)}) collective-permute-start(bf16[32,896]{1,0:T(8,128)(2,1)S(1)} %add_convert_fusion.refs_0_), channel_id=1, source_target_pairs={{0,24},{8,16},{16,8},{24,0},{32,56},{40,48},{48,40},{56,32},{64,88... | collective-permute-start | bytes 172040 | tf_op jit(solution)/shard_map/ppermute | solution.py:25
  43.8 3.9 %collective-permute-start.17 = (bf16[32,896]{1,0:T(8,128)(2,1)S(1)}, bf16[32,896]{1,0:T(8,128)(2,1)S(1)}, u32[]{:S(2)}, u32[]{:S(2)}) collective-permute-start(bf16[32,896]{1,0:T(8,128)(2,1)S(1)} %add_convert_fusion.refs_0_), channel_id=1, source_target_pairs={{0,8},{8,0},{16,24},{24,16},{32,40},{40,32},{48,56},{56,48},{64,72... | collective-permute-start | bytes 172040 | tf_op jit(solution)/shard_map/ppermute | solution.py:25
  44.6 3.1 %collective-permute-start.18 = (bf16[32,896]{1,0:T(8,128)(2,1)S(1)}, bf16[32,896]{1,0:T(8,128)(2,1)S(1)}, u32[]{:S(2)}, u32[]{:S(2)}) collective-permute-start(bf16[32,896]{1,0:T(8,128)(2,1)S(1)} %collective-permute-done.14.refs_1_), channel_id=1, source_target_pairs={{0,8},{8,0},{16,24},{24,16},{32,40},{40,32},{48,56},{56,48},{64,72... | collective-permute-start | bytes 172040 | tf_op jit(solution)/shard_map/ppermute | solution.py:25
  47.0 1.2 %collective-permute-start.19 = (bf16[32,896]{1,0:T(8,128)(2,1)S(1)}, bf16[32,896]{1,0:T(8,128)(2,1)S(1)}, u32[]{:S(2)}, u32[]{:S(2)}) collective-permute-start(bf16[32,896]{1,0:T(8,128)(2,1)S(1)} %collective-permute-done.15.refs_2_), channel_id=1, source_target_pairs={{0,8},{8,0},{16,24},{24,16},{32,40},{40,32},{48,56},{56,48},{64,72... | collective-permute-start | bytes 172040 | tf_op jit(solution)/shard_map/ppermute | solution.py:25
  47.1 1.3 %collective-permute-start.20 = (bf16[32,896]{1,0:T(8,128)(2,1)S(1)}, bf16[32,896]{1,0:T(8,128)(2,1)S(1)}, u32[]{:S(2)}, u32[]{:S(2)}) collective-permute-start(bf16[32,896]{1,0:T(8,128)(2,1)S(1)} %collective-permute-done.16.refs_3_), channel_id=1, source_target_pairs={{0,8},{8,0},{16,24},{24,16},{32,40},{40,32},{48,56},{56,48},{64,72... | collective-permute-start | bytes 172040 | tf_op jit(solution)/shard_map/ppermute | solution.py:25

commit v9 on v8

--- a/solution.py
+++ b/solution.py
@@ -56,19 +56,17 @@
     counts_hbm,
     coupling_hbm,
     waves_hbm,
-    left_ref,
-    waves_ref,
-    placed_ref,
-    offsets_ref,
-    counts_ref,
-    coupling_ref,
-    sem,
+    *refs,
 ):
+    pieces = refs[:4]
+    left_ref, waves_ref, near_ref = refs[4:7]
+    placed_ref, offsets_ref, counts_ref, coupling_ref, rows_ref, sem = refs[7:]
     pairs = (
         (offsets_hbm, offsets_ref),
         (counts_hbm, counts_ref),
         (coupling_hbm, coupling_ref),
-        (waves_hbm, waves_ref),
+        (waves_hbm.at[0], waves_ref.at[0]),
+        (waves_hbm.at[1], waves_ref.at[1]),
     )
     copies = [pltpu.make_async_copy(a, b, sem.at[i]) for i, (a, b) in enumerate(pairs)]
     for copy in copies:
@@ -97,7 +95,9 @@
         left_ref[h] = jnp.concatenate(
             [high[:, columns], high[:, columns], low[:, columns]], axis=1
         )
-    copies[3].wait()
+    near_ref[0], near_ref[1] = coupled_parts(
+        0, pieces, left_ref, waves_ref, rows_ref, copies[3:]
+    )
 
 
 def pick_kernel(y_ref, band_ref, pick_ref):
@@ -124,35 +124,41 @@
     )(y, band)
 
 
-def ahead(pick, offsets, counts, coupling, waves):
+def ahead(pick, offsets, counts, coupling, waves, pieces):
     hbm = pl.BlockSpec(memory_space=pltpu.HBM)
     return pl.pallas_call(
         ahead_kernel,
         out_shape=(
             jax.ShapeDtypeStruct((2, NP, 3 * HALF), BF16),
             jax.ShapeDtypeStruct(waves.shape, BF16),
+            jax.ShapeDtypeStruct((2, NP, NB_DEV), F32),
         ),
-        in_specs=[vmem()] + [hbm] * 4,
-        out_specs=(vmem(), vmem()),
+        in_specs=[vmem()] + [hbm] * 4 + [vmem()] * 4,
+        out_specs=(vmem(), vmem(), vmem()),
         scratch_shapes=[
             pltpu.VMEM((NP + ROWS, NP), F32),
             pltpu.SMEM((NATOM,), jnp.int32),
             pltpu.SMEM((NATOM,), jnp.int32),
             pltpu.VMEM((NATOM, M, M), F32),
-            pltpu.SemaphoreType.DMA((4,)),
+            pltpu.VMEM((NP, NPW_DEV), BF16),
+            pltpu.SemaphoreType.DMA((5,)),
         ],
         compiler_params=params(46),
         cost_estimate=cost(2 * 10**9, 8 * MIB),
-    )(pick, offsets, counts, coupling, waves)
-
-
-def coupled_parts(h, pieces, left_ref, waves_ref, rows_ref):
+    )(pick, offsets, counts, coupling, waves, *pieces)
+
+
+def coupled_parts(h, pieces, left_ref, waves_ref, rows_ref, copies=()):
     for i, piece in enumerate(pieces):
         at = ORDER[h][i] * ROWS
         rows_ref[pl.ds(at, ROWS), :] = piece[0]
         rows_ref[pl.ds(HALF + at, ROWS), :] = piece[1]
     rows = rows_ref[...]
+    for copy in copies[:1]:
+        copy.wait()
     first = jnp.dot(rows, waves_ref[0], preferred_element_type=F32)
+    for copy in copies[1:]:
+        copy.wait()
     second = jnp.dot(rows, waves_ref[1], preferred_element_type=F32)
     left = left_ref[h]
 
@@ -162,23 +168,6 @@
         return jnp.dot(left, right, preferred_element_type=F32)
 
     return couple(first[:HALF] + second[HALF:]), couple(second[:HALF] - first[HALF:])
-
-
-def near_kernel(left_ref, waves_ref, *refs):
-    pieces, (out_ref, rows_ref) = refs[:4], refs[4:]
-    out_ref[0], out_ref[1] = coupled_parts(0, pieces, left_ref, waves_ref, rows_ref)
-
-
-def project_near(left, waves, pieces):
-    return pl.pallas_call(
-        near_kernel,
-        out_shape=jax.ShapeDtypeStruct((2, NP, NB_DEV), F32),
-        in_specs=[vmem()] * 6,
-        out_specs=vmem(),
-        scratch_shapes=[pltpu.VMEM((NP, NPW_DEV), BF16)],
-        compiler_params=params(16),
-        cost_estimate=cost(4 * NP * NPW_DEV * NB_DEV, 6 * MIB),
-    )(left, waves, *pieces)
 
 
 def far_kernel(core_ref, near_ref, left_ref, waves_ref, *refs):
@@ -290,8 +279,7 @@
     far = [over_band(distant, bits) for bits in (4, 6, 2)] + [distant]
     pick = gathered_order(y, band)
     pick, _ = lax.optimization_barrier((pick, distant))
-    left, waves = ahead(pick, offsets, counts, coupling, waves)
-    sums = project_near(left, waves, near)
+    left, waves, sums = ahead(pick, offsets, counts, coupling, waves, near)
     keep, send = project_far(core, sums, left, waves, far)
     turned = turn(near + far)
     total = (keep + over_pw(send, 1).astype(F32)).reshape(4, CHUNK, NB_DEV)

time: 51.2 us -> 51.3 us (level)
    pallas_call x1 -> x0, Pallas kernels: 1.17 us -> none  [project_near(): pl.pallas_call(near_kernel, out_shape=jax.ShapeDtypeStruct((2, NP, NB_DEV...]
    pallas_call x1, Pallas kernels: 2.35 us -> 3.19 us  [ahead(): pl.pallas_call(ahead_kernel, out_shape=(jax.ShapeDtypeStruct((2, NP, 3 *...]
  transfers between devices with their start and end apart: 21 -> 21, of which waited for: 13 -> 14; matrix products, arithmetic and copies ran while one was open for 0% -> 0% of each run, Pallas kernels for 8% -> 7%
where the time goes in v9:
time: 51.3 us; the launch traced here: 51.2 us
  starting transfers between devices  31.4 us (61%)
  waiting for transfers between devices  12.1 us (24%)
  Pallas kernels  7.24 us (14%)
    ppermute x14, starting transfers between devices, over_pw(): return lax.ppermute(x, 'pw', [(i, i ^ bits) for i in range(32)])  16.7 us
    ppermute x7, starting transfers between devices, over_band(): return lax.ppermute(x, 'band', [(i, i ^ bits) for i in range(8)])  14.7 us
    ppermute x14, waiting for transfers between devices, over_pw(): return lax.ppermute(x, 'pw', [(i, i ^ bits) for i in range(32)])  11.1 us
    pallas_call x1, Pallas kernels, ahead(): pl.pallas_call(ahead_kernel, out_shape=(jax.ShapeDtypeStruct((2, NP, 3 *...  3.19 us
    pallas_call x1, Pallas kernels, spread_back(): pl.pallas_call(spread_kernel, out_shape=jax.ShapeDtypeStruct((2, NPW_DEV,...  2.58 us
    pallas_call x1, Pallas kernels, project_far(): pl.pallas_call(far_kernel, out_shape=halves, in_specs=[smem()] + [vmem()]...  1.14 us
  transfers between devices with their start and end apart: 21, of which 14 were waited for; matrix products, arithmetic and copies ran while one was open for 0% of the time, Pallas kernels for 7%

profile of v9, /device:TPU:1, one launch (start us, length us, event | category | flops | bytes accessed | tf_op | source)
XLA Modules:
  0.0 51.2 jit_solution(13468855522031284211)
XLA Ops:
  0.0 7.7 %collective-permute-start = (bf16[2,16,1280]{2,1,0:T(8,128)(2,1)}, bf16[2,16,1280]{2,1,0:T(8,128)(2,1)S(1)}, u32[]{:S(2)}, u32[]{:S(2)}) collective-permute-start(bf16[2,16,1280]{2,1,0:T(8,128)(2,1)} %refs_3_.3), channel_id=1, source_target_pairs={{0,1},{1,0},{2,3},{3,2},{4,5},{5,4},{6,7},{7,6},{8,9},{9,8},{10,11... | collective-permute-start | bytes 245768 | tf_op jit(solution)/shard_map/ppermute | solution.py:29
  7.7 2.5 %collective-permute-start.1 = (bf16[2,16,1280]{2,1,0:T(8,128)(2,1)}, bf16[2,16,1280]{2,1,0:T(8,128)(2,1)S(1)}, u32[]{:S(2)}, u32[]{:S(2)}) collective-permute-start(bf16[2,16,1280]{2,1,0:T(8,128)(2,1)} %refs_3_.3), channel_id=1, source_target_pairs={{0,6},{1,7},{2,4},{3,5},{4,2},{5,3},{6,0},{7,1},{8,14},{9,15},{10,... | collective-permute-start | bytes 245768 | tf_op jit(solution)/shard_map/ppermute | solution.py:29
  10.2 0.5 %collective-permute-start.2 = (bf16[2,16,1280]{2,1,0:T(8,128)(2,1)}, bf16[2,16,1280]{2,1,0:T(8,128)(2,1)S(1)}, u32[]{:S(2)}, u32[]{:S(2)}) collective-permute-start(bf16[2,16,1280]{2,1,0:T(8,128)(2,1)} %refs_3_.3), channel_id=1, source_target_pairs={{0,4},{1,5},{2,6},{3,7},{4,0},{5,1},{6,2},{7,3},{8,12},{9,13},{10,... | collective-permute-start | bytes 245768 | tf_op jit(solution)/shard_map/ppermute | solution.py:29
  10.7 0.3 collective-permute-start.3
  11.1 2.8 %collective-permute-start.4 = (bf16[2,16,1280]{2,1,0:T(8,128)(2,1)S(1)}, bf16[2,16,1280]{2,1,0:T(8,128)(2,1)S(1)}, u32[]{:S(2)}, u32[]{:S(2)}) collective-permute-start(bf16[2,16,1280]{2,1,0:T(8,128)(2,1)S(1)} %collective-permute-done.refs_3_.refs_7_), channel_id=1, source_target_pairs={{0,4},{1,5},{2,6},{3,7},{4,0},{5,1},{6,2},{7,3},{8,12},{9,13},{10,... | collective-permute-start | bytes 245768 | tf_op jit(solution)/shard_map/ppermute | solution.py:29
  14.0 0.9 %collective-permute-start.5 = (bf16[2,16,1280]{2,1,0:T(8,128)(2,1)S(1)}, bf16[2,16,1280]{2,1,0:T(8,128)(2,1)S(1)}, u32[]{:S(2)}, u32[]{:S(2)}) collective-permute-start(bf16[2,16,1280]{2,1,0:T(8,128)(2,1)S(1)} %collective-permute-done.refs_3_.refs_7_), channel_id=1, source_target_pairs={{0,6},{1,7},{2,4},{3,5},{4,2},{5,3},{6,0},{7,1},{8,14},{9,15},{10,... | collective-permute-start | bytes 245768 | tf_op jit(solution)/shard_map/ppermute | solution.py:29
  14.8 0.4 collective-permute-done.2.refs_1_
  15.3 3.2 %shard_map.56 = (bf16[2,128,192]{2,1,0:T(8,128)(2,1)S(1)}, bf16[2,1280,896]{2,1,0:T(8,128)(2,1)S(1)}, f32[2,128,896]{2,1,0:T(8,128)S(1)}) custom-call(bf16[2,128,128]{2,1,0:T(8,128)(2,1)S(1)} %shard_map.55.pick_ref, s32[12]{0:T(128)S(1)} %copy-done.2, s32[12]{0:T(128)S(1)} %copy-done.3, f32[12,13,13]{2,1,0:T(8,128)S(1)} %copy-done.1, ...), custom_call_target="tpu_custom_call" | custom-call | flops 2000000000 | bytes 8388608 | tf_op jit(solution)/shard_map/pallas_call | solution.py:129
  18.5 0.3 collective-permute-done.5.refs_1_.refs_5_
  18.7 0.3 collective-permute-done.6.refs_2_.refs_6_
  19.0 1.1 %shard_map.57 = (f32[128,896]{1,0:T(8,128)S(1)}, bf16[128,896]{1,0:T(8,128)(2,1)S(1)}) custom-call(s32[1]{0:T(128)} %bitcast.core_ref, f32[2,128,896]{2,1,0:T(8,128)S(1)} %get-tuple-element.12.near_ref, bf16[2,128,192]{2,1,0:T(8,128)(2,1)S(1)} %get-tuple-element.13.left_ref, bf16[2,1280,896]{2,1,0:T(8,128)(2,1)S(1)} %get-tuple-element.14.waves_ref, ...), custom_call_target="tpu_custom_call" | custom-call | flops 587202560 | bytes 6291456 | tf_op jit(solution)/shard_map/pallas_call | solution.py:192
  20.2 2.9 %collective-permute-start.7 = (bf16[128,896]{1,0:T(8,128)(2,1)S(1)}, bf16[128,896]{1,0:T(8,128)(2,1)S(1)}, u32[]{:S(2)}, u32[]{:S(2)}) collective-permute-start(bf16[128,896]{1,0:T(8,128)(2,1)S(1)} %get-tuple-element.16), channel_id=1, source_target_pairs={{0,8},{8,0},{16,24},{24,16},{32,40},{40,32},{48,56},{56,48},{64,72... | collective-permute-start | bytes 688136 | tf_op jit(solution)/shard_map/ppermute | solution.py:25
  23.1 1.1 %collective-permute-done.7 = bf16[128,896]{1,0:T(8,128)(2,1)S(1)} collective-permute-done((bf16[128,896]{1,0:T(8,128)(2,1)S(1)}, bf16[128,896]{1,0:T(8,128)(2,1)S(1)}, u32[]{:S(2)}, u32[]{:S(2)}) %collective-permute-start.7) | collective-permute-done | bytes 229408 | tf_op jit(solution)/shard_map/ppermute | solution.py:25
  24.3 3.0 %collective-permute-start.10 = (bf16[32,896]{1,0:T(8,128)(2,1)S(1)}, bf16[32,896]{1,0:T(8,128)(2,1)S(1)}, u32[]{:S(2)}, u32[]{:S(2)}) collective-permute-start(bf16[32,896]{1,0:T(8,128)(2,1)S(1)} %get-tuple-element.20), channel_id=1, source_target_pairs={{0,32},{8,40},{16,48},{24,56},{32,0},{40,8},{48,16},{56,24},{64,96... | collective-permute-start | bytes 172040 | tf_op jit(solution)/shard_map/ppermute | solution.py:25
  27.3 0.8 %collective-permute-start.8 = (bf16[32,896]{1,0:T(8,128)(2,1)S(1)}, bf16[32,896]{1,0:T(8,128)(2,1)S(1)}, u32[]{:S(2)}, u32[]{:S(2)}) collective-permute-start(bf16[32,896]{1,0:T(8,128)(2,1)S(1)} %get-tuple-element.19), channel_id=1, source_target_pairs={{0,48},{8,56},{16,32},{24,40},{32,16},{40,24},{48,0},{56,8},{64,11... | collective-permute-start | bytes 172040 | tf_op jit(solution)/shard_map/ppermute | solution.py:25
  28.1 0.8 %collective-permute-done.10 = bf16[32,896]{1,0:T(8,128)(2,1)S(1)} collective-permute-done((bf16[32,896]{1,0:T(8,128)(2,1)S(1)}, bf16[32,896]{1,0:T(8,128)(2,1)S(1)}, u32[]{:S(2)}, u32[]{:S(2)}) %collective-permute-start.10) | collective-permute-done | bytes 57376 | tf_op jit(solution)/shard_map/ppermute | solution.py:25
  28.9 2.6 %collective-permute-done.8 = bf16[32,896]{1,0:T(8,128)(2,1)S(1)} collective-permute-done((bf16[32,896]{1,0:T(8,128)(2,1)S(1)}, bf16[32,896]{1,0:T(8,128)(2,1)S(1)}, u32[]{:S(2)}, u32[]{:S(2)}) %collective-permute-start.8) | collective-permute-done | bytes 57376 | tf_op jit(solution)/shard_map/ppermute | solution.py:25
  31.6 1.7 %collective-permute-start.11 = (bf16[32,896]{1,0:T(8,128)(2,1)S(1)}, bf16[32,896]{1,0:T(8,128)(2,1)S(1)}, u32[]{:S(2)}, u32[]{:S(2)}) collective-permute-start(bf16[32,896]{1,0:T(8,128)(2,1)S(1)} %fusion.2), channel_id=1, source_target_pairs={{0,192},{8,200},{16,208},{24,216},{32,224},{40,232},{48,240},{56,2... | collective-permute-start | bytes 172040 | tf_op jit(solution)/shard_map/ppermute | solution.py:25
  33.4 1.8 %collective-permute-start.13 = (bf16[32,896]{1,0:T(8,128)(2,1)S(1)}, bf16[32,896]{1,0:T(8,128)(2,1)S(1)}, u32[]{:S(2)}, u32[]{:S(2)}) collective-permute-start(bf16[32,896]{1,0:T(8,128)(2,1)S(1)} %fusion.2), channel_id=1, source_target_pairs={{0,128},{8,136},{16,144},{24,152},{32,160},{40,168},{48,176},{56,1... | collective-permute-start | bytes 172040 | tf_op jit(solution)/shard_map/ppermute | solution.py:25
  35.2 1.4 %collective-permute-done.11 = bf16[32,896]{1,0:T(8,128)(2,1)S(1)} collective-permute-done((bf16[32,896]{1,0:T(8,128)(2,1)S(1)}, bf16[32,896]{1,0:T(8,128)(2,1)S(1)}, u32[]{:S(2)}, u32[]{:S(2)}) %collective-permute-start.11) | collective-permute-done | bytes 57376 | tf_op jit(solution)/shard_map/ppermute | solution.py:25
  36.6 0.6 %collective-permute-done.12 = bf16[32,896]{1,0:T(8,128)(2,1)S(1)} collective-permute-done((bf16[32,896]{1,0:T(8,128)(2,1)S(1)}, bf16[32,896]{1,0:T(8,128)(2,1)S(1)}, u32[]{:S(2)}, u32[]{:S(2)}) %collective-permute-start.12) | collective-permute-done | bytes 57376 | tf_op jit(solution)/shard_map/ppermute | solution.py:25
  37.2 2.2 %collective-permute-done.13 = bf16[32,896]{1,0:T(8,128)(2,1)S(1)} collective-permute-done((bf16[32,896]{1,0:T(8,128)(2,1)S(1)}, bf16[32,896]{1,0:T(8,128)(2,1)S(1)}, u32[]{:S(2)}, u32[]{:S(2)}) %collective-permute-start.13) | collective-permute-done | bytes 57376 | tf_op jit(solution)/shard_map/ppermute | solution.py:25
  39.4 2.7 %collective-permute-start.14 = (bf16[32,896]{1,0:T(8,128)(2,1)S(1)}, bf16[32,896]{1,0:T(8,128)(2,1)S(1)}, u32[]{:S(2)}, u32[]{:S(2)}) collective-permute-start(bf16[32,896]{1,0:T(8,128)(2,1)S(1)} %add_convert_fusion.refs_0_), channel_id=1, source_target_pairs={{0,40},{8,32},{16,56},{24,48},{32,8},{40,0},{48,24},{56,16},{64,10... | collective-permute-start | bytes 172040 | tf_op jit(solution)/shard_map/ppermute | solution.py:25
  42.2 0.8 %collective-permute-start.15 = (bf16[32,896]{1,0:T(8,128)(2,1)S(1)}, bf16[32,896]{1,0:T(8,128)(2,1)S(1)}, u32[]{:S(2)}, u32[]{:S(2)}) collective-permute-start(bf16[32,896]{1,0:T(8,128)(2,1)S(1)} %add_convert_fusion.refs_0_), channel_id=1, source_target_pairs={{0,56},{8,48},{16,40},{24,32},{32,24},{40,16},{48,8},{56,0},{64,12... | collective-permute-start | bytes 172040 | tf_op jit(solution)/shard_map/ppermute | solution.py:25
  42.9 0.9 %collective-permute-start.16 = (bf16[32,896]{1,0:T(8,128)(2,1)S(1)}, bf16[32,896]{1,0:T(8,128)(2,1)S(1)}, u32[]{:S(2)}, u32[]{:S(2)}) collective-permute-start(bf16[32,896]{1,0:T(8,128)(2,1)S(1)} %add_convert_fusion.refs_0_), channel_id=1, source_target_pairs={{0,24},{8,16},{16,8},{24,0},{32,56},{40,48},{48,40},{56,32},{64,88... | collective-permute-start | bytes 172040 | tf_op jit(solution)/shard_map/ppermute | solution.py:25
  43.8 0.8 %collective-permute-done.14.refs_1_ = bf16[32,896]{1,0:T(8,128)(2,1)S(1)} collective-permute-done((bf16[32,896]{1,0:T(8,128)(2,1)S(1)}, bf16[32,896]{1,0:T(8,128)(2,1)S(1)}, u32[]{:S(2)}, u32[]{:S(2)}) %collective-permute-start.14) | collective-permute-done | bytes 57376 | tf_op jit(solution)/shard_map/ppermute | solution.py:25
  44.6 1.6 %collective-permute-start.18 = (bf16[32,896]{1,0:T(8,128)(2,1)S(1)}, bf16[32,896]{1,0:T(8,128)(2,1)S(1)}, u32[]{:S(2)}, u32[]{:S(2)}) collective-permute-start(bf16[32,896]{1,0:T(8,128)(2,1)S(1)} %collective-permute-done.14.refs_1_), channel_id=1, source_target_pairs={{0,8},{8,0},{16,24},{24,16},{32,40},{40,32},{48,56},{56,48},{64,72... | collective-permute-start | bytes 172040 | tf_op jit(solution)/shard_map/ppermute | solution.py:25
  46.2 0.7 %collective-permute-done.15.refs_2_ = bf16[32,896]{1,0:T(8,128)(2,1)S(1)} collective-permute-done((bf16[32,896]{1,0:T(8,128)(2,1)S(1)}, bf16[32,896]{1,0:T(8,128)(2,1)S(1)}, u32[]{:S(2)}, u32[]{:S(2)}) %collective-permute-start.15) | collective-permute-done | bytes 57376 | tf_op jit(solution)/shard_map/ppermute | solution.py:25
  47.2 0.4 collective-permute-start.20
  47.6 0.2 shard_map.58.refs_8_
  47.8 0.4 collective-permute-done.19.refs_6_
  48.4 2.6 %shard_map.59 = bf16[2,1280,896]{2,1,0:T(8,128)(2,1)} custom-call(s32[1]{0:T(128)} %bitcast.core_ref, s32[1]{0:T(128)} %bitcast.1.y_ref, bf16[32,896]{1,0:T(8,128)(2,1)S(1)} %add_convert_fusion.refs_0_, bf16[32,896]{1,0:T(8,128)(2,1)S(1)} %collective-permute-done.14.refs_1_, bf16[32,896]{1,0:T(8,128)(2,1)S(1)} %collective-permute-done.15.refs_2_, ...), custom_call_target="tpu_custom_call" | custom-call | flops 1174405120 | bytes 6291456 | tf_op jit(solution)/shard_map/pallas_call | solution.py:258
  (27 shorter events, 0.8 us)
Async XLA Ops:
  0.0 11.1 %collective-permute-start = (bf16[2,16,1280]{2,1,0:T(8,128)(2,1)}, bf16[2,16,1280]{2,1,0:T(8,128)(2,1)S(1)}, u32[]{:S(2)}, u32[]{:S(2)}) collective-permute-start(bf16[2,16,1280]{2,1,0:T(8,128)(2,1)} %refs_3_.3), channel_id=1, source_target_pairs={{0,1},{1,0},{2,3},{3,2},{4,5},{5,4},{6,7},{7,6},{8,9},{9,8},{10,11... | collective-permute-start | bytes 245768 | tf_op jit(solution)/shard_map/ppermute | solution.py:29
  7.7 7.1 %collective-permute-start.1 = (bf16[2,16,1280]{2,1,0:T(8,128)(2,1)}, bf16[2,16,1280]{2,1,0:T(8,128)(2,1)S(1)}, u32[]{:S(2)}, u32[]{:S(2)}) collective-permute-start(bf16[2,16,1280]{2,1,0:T(8,128)(2,1)} %refs_3_.3), channel_id=1, source_target_pairs={{0,6},{1,7},{2,4},{3,5},{4,2},{5,3},{6,0},{7,1},{8,14},{9,15},{10,... | collective-permute-start | bytes 245768 | tf_op jit(solution)/shard_map/ppermute | solution.py:29
  10.2 5.0 %collective-permute-start.2 = (bf16[2,16,1280]{2,1,0:T(8,128)(2,1)}, bf16[2,16,1280]{2,1,0:T(8,128)(2,1)S(1)}, u32[]{:S(2)}, u32[]{:S(2)}) collective-permute-start(bf16[2,16,1280]{2,1,0:T(8,128)(2,1)} %refs_3_.3), channel_id=1, source_target_pairs={{0,4},{1,5},{2,6},{3,7},{4,0},{5,1},{6,2},{7,3},{8,12},{9,13},{10,... | collective-permute-start | bytes 245768 | tf_op jit(solution)/shard_map/ppermute | solution.py:29
  10.7 4.5 %collective-permute-start.3 = (bf16[2,16,1280]{2,1,0:T(8,128)(2,1)}, bf16[2,16,1280]{2,1,0:T(8,128)(2,1)S(1)}, u32[]{:S(2)}, u32[]{:S(2)}) collective-permute-start(bf16[2,16,1280]{2,1,0:T(8,128)(2,1)} %refs_3_.3), channel_id=1, source_target_pairs={{0,2},{1,3},{2,0},{3,1},{4,6},{5,7},{6,4},{7,5},{8,10},{9,11},{10,... | collective-permute-start | bytes 245768 | tf_op jit(solution)/shard_map/ppermute | solution.py:29
  11.0 4.2 %copy-start = (bf16[2,16,1280]{2,1,0:T(8,128)(2,1)S(1)}, bf16[2,16,1280]{2,1,0:T(8,128)(2,1)}, u32[]{:S(2)}) copy-start(bf16[2,16,1280]{2,1,0:T(8,128)(2,1)} %refs_3_.3) | copy-start | bytes 245764
  11.0 4.2 %copy-start.1 = (f32[12,13,13]{2,1,0:T(8,128)S(1)}, f32[12,13,13]{2,1,0:T(8,128)}, u32[]{:S(2)}) copy-start(f32[12,13,13]{2,1,0:T(8,128)} %coupling_hbm.1) | copy-start | bytes 24340
  11.0 4.2 %copy-start.2 = (s32[12]{0:T(128)S(1)}, s32[12]{0:T(128)}, u32[]{:S(2)}) copy-start(s32[12]{0:T(128)} %offsets_hbm.1) | copy-start | bytes 148
  11.0 4.2 %copy-start.3 = (s32[12]{0:T(128)S(1)}, s32[12]{0:T(128)}, u32[]{:S(2)}) copy-start(s32[12]{0:T(128)} %counts_hbm.1) | copy-start | bytes 148
  11.1 7.3 %collective-permute-start.4 = (bf16[2,16,1280]{2,1,0:T(8,128)(2,1)S(1)}, bf16[2,16,1280]{2,1,0:T(8,128)(2,1)S(1)}, u32[]{:S(2)}, u32[]{:S(2)}) collective-permute-start(bf16[2,16,1280]{2,1,0:T(8,128)(2,1)S(1)} %collective-permute-done.refs_3_.refs_7_), channel_id=1, source_target_pairs={{0,4},{1,5},{2,6},{3,7},{4,0},{5,1},{6,2},{7,3},{8,12},{9,13},{10,... | collective-permute-start | bytes 245768 | tf_op jit(solution)/shard_map/ppermute | solution.py:29
  14.0 4.8 %collective-permute-start.5 = (bf16[2,16,1280]{2,1,0:T(8,128)(2,1)S(1)}, bf16[2,16,1280]{2,1,0:T(8,128)(2,1)S(1)}, u32[]{:S(2)}, u32[]{:S(2)}) collective-permute-start(bf16[2,16,1280]{2,1,0:T(8,128)(2,1)S(1)} %collective-permute-done.refs_3_.refs_7_), channel_id=1, source_target_pairs={{0,6},{1,7},{2,4},{3,5},{4,2},{5,3},{6,0},{7,1},{8,14},{9,15},{10,... | collective-permute-start | bytes 245768 | tf_op jit(solution)/shard_map/ppermute | solution.py:29
  14.8 4.2 %collective-permute-start.6 = (bf16[2,16,1280]{2,1,0:T(8,128)(2,1)S(1)}, bf16[2,16,1280]{2,1,0:T(8,128)(2,1)S(1)}, u32[]{:S(2)}, u32[]{:S(2)}) collective-permute-start(bf16[2,16,1280]{2,1,0:T(8,128)(2,1)S(1)} %collective-permute-done.refs_3_.refs_7_), channel_id=1, source_target_pairs={{0,2},{1,3},{2,0},{3,1},{4,6},{5,7},{6,4},{7,5},{8,10},{9,11},{10,... | collective-permute-start | bytes 245768 | tf_op jit(solution)/shard_map/ppermute | solution.py:29
  20.2 4.0 %collective-permute-start.7 = (bf16[128,896]{1,0:T(8,128)(2,1)S(1)}, bf16[128,896]{1,0:T(8,128)(2,1)S(1)}, u32[]{:S(2)}, u32[]{:S(2)}) collective-permute-start(bf16[128,896]{1,0:T(8,128)(2,1)S(1)} %get-tuple-element.16), channel_id=1, source_target_pairs={{0,8},{8,0},{16,24},{24,16},{32,40},{40,32},{48,56},{56,48},{64,72... | collective-permute-start | bytes 688136 | tf_op jit(solution)/shard_map/ppermute | solution.py:25
  24.3 4.6 %collective-permute-start.10 = (bf16[32,896]{1,0:T(8,128)(2,1)S(1)}, bf16[32,896]{1,0:T(8,128)(2,1)S(1)}, u32[]{:S(2)}, u32[]{:S(2)}) collective-permute-start(bf16[32,896]{1,0:T(8,128)(2,1)S(1)} %get-tuple-element.20), channel_id=1, source_target_pairs={{0,32},{8,40},{16,48},{24,56},{32,0},{40,8},{48,16},{56,24},{64,96... | collective-permute-start | bytes 172040 | tf_op jit(solution)/shard_map/ppermute | solution.py:25
  27.3 4.2 %collective-permute-start.8 = (bf16[32,896]{1,0:T(8,128)(2,1)S(1)}, bf16[32,896]{1,0:T(8,128)(2,1)S(1)}, u32[]{:S(2)}, u32[]{:S(2)}) collective-permute-start(bf16[32,896]{1,0:T(8,128)(2,1)S(1)} %get-tuple-element.19), channel_id=1, source_target_pairs={{0,48},{8,56},{16,32},{24,40},{32,16},{40,24},{48,0},{56,8},{64,11... | collective-permute-start | bytes 172040 | tf_op jit(solution)/shard_map/ppermute | solution.py:25
  28.1 3.5 %collective-permute-start.9 = (bf16[32,896]{1,0:T(8,128)(2,1)S(1)}, bf16[32,896]{1,0:T(8,128)(2,1)S(1)}, u32[]{:S(2)}, u32[]{:S(2)}) collective-permute-start(bf16[32,896]{1,0:T(8,128)(2,1)S(1)} %get-tuple-element.21), channel_id=1, source_target_pairs={{0,16},{8,24},{16,0},{24,8},{32,48},{40,56},{48,32},{56,40},{64,80... | collective-permute-start | bytes 172040 | tf_op jit(solution)/shard_map/ppermute | solution.py:25
  31.6 5.0 %collective-permute-start.11 = (bf16[32,896]{1,0:T(8,128)(2,1)S(1)}, bf16[32,896]{1,0:T(8,128)(2,1)S(1)}, u32[]{:S(2)}, u32[]{:S(2)}) collective-permute-start(bf16[32,896]{1,0:T(8,128)(2,1)S(1)} %fusion.2), channel_id=1, source_target_pairs={{0,192},{8,200},{16,208},{24,216},{32,224},{40,232},{48,240},{56,2... | collective-permute-start | bytes 172040 | tf_op jit(solution)/shard_map/ppermute | solution.py:25
  33.3 3.9 %collective-permute-start.12 = (bf16[32,896]{1,0:T(8,128)(2,1)S(1)}, bf16[32,896]{1,0:T(8,128)(2,1)S(1)}, u32[]{:S(2)}, u32[]{:S(2)}) collective-permute-start(bf16[32,896]{1,0:T(8,128)(2,1)S(1)} %fusion.2), channel_id=1, source_target_pairs={{0,64},{8,72},{16,80},{24,88},{32,96},{40,104},{48,112},{56,120},{... | collective-permute-start | bytes 172040 | tf_op jit(solution)/shard_map/ppermute | solution.py:25
  33.4 5.9 %collective-permute-start.13 = (bf16[32,896]{1,0:T(8,128)(2,1)S(1)}, bf16[32,896]{1,0:T(8,128)(2,1)S(1)}, u32[]{:S(2)}, u32[]{:S(2)}) collective-permute-start(bf16[32,896]{1,0:T(8,128)(2,1)S(1)} %fusion.2), channel_id=1, source_target_pairs={{0,128},{8,136},{16,144},{24,152},{32,160},{40,168},{48,176},{56,1... | collective-permute-start | bytes 172040 | tf_op jit(solution)/shard_map/ppermute | solution.py:25
  39.4 5.2 %collective-permute-start.14 = (bf16[32,896]{1,0:T(8,128)(2,1)S(1)}, bf16[32,896]{1,0:T(8,128)(2,1)S(1)}, u32[]{:S(2)}, u32[]{:S(2)}) collective-permute-start(bf16[32,896]{1,0:T(8,128)(2,1)S(1)} %add_convert_fusion.refs_0_), channel_id=1, source_target_pairs={{0,40},{8,32},{16,56},{24,48},{32,8},{40,0},{48,24},{56,16},{64,10... | collective-permute-start | bytes 172040 | tf_op jit(solution)/shard_map/ppermute | solution.py:25
  42.2 4.8 %collective-permute-start.15 = (bf16[32,896]{1,0:T(8,128)(2,1)S(1)}, bf16[32,896]{1,0:T(8,128)(2,1)S(1)}, u32[]{:S(2)}, u32[]{:S(2)}) collective-permute-start(bf16[32,896]{1,0:T(8,128)(2,1)S(1)} %add_convert_fusion.refs_0_), channel_id=1, source_target_pairs={{0,56},{8,48},{16,40},{24,32},{32,24},{40,16},{48,8},{56,0},{64,12... | collective-permute-start | bytes 172040 | tf_op jit(solution)/shard_map/ppermute | solution.py:25
  42.9 4.2 %collective-permute-start.16 = (bf16[32,896]{1,0:T(8,128)(2,1)S(1)}, bf16[32,896]{1,0:T(8,128)(2,1)S(1)}, u32[]{:S(2)}, u32[]{:S(2)}) collective-permute-start(bf16[32,896]{1,0:T(8,128)(2,1)S(1)} %add_convert_fusion.refs_0_), channel_id=1, source_target_pairs={{0,24},{8,16},{16,8},{24,0},{32,56},{40,48},{48,40},{56,32},{64,88... | collective-permute-start | bytes 172040 | tf_op jit(solution)/shard_map/ppermute | solution.py:25
  43.8 3.9 %collective-permute-start.17 = (bf16[32,896]{1,0:T(8,128)(2,1)S(1)}, bf16[32,896]{1,0:T(8,128)(2,1)S(1)}, u32[]{:S(2)}, u32[]{:S(2)}) collective-permute-start(bf16[32,896]{1,0:T(8,128)(2,1)S(1)} %add_convert_fusion.refs_0_), channel_id=1, source_target_pairs={{0,8},{8,0},{16,24},{24,16},{32,40},{40,32},{48,56},{56,48},{64,72... | collective-permute-start | bytes 172040 | tf_op jit(solution)/shard_map/ppermute | solution.py:25
  44.6 3.2 %collective-permute-start.18 = (bf16[32,896]{1,0:T(8,128)(2,1)S(1)}, bf16[32,896]{1,0:T(8,128)(2,1)S(1)}, u32[]{:S(2)}, u32[]{:S(2)}) collective-permute-start(bf16[32,896]{1,0:T(8,128)(2,1)S(1)} %collective-permute-done.14.refs_1_), channel_id=1, source_target_pairs={{0,8},{8,0},{16,24},{24,16},{32,40},{40,32},{48,56},{56,48},{64,72... | collective-permute-start | bytes 172040 | tf_op jit(solution)/shard_map/ppermute | solution.py:25
  47.0 1.2 %collective-permute-start.19 = (bf16[32,896]{1,0:T(8,128)(2,1)S(1)}, bf16[32,896]{1,0:T(8,128)(2,1)S(1)}, u32[]{:S(2)}, u32[]{:S(2)}) collective-permute-start(bf16[32,896]{1,0:T(8,128)(2,1)S(1)} %collective-permute-done.15.refs_2_), channel_id=1, source_target_pairs={{0,8},{8,0},{16,24},{24,16},{32,40},{40,32},{48,56},{56,48},{64,72... | collective-permute-start | bytes 172040 | tf_op jit(solution)/shard_map/ppermute | solution.py:25
  47.2 1.3 %collective-permute-start.20 = (bf16[32,896]{1,0:T(8,128)(2,1)S(1)}, bf16[32,896]{1,0:T(8,128)(2,1)S(1)}, u32[]{:S(2)}, u32[]{:S(2)}) collective-permute-start(bf16[32,896]{1,0:T(8,128)(2,1)S(1)} %collective-permute-done.16.refs_3_), channel_id=1, source_target_pairs={{0,8},{8,0},{16,24},{24,16},{32,40},{40,32},{48,56},{56,48},{64,72... | collective-permute-start | bytes 172040 | tf_op jit(solution)/shard_map/ppermute | solution.py:25

commit v10 on v8

--- a/solution.py
+++ b/solution.py
@@ -15,7 +15,7 @@
 CHUNK = 32
 ORDER = ((3, 2, 1, 0), (2, 3, 1, 0))
 SLOTS = (0, 2, 3, 1)
-BLOCK_PW = 320
+BLOCK_PW = 256
 BF16 = jnp.bfloat16
 F32 = jnp.float32
 MIB = 1024 * 1024

time: 51.2 us -> 51.2 us (level)
  no operation moved by 1% of the time
where the time goes in v10:
time: 51.2 us; the launch traced here: 51.1 us
  starting transfers between devices  31.4 us (61%)
  waiting for transfers between devices  11.7 us (23%)
  Pallas kernels  7.55 us (15%)
    ppermute x14, starting transfers between devices, over_pw(): return lax.ppermute(x, 'pw', [(i, i ^ bits) for i in range(32)])  16.7 us
    ppermute x7, starting transfers between devices, over_band(): return lax.ppermute(x, 'band', [(i, i ^ bits) for i in range(8)])  14.7 us
    ppermute x14, waiting for transfers between devices, over_pw(): return lax.ppermute(x, 'pw', [(i, i ^ bits) for i in range(32)])  11 us
    pallas_call x1, Pallas kernels, spread_back(): pl.pallas_call(spread_kernel, out_shape=jax.ShapeDtypeStruct((2, NPW_DEV,...  2.55 us
    pallas_call x1, Pallas kernels, ahead(): pl.pallas_call(ahead_kernel, out_shape=(jax.ShapeDtypeStruct((2, NP, 3 *...  2.35 us
    pallas_call x1, Pallas kernels, project_near(): pl.pallas_call(near_kernel, out_shape=jax.ShapeDtypeStruct((2, NP, NB_DEV...  1.17 us
    pallas_call x1, Pallas kernels, project_far(): pl.pallas_call(far_kernel, out_shape=halves, in_specs=[smem()] + [vmem()]...  1.15 us
  transfers between devices with their start and end apart: 21, of which 13 were waited for; matrix products, arithmetic and copies ran while one was open for 0% of the time, Pallas kernels for 8%

profile of v10, /device:TPU:1, one launch (start us, length us, event | category | flops | bytes accessed | tf_op | source)
XLA Modules:
  0.0 51.1 jit_solution(11893711337101116846)
XLA Ops:
  0.0 7.7 %collective-permute-start = (bf16[2,16,1280]{2,1,0:T(8,128)(2,1)}, bf16[2,16,1280]{2,1,0:T(8,128)(2,1)S(1)}, u32[]{:S(2)}, u32[]{:S(2)}) collective-permute-start(bf16[2,16,1280]{2,1,0:T(8,128)(2,1)} %refs_3_.3), channel_id=1, source_target_pairs={{0,1},{1,0},{2,3},{3,2},{4,5},{5,4},{6,7},{7,6},{8,9},{9,8},{10,11... | collective-permute-start | bytes 245768 | tf_op jit(solution)/shard_map/ppermute | solution.py:29
  7.7 2.5 %collective-permute-start.1 = (bf16[2,16,1280]{2,1,0:T(8,128)(2,1)}, bf16[2,16,1280]{2,1,0:T(8,128)(2,1)S(1)}, u32[]{:S(2)}, u32[]{:S(2)}) collective-permute-start(bf16[2,16,1280]{2,1,0:T(8,128)(2,1)} %refs_3_.3), channel_id=1, source_target_pairs={{0,6},{1,7},{2,4},{3,5},{4,2},{5,3},{6,0},{7,1},{8,14},{9,15},{10,... | collective-permute-start | bytes 245768 | tf_op jit(solution)/shard_map/ppermute | solution.py:29
  10.2 0.5 %collective-permute-start.2 = (bf16[2,16,1280]{2,1,0:T(8,128)(2,1)}, bf16[2,16,1280]{2,1,0:T(8,128)(2,1)S(1)}, u32[]{:S(2)}, u32[]{:S(2)}) collective-permute-start(bf16[2,16,1280]{2,1,0:T(8,128)(2,1)} %refs_3_.3), channel_id=1, source_target_pairs={{0,4},{1,5},{2,6},{3,7},{4,0},{5,1},{6,2},{7,3},{8,12},{9,13},{10,... | collective-permute-start | bytes 245768 | tf_op jit(solution)/shard_map/ppermute | solution.py:29
  10.7 0.3 collective-permute-start.3
  11.1 2.8 %collective-permute-start.4 = (bf16[2,16,1280]{2,1,0:T(8,128)(2,1)S(1)}, bf16[2,16,1280]{2,1,0:T(8,128)(2,1)S(1)}, u32[]{:S(2)}, u32[]{:S(2)}) collective-permute-start(bf16[2,16,1280]{2,1,0:T(8,128)(2,1)S(1)} %collective-permute-done.refs_3_.refs_7_), channel_id=1, source_target_pairs={{0,4},{1,5},{2,6},{3,7},{4,0},{5,1},{6,2},{7,3},{8,12},{9,13},{10,... | collective-permute-start | bytes 245768 | tf_op jit(solution)/shard_map/ppermute | solution.py:29
  14.0 0.9 %collective-permute-start.5 = (bf16[2,16,1280]{2,1,0:T(8,128)(2,1)S(1)}, bf16[2,16,1280]{2,1,0:T(8,128)(2,1)S(1)}, u32[]{:S(2)}, u32[]{:S(2)}) collective-permute-start(bf16[2,16,1280]{2,1,0:T(8,128)(2,1)S(1)} %collective-permute-done.refs_3_.refs_7_), channel_id=1, source_target_pairs={{0,6},{1,7},{2,4},{3,5},{4,2},{5,3},{6,0},{7,1},{8,14},{9,15},{10,... | collective-permute-start | bytes 245768 | tf_op jit(solution)/shard_map/ppermute | solution.py:29
  14.9 2.3 %shard_map.56 = (bf16[2,128,192]{2,1,0:T(8,128)(2,1)S(1)}, bf16[2,1280,896]{2,1,0:T(8,128)(2,1)S(1)}) custom-call(bf16[2,128,128]{2,1,0:T(8,128)(2,1)S(1)} %shard_map.55.pick_ref, s32[12]{0:T(128)S(1)} %copy-done.2, s32[12]{0:T(128)S(1)} %copy-done.3, f32[12,13,13]{2,1,0:T(8,128)S(1)} %copy-done.1, bf16[2,1280,896]{2,1,0:T(8,128)(2,1)} %waves_hbm.1), custom_call_target="tpu_custom_call" | custom-call | flops 2000000000 | bytes 8388608 | tf_op jit(solution)/shard_map/pallas_call | solution.py:129
  17.2 1.2 %shard_map.57.near_ref = f32[2,128,896]{2,1,0:T(8,128)S(1)} custom-call(bf16[2,128,192]{2,1,0:T(8,128)(2,1)S(1)} %get-tuple-element.11.left_ref, bf16[2,1280,896]{2,1,0:T(8,128)(2,1)S(1)} %get-tuple-element.12.waves_ref, bf16[2,16,1280]{2,1,0:T(8,128)(2,1)S(1)} %collective-permute-done.1.refs_0_, bf16[2,16,1280]{2,1,0:T(8,128)(2,1)S(1)} %collective-permute-done.2.refs_1_, ...), custom_call_target="tpu_custom_call" | custom-call | flops 587202560 | bytes 6291456 | tf_op jit(solution)/shard_map/pallas_call | solution.py:173
  18.4 0.3 collective-permute-done.5.refs_1_.refs_5_
  18.7 0.3 collective-permute-done.6.refs_2_.refs_6_
  19.1 1.2 %shard_map.58 = (f32[128,896]{1,0:T(8,128)S(1)}, bf16[128,896]{1,0:T(8,128)(2,1)S(1)}) custom-call(s32[1]{0:T(128)} %bitcast.core_ref, f32[2,128,896]{2,1,0:T(8,128)S(1)} %shard_map.57.near_ref, bf16[2,128,192]{2,1,0:T(8,128)(2,1)S(1)} %get-tuple-element.11.left_ref, bf16[2,1280,896]{2,1,0:T(8,128)(2,1)S(1)} %get-tuple-element.12.waves_ref, ...), custom_call_target="tpu_custom_call" | custom-call | flops 587202560 | bytes 6291456 | tf_op jit(solution)/shard_map/pallas_call | solution.py:203
  20.2 2.9 %collective-permute-start.7 = (bf16[128,896]{1,0:T(8,128)(2,1)S(1)}, bf16[128,896]{1,0:T(8,128)(2,1)S(1)}, u32[]{:S(2)}, u32[]{:S(2)}) collective-permute-start(bf16[128,896]{1,0:T(8,128)(2,1)S(1)} %get-tuple-element.14), channel_id=1, source_target_pairs={{0,8},{8,0},{16,24},{24,16},{32,40},{40,32},{48,56},{56,48},{64,72... | collective-permute-start | bytes 688136 | tf_op jit(solution)/shard_map/ppermute | solution.py:25
  23.1 1.1 %collective-permute-done.7 = bf16[128,896]{1,0:T(8,128)(2,1)S(1)} collective-permute-done((bf16[128,896]{1,0:T(8,128)(2,1)S(1)}, bf16[128,896]{1,0:T(8,128)(2,1)S(1)}, u32[]{:S(2)}, u32[]{:S(2)}) %collective-permute-start.7) | collective-permute-done | bytes 229408 | tf_op jit(solution)/shard_map/ppermute | solution.py:25
  24.3 3.0 %collective-permute-start.10 = (bf16[32,896]{1,0:T(8,128)(2,1)S(1)}, bf16[32,896]{1,0:T(8,128)(2,1)S(1)}, u32[]{:S(2)}, u32[]{:S(2)}) collective-permute-start(bf16[32,896]{1,0:T(8,128)(2,1)S(1)} %get-tuple-element.18), channel_id=1, source_target_pairs={{0,32},{8,40},{16,48},{24,56},{32,0},{40,8},{48,16},{56,24},{64,96... | collective-permute-start | bytes 172040 | tf_op jit(solution)/shard_map/ppermute | solution.py:25
  27.3 0.8 %collective-permute-start.8 = (bf16[32,896]{1,0:T(8,128)(2,1)S(1)}, bf16[32,896]{1,0:T(8,128)(2,1)S(1)}, u32[]{:S(2)}, u32[]{:S(2)}) collective-permute-start(bf16[32,896]{1,0:T(8,128)(2,1)S(1)} %get-tuple-element.17), channel_id=1, source_target_pairs={{0,48},{8,56},{16,32},{24,40},{32,16},{40,24},{48,0},{56,8},{64,11... | collective-permute-start | bytes 172040 | tf_op jit(solution)/shard_map/ppermute | solution.py:25
  28.0 0.8 %collective-permute-done.10 = bf16[32,896]{1,0:T(8,128)(2,1)S(1)} collective-permute-done((bf16[32,896]{1,0:T(8,128)(2,1)S(1)}, bf16[32,896]{1,0:T(8,128)(2,1)S(1)}, u32[]{:S(2)}, u32[]{:S(2)}) %collective-permute-start.10) | collective-permute-done | bytes 57376 | tf_op jit(solution)/shard_map/ppermute | solution.py:25
  28.9 2.6 %collective-permute-done.8 = bf16[32,896]{1,0:T(8,128)(2,1)S(1)} collective-permute-done((bf16[32,896]{1,0:T(8,128)(2,1)S(1)}, bf16[32,896]{1,0:T(8,128)(2,1)S(1)}, u32[]{:S(2)}, u32[]{:S(2)}) %collective-permute-start.8) | collective-permute-done | bytes 57376 | tf_op jit(solution)/shard_map/ppermute | solution.py:25
  31.5 1.7 %collective-permute-start.11 = (bf16[32,896]{1,0:T(8,128)(2,1)S(1)}, bf16[32,896]{1,0:T(8,128)(2,1)S(1)}, u32[]{:S(2)}, u32[]{:S(2)}) collective-permute-start(bf16[32,896]{1,0:T(8,128)(2,1)S(1)} %fusion.2), channel_id=1, source_target_pairs={{0,192},{8,200},{16,208},{24,216},{32,224},{40,232},{48,240},{56,2... | collective-permute-start | bytes 172040 | tf_op jit(solution)/shard_map/ppermute | solution.py:25
  33.4 1.8 %collective-permute-start.13 = (bf16[32,896]{1,0:T(8,128)(2,1)S(1)}, bf16[32,896]{1,0:T(8,128)(2,1)S(1)}, u32[]{:S(2)}, u32[]{:S(2)}) collective-permute-start(bf16[32,896]{1,0:T(8,128)(2,1)S(1)} %fusion.2), channel_id=1, source_target_pairs={{0,128},{8,136},{16,144},{24,152},{32,160},{40,168},{48,176},{56,1... | collective-permute-start | bytes 172040 | tf_op jit(solution)/shard_map/ppermute | solution.py:25
  35.2 1.4 %collective-permute-done.11 = bf16[32,896]{1,0:T(8,128)(2,1)S(1)} collective-permute-done((bf16[32,896]{1,0:T(8,128)(2,1)S(1)}, bf16[32,896]{1,0:T(8,128)(2,1)S(1)}, u32[]{:S(2)}, u32[]{:S(2)}) %collective-permute-start.11) | collective-permute-done | bytes 57376 | tf_op jit(solution)/shard_map/ppermute | solution.py:25
  36.6 0.6 %collective-permute-done.12 = bf16[32,896]{1,0:T(8,128)(2,1)S(1)} collective-permute-done((bf16[32,896]{1,0:T(8,128)(2,1)S(1)}, bf16[32,896]{1,0:T(8,128)(2,1)S(1)}, u32[]{:S(2)}, u32[]{:S(2)}) %collective-permute-start.12) | collective-permute-done | bytes 57376 | tf_op jit(solution)/shard_map/ppermute | solution.py:25
  37.1 2.2 %collective-permute-done.13 = bf16[32,896]{1,0:T(8,128)(2,1)S(1)} collective-permute-done((bf16[32,896]{1,0:T(8,128)(2,1)S(1)}, bf16[32,896]{1,0:T(8,128)(2,1)S(1)}, u32[]{:S(2)}, u32[]{:S(2)}) %collective-permute-start.13) | collective-permute-done | bytes 57376 | tf_op jit(solution)/shard_map/ppermute | solution.py:25
  39.4 2.7 %collective-permute-start.14 = (bf16[32,896]{1,0:T(8,128)(2,1)S(1)}, bf16[32,896]{1,0:T(8,128)(2,1)S(1)}, u32[]{:S(2)}, u32[]{:S(2)}) collective-permute-start(bf16[32,896]{1,0:T(8,128)(2,1)S(1)} %add_convert_fusion.refs_0_), channel_id=1, source_target_pairs={{0,40},{8,32},{16,56},{24,48},{32,8},{40,0},{48,24},{56,16},{64,10... | collective-permute-start | bytes 172040 | tf_op jit(solution)/shard_map/ppermute | solution.py:25
  42.1 0.8 %collective-permute-start.15 = (bf16[32,896]{1,0:T(8,128)(2,1)S(1)}, bf16[32,896]{1,0:T(8,128)(2,1)S(1)}, u32[]{:S(2)}, u32[]{:S(2)}) collective-permute-start(bf16[32,896]{1,0:T(8,128)(2,1)S(1)} %add_convert_fusion.refs_0_), channel_id=1, source_target_pairs={{0,56},{8,48},{16,40},{24,32},{32,24},{40,16},{48,8},{56,0},{64,12... | collective-permute-start | bytes 172040 | tf_op jit(solution)/shard_map/ppermute | solution.py:25
  42.9 0.9 %collective-permute-start.16 = (bf16[32,896]{1,0:T(8,128)(2,1)S(1)}, bf16[32,896]{1,0:T(8,128)(2,1)S(1)}, u32[]{:S(2)}, u32[]{:S(2)}) collective-permute-start(bf16[32,896]{1,0:T(8,128)(2,1)S(1)} %add_convert_fusion.refs_0_), channel_id=1, source_target_pairs={{0,24},{8,16},{16,8},{24,0},{32,56},{40,48},{48,40},{56,32},{64,88... | collective-permute-start | bytes 172040 | tf_op jit(solution)/shard_map/ppermute | solution.py:25
  43.8 0.8 %collective-permute-done.14.refs_1_ = bf16[32,896]{1,0:T(8,128)(2,1)S(1)} collective-permute-done((bf16[32,896]{1,0:T(8,128)(2,1)S(1)}, bf16[32,896]{1,0:T(8,128)(2,1)S(1)}, u32[]{:S(2)}, u32[]{:S(2)}) %collective-permute-start.14) | collective-permute-done | bytes 57376 | tf_op jit(solution)/shard_map/ppermute | solution.py:25
  44.6 1.6 %collective-permute-start.18 = (bf16[32,896]{1,0:T(8,128)(2,1)S(1)}, bf16[32,896]{1,0:T(8,128)(2,1)S(1)}, u32[]{:S(2)}, u32[]{:S(2)}) collective-permute-start(bf16[32,896]{1,0:T(8,128)(2,1)S(1)} %collective-permute-done.14.refs_1_), channel_id=1, source_target_pairs={{0,8},{8,0},{16,24},{24,16},{32,40},{40,32},{48,56},{56,48},{64,72... | collective-permute-start | bytes 172040 | tf_op jit(solution)/shard_map/ppermute | solution.py:25
  46.2 0.7 %collective-permute-done.15.refs_2_ = bf16[32,896]{1,0:T(8,128)(2,1)S(1)} collective-permute-done((bf16[32,896]{1,0:T(8,128)(2,1)S(1)}, bf16[32,896]{1,0:T(8,128)(2,1)S(1)}, u32[]{:S(2)}, u32[]{:S(2)}) %collective-permute-start.15) | collective-permute-done | bytes 57376 | tf_op jit(solution)/shard_map/ppermute | solution.py:25
  47.1 0.4 collective-permute-start.20
  47.5 0.2 shard_map.59.refs_8_
  47.8 0.4 collective-permute-done.19.refs_6_
  48.4 2.6 %shard_map.60 = bf16[2,1280,896]{2,1,0:T(8,128)(2,1)} custom-call(s32[1]{0:T(128)} %bitcast.core_ref, s32[1]{0:T(128)} %bitcast.1.y_ref, bf16[32,896]{1,0:T(8,128)(2,1)S(1)} %add_convert_fusion.refs_0_, bf16[32,896]{1,0:T(8,128)(2,1)S(1)} %collective-permute-done.14.refs_1_, bf16[32,896]{1,0:T(8,128)(2,1)S(1)} %collective-permute-done.15.refs_2_, ...), custom_call_target="tpu_custom_call" | custom-call | flops 1174405120 | bytes 6291456 | tf_op jit(solution)/shard_map/pallas_call | solution.py:269
  (28 shorter events, 0.8 us)
Async XLA Ops:
  0.0 11.1 %collective-permute-start = (bf16[2,16,1280]{2,1,0:T(8,128)(2,1)}, bf16[2,16,1280]{2,1,0:T(8,128)(2,1)S(1)}, u32[]{:S(2)}, u32[]{:S(2)}) collective-permute-start(bf16[2,16,1280]{2,1,0:T(8,128)(2,1)} %refs_3_.3), channel_id=1, source_target_pairs={{0,1},{1,0},{2,3},{3,2},{4,5},{5,4},{6,7},{7,6},{8,9},{9,8},{10,11... | collective-permute-start | bytes 245768 | tf_op jit(solution)/shard_map/ppermute | solution.py:29
  7.7 7.1 %collective-permute-start.1 = (bf16[2,16,1280]{2,1,0:T(8,128)(2,1)}, bf16[2,16,1280]{2,1,0:T(8,128)(2,1)S(1)}, u32[]{:S(2)}, u32[]{:S(2)}) collective-permute-start(bf16[2,16,1280]{2,1,0:T(8,128)(2,1)} %refs_3_.3), channel_id=1, source_target_pairs={{0,6},{1,7},{2,4},{3,5},{4,2},{5,3},{6,0},{7,1},{8,14},{9,15},{10,... | collective-permute-start | bytes 245768 | tf_op jit(solution)/shard_map/ppermute | solution.py:29
  10.2 7.0 %collective-permute-start.2 = (bf16[2,16,1280]{2,1,0:T(8,128)(2,1)}, bf16[2,16,1280]{2,1,0:T(8,128)(2,1)S(1)}, u32[]{:S(2)}, u32[]{:S(2)}) collective-permute-start(bf16[2,16,1280]{2,1,0:T(8,128)(2,1)} %refs_3_.3), channel_id=1, source_target_pairs={{0,4},{1,5},{2,6},{3,7},{4,0},{5,1},{6,2},{7,3},{8,12},{9,13},{10,... | collective-permute-start | bytes 245768 | tf_op jit(solution)/shard_map/ppermute | solution.py:29
  10.7 6.5 %collective-permute-start.3 = (bf16[2,16,1280]{2,1,0:T(8,128)(2,1)}, bf16[2,16,1280]{2,1,0:T(8,128)(2,1)S(1)}, u32[]{:S(2)}, u32[]{:S(2)}) collective-permute-start(bf16[2,16,1280]{2,1,0:T(8,128)(2,1)} %refs_3_.3), channel_id=1, source_target_pairs={{0,2},{1,3},{2,0},{3,1},{4,6},{5,7},{6,4},{7,5},{8,10},{9,11},{10,... | collective-permute-start | bytes 245768 | tf_op jit(solution)/shard_map/ppermute | solution.py:29
  11.0 3.8 %copy-start.1 = (f32[12,13,13]{2,1,0:T(8,128)S(1)}, f32[12,13,13]{2,1,0:T(8,128)}, u32[]{:S(2)}) copy-start(f32[12,13,13]{2,1,0:T(8,128)} %coupling_hbm.1) | copy-start | bytes 24340
  11.0 3.8 %copy-start.2 = (s32[12]{0:T(128)S(1)}, s32[12]{0:T(128)}, u32[]{:S(2)}) copy-start(s32[12]{0:T(128)} %offsets_hbm.1) | copy-start | bytes 148
  11.0 3.9 %copy-start.3 = (s32[12]{0:T(128)S(1)}, s32[12]{0:T(128)}, u32[]{:S(2)}) copy-start(s32[12]{0:T(128)} %counts_hbm.1) | copy-start | bytes 148
  11.1 6.1 %copy-start = (bf16[2,16,1280]{2,1,0:T(8,128)(2,1)S(1)}, bf16[2,16,1280]{2,1,0:T(8,128)(2,1)}, u32[]{:S(2)}) copy-start(bf16[2,16,1280]{2,1,0:T(8,128)(2,1)} %refs_3_.3) | copy-start | bytes 245764
  11.1 7.3 %collective-permute-start.4 = (bf16[2,16,1280]{2,1,0:T(8,128)(2,1)S(1)}, bf16[2,16,1280]{2,1,0:T(8,128)(2,1)S(1)}, u32[]{:S(2)}, u32[]{:S(2)}) collective-permute-start(bf16[2,16,1280]{2,1,0:T(8,128)(2,1)S(1)} %collective-permute-done.refs_3_.refs_7_), channel_id=1, source_target_pairs={{0,4},{1,5},{2,6},{3,7},{4,0},{5,1},{6,2},{7,3},{8,12},{9,13},{10,... | collective-permute-start | bytes 245768 | tf_op jit(solution)/shard_map/ppermute | solution.py:29
  14.0 4.8 %collective-permute-start.5 = (bf16[2,16,1280]{2,1,0:T(8,128)(2,1)S(1)}, bf16[2,16,1280]{2,1,0:T(8,128)(2,1)S(1)}, u32[]{:S(2)}, u32[]{:S(2)}) collective-permute-start(bf16[2,16,1280]{2,1,0:T(8,128)(2,1)S(1)} %collective-permute-done.refs_3_.refs_7_), channel_id=1, source_target_pairs={{0,6},{1,7},{2,4},{3,5},{4,2},{5,3},{6,0},{7,1},{8,14},{9,15},{10,... | collective-permute-start | bytes 245768 | tf_op jit(solution)/shard_map/ppermute | solution.py:29
  14.8 4.2 %collective-permute-start.6 = (bf16[2,16,1280]{2,1,0:T(8,128)(2,1)S(1)}, bf16[2,16,1280]{2,1,0:T(8,128)(2,1)S(1)}, u32[]{:S(2)}, u32[]{:S(2)}) collective-permute-start(bf16[2,16,1280]{2,1,0:T(8,128)(2,1)S(1)} %collective-permute-done.refs_3_.refs_7_), channel_id=1, source_target_pairs={{0,2},{1,3},{2,0},{3,1},{4,6},{5,7},{6,4},{7,5},{8,10},{9,11},{10,... | collective-permute-start | bytes 245768 | tf_op jit(solution)/shard_map/ppermute | solution.py:29
  20.2 4.0 %collective-permute-start.7 = (bf16[128,896]{1,0:T(8,128)(2,1)S(1)}, bf16[128,896]{1,0:T(8,128)(2,1)S(1)}, u32[]{:S(2)}, u32[]{:S(2)}) collective-permute-start(bf16[128,896]{1,0:T(8,128)(2,1)S(1)} %get-tuple-element.14), channel_id=1, source_target_pairs={{0,8},{8,0},{16,24},{24,16},{32,40},{40,32},{48,56},{56,48},{64,72... | collective-permute-start | bytes 688136 | tf_op jit(solution)/shard_map/ppermute | solution.py:25
  24.3 4.6 %collective-permute-start.10 = (bf16[32,896]{1,0:T(8,128)(2,1)S(1)}, bf16[32,896]{1,0:T(8,128)(2,1)S(1)}, u32[]{:S(2)}, u32[]{:S(2)}) collective-permute-start(bf16[32,896]{1,0:T(8,128)(2,1)S(1)} %get-tuple-element.18), channel_id=1, source_target_pairs={{0,32},{8,40},{16,48},{24,56},{32,0},{40,8},{48,16},{56,24},{64,96... | collective-permute-start | bytes 172040 | tf_op jit(solution)/shard_map/ppermute | solution.py:25
  27.3 4.2 %collective-permute-start.8 = (bf16[32,896]{1,0:T(8,128)(2,1)S(1)}, bf16[32,896]{1,0:T(8,128)(2,1)S(1)}, u32[]{:S(2)}, u32[]{:S(2)}) collective-permute-start(bf16[32,896]{1,0:T(8,128)(2,1)S(1)} %get-tuple-element.17), channel_id=1, source_target_pairs={{0,48},{8,56},{16,32},{24,40},{32,16},{40,24},{48,0},{56,8},{64,11... | collective-permute-start | bytes 172040 | tf_op jit(solution)/shard_map/ppermute | solution.py:25
  28.0 3.5 %collective-permute-start.9 = (bf16[32,896]{1,0:T(8,128)(2,1)S(1)}, bf16[32,896]{1,0:T(8,128)(2,1)S(1)}, u32[]{:S(2)}, u32[]{:S(2)}) collective-permute-start(bf16[32,896]{1,0:T(8,128)(2,1)S(1)} %get-tuple-element.19), channel_id=1, source_target_pairs={{0,16},{8,24},{16,0},{24,8},{32,48},{40,56},{48,32},{56,40},{64,80... | collective-permute-start | bytes 172040 | tf_op jit(solution)/shard_map/ppermute | solution.py:25
  31.5 5.0 %collective-permute-start.11 = (bf16[32,896]{1,0:T(8,128)(2,1)S(1)}, bf16[32,896]{1,0:T(8,128)(2,1)S(1)}, u32[]{:S(2)}, u32[]{:S(2)}) collective-permute-start(bf16[32,896]{1,0:T(8,128)(2,1)S(1)} %fusion.2), channel_id=1, source_target_pairs={{0,192},{8,200},{16,208},{24,216},{32,224},{40,232},{48,240},{56,2... | collective-permute-start | bytes 172040 | tf_op jit(solution)/shard_map/ppermute | solution.py:25
  33.3 3.9 %collective-permute-start.12 = (bf16[32,896]{1,0:T(8,128)(2,1)S(1)}, bf16[32,896]{1,0:T(8,128)(2,1)S(1)}, u32[]{:S(2)}, u32[]{:S(2)}) collective-permute-start(bf16[32,896]{1,0:T(8,128)(2,1)S(1)} %fusion.2), channel_id=1, source_target_pairs={{0,64},{8,72},{16,80},{24,88},{32,96},{40,104},{48,112},{56,120},{... | collective-permute-start | bytes 172040 | tf_op jit(solution)/shard_map/ppermute | solution.py:25
  33.4 5.9 %collective-permute-start.13 = (bf16[32,896]{1,0:T(8,128)(2,1)S(1)}, bf16[32,896]{1,0:T(8,128)(2,1)S(1)}, u32[]{:S(2)}, u32[]{:S(2)}) collective-permute-start(bf16[32,896]{1,0:T(8,128)(2,1)S(1)} %fusion.2), channel_id=1, source_target_pairs={{0,128},{8,136},{16,144},{24,152},{32,160},{40,168},{48,176},{56,1... | collective-permute-start | bytes 172040 | tf_op jit(solution)/shard_map/ppermute | solution.py:25
  39.4 5.2 %collective-permute-start.14 = (bf16[32,896]{1,0:T(8,128)(2,1)S(1)}, bf16[32,896]{1,0:T(8,128)(2,1)S(1)}, u32[]{:S(2)}, u32[]{:S(2)}) collective-permute-start(bf16[32,896]{1,0:T(8,128)(2,1)S(1)} %add_convert_fusion.refs_0_), channel_id=1, source_target_pairs={{0,40},{8,32},{16,56},{24,48},{32,8},{40,0},{48,24},{56,16},{64,10... | collective-permute-start | bytes 172040 | tf_op jit(solution)/shard_map/ppermute | solution.py:25
  42.1 4.8 %collective-permute-start.15 = (bf16[32,896]{1,0:T(8,128)(2,1)S(1)}, bf16[32,896]{1,0:T(8,128)(2,1)S(1)}, u32[]{:S(2)}, u32[]{:S(2)}) collective-permute-start(bf16[32,896]{1,0:T(8,128)(2,1)S(1)} %add_convert_fusion.refs_0_), channel_id=1, source_target_pairs={{0,56},{8,48},{16,40},{24,32},{32,24},{40,16},{48,8},{56,0},{64,12... | collective-permute-start | bytes 172040 | tf_op jit(solution)/shard_map/ppermute | solution.py:25
  42.9 4.2 %collective-permute-start.16 = (bf16[32,896]{1,0:T(8,128)(2,1)S(1)}, bf16[32,896]{1,0:T(8,128)(2,1)S(1)}, u32[]{:S(2)}, u32[]{:S(2)}) collective-permute-start(bf16[32,896]{1,0:T(8,128)(2,1)S(1)} %add_convert_fusion.refs_0_), channel_id=1, source_target_pairs={{0,24},{8,16},{16,8},{24,0},{32,56},{40,48},{48,40},{56,32},{64,88... | collective-permute-start | bytes 172040 | tf_op jit(solution)/shard_map/ppermute | solution.py:25
  43.8 3.9 %collective-permute-start.17 = (bf16[32,896]{1,0:T(8,128)(2,1)S(1)}, bf16[32,896]{1,0:T(8,128)(2,1)S(1)}, u32[]{:S(2)}, u32[]{:S(2)}) collective-permute-start(bf16[32,896]{1,0:T(8,128)(2,1)S(1)} %add_convert_fusion.refs_0_), channel_id=1, source_target_pairs={{0,8},{8,0},{16,24},{24,16},{32,40},{40,32},{48,56},{56,48},{64,72... | collective-permute-start | bytes 172040 | tf_op jit(solution)/shard_map/ppermute | solution.py:25
  44.6 3.1 %collective-permute-start.18 = (bf16[32,896]{1,0:T(8,128)(2,1)S(1)}, bf16[32,896]{1,0:T(8,128)(2,1)S(1)}, u32[]{:S(2)}, u32[]{:S(2)}) collective-permute-start(bf16[32,896]{1,0:T(8,128)(2,1)S(1)} %collective-permute-done.14.refs_1_), channel_id=1, source_target_pairs={{0,8},{8,0},{16,24},{24,16},{32,40},{40,32},{48,56},{56,48},{64,72... | collective-permute-start | bytes 172040 | tf_op jit(solution)/shard_map/ppermute | solution.py:25
  47.0 1.2 %collective-permute-start.19 = (bf16[32,896]{1,0:T(8,128)(2,1)S(1)}, bf16[32,896]{1,0:T(8,128)(2,1)S(1)}, u32[]{:S(2)}, u32[]{:S(2)}) collective-permute-start(bf16[32,896]{1,0:T(8,128)(2,1)S(1)} %collective-permute-done.15.refs_2_), channel_id=1, source_target_pairs={{0,8},{8,0},{16,24},{24,16},{32,40},{40,32},{48,56},{56,48},{64,72... | collective-permute-start | bytes 172040 | tf_op jit(solution)/shard_map/ppermute | solution.py:25
  47.1 1.3 %collective-permute-start.20 = (bf16[32,896]{1,0:T(8,128)(2,1)S(1)}, bf16[32,896]{1,0:T(8,128)(2,1)S(1)}, u32[]{:S(2)}, u32[]{:S(2)}) collective-permute-start(bf16[32,896]{1,0:T(8,128)(2,1)S(1)} %collective-permute-done.16.refs_3_), channel_id=1, source_target_pairs={{0,8},{8,0},{16,24},{24,16},{32,40},{40,32},{48,56},{56,48},{64,72... | collective-permute-start | bytes 172040 | tf_op jit(solution)/shard_map/ppermute | solution.py:25
